TPU v7x, 256 devices: a whole 4x4x8 slice. The times are simulated.
256 devices in a mesh: ctx: 8 (over z_hi, x), exp: 32 (over y, z_lo, core).
Axes of the slice: x: 4, y: 4, z: 8 (z_hi: 2, z_lo: 4; z = z_hi * 4 + z_lo), core: 2. Of those that a mesh axis runs over, the one named last changes fastest.
Arguments:
- queries: bfloat16 [32, 1024, 2048], P('exp', 'ctx'), may hold values from -8 to 8
- key_rows: bfloat16 [32, 1024, 256], P('exp', 'ctx'), may hold values from -8 to 8
- value_rows: bfloat16 [32, 1024, 256], P('exp', 'ctx'), may hold values from -6 to 6
- out_grad: bfloat16 [32, 1024, 2048], P('exp', 'ctx'), may hold values from -6 to 6
- tokens: bfloat16 [32, 1024, 2880], P('exp', 'ctx'), may hold values from -6 to 6
- token_grad: bfloat16 [32, 1024, 2880], P('exp', 'ctx'), may hold values from -6 to 6
- route_ids: int32 [32, 1024, 4], P('exp', 'ctx'), may hold values from 0 to 127, as said below
- route_probs: float32 [32, 1024, 4], P('exp', 'ctx'), may hold values from 0.05 to 1
- entry_weight: bfloat16 [32, 2880, 2, 1440], P('exp', None, None, 'ctx'), may hold values from -0.109375 to 0.109375
- exit_weight: bfloat16 [32, 1440, 2880], P('exp', 'ctx'), may hold values from -0.15625 to 0.15625
Outputs:
- query_grad: bfloat16 [32, 1024, 2048], P('exp', 'ctx')
- key_grad: bfloat16 [32, 1024, 256], P('exp', 'ctx')
- value_grad: bfloat16 [32, 1024, 256], P('exp', 'ctx')
- input_grad: bfloat16 [32, 1024, 2880], P('exp', 'ctx')
- entry_grad: bfloat16 [32, 2880, 2, 1440], P('exp', None, None, 'ctx')
- exit_grad: bfloat16 [32, 1440, 2880], P('exp', 'ctx')
Inputs may be any that keep to these rules, and one draw needn't show every extreme that they name: `route_ids`: each token names 4 different experts. Tokens form aligned blocks of 128 positions in order (sequence by sequence); within one block no expert is named more than 5 times, and in every draw one expert below 32 is named exactly 5 times in every block.
All inputs are finite; a program needn't handle non-finite values.
Results may differ from a plain program's by a relative error of at most 0.017.
Values may be sent and summed in bfloat16 or wider, within the bound.
A program may use at most 192 MiB of HBM per device.

v0:
```python
import jax
import jax.numpy as jnp
from jax import lax
from jax.sharding import PartitionSpec as P

HEAD = 64
CAP = 5


score_scale = 0.125
masked_score = -1e30


def from_behind(shard, axis, by):
    length = lax.axis_size(axis)
    pairs = [(i, i + by) for i in range(length) if 0 <= i + by < length]
    return lax.ppermute(shard, axis, pairs)


def from_behind_2(shard, axis, by):
    length = lax.axis_size(axis)
    return lax.ppermute(shard, axis, [(i, (i + by) % length) for i in range(length)])


def block_scores(query_heads, key_block, key_first, query_first):
    length = query_heads.shape[0]
    key_count = key_block.shape[0]
    key_view = key_block.reshape(key_count, query_heads.shape[1], HEAD)
    scores = (
        jnp.einsum("ihgd,jhd->hgij", query_heads, key_view, preferred_element_type=jnp.float32)
        * score_scale
    )
    query_pos = query_first + jnp.arange(length)
    key_pos = key_first + jnp.arange(key_count)
    causal = key_pos[None, :] <= query_pos[:, None]
    return (scores, causal)


def forward_block(state, query_heads, grad_heads, key_block, value_block, key_first, query_first):
    scores, causal = block_scores(query_heads, key_block, key_first, query_first)
    value_view = value_block.reshape(value_block.shape[0], query_heads.shape[1], HEAD)
    prob_grad = jnp.einsum(
        "ihgd,jhd->hgij", grad_heads, value_view, preferred_element_type=jnp.float32
    )
    running_max, running_sum, running_dot = state
    block_max = jnp.max(jnp.where(causal, scores, masked_score), axis=-1)
    new_max = jnp.maximum(running_max, block_max)
    rescale = jnp.exp(running_max - new_max)
    weights = jnp.where(causal, jnp.exp(scores - new_max[..., None]), 0.0)
    running_sum = running_sum * rescale + jnp.sum(weights, axis=-1)
    running_dot = running_dot * rescale + jnp.sum(weights * prob_grad, axis=-1)
    return (new_max, running_sum, running_dot)


def backward_block(
    query_heads, grad_heads, key_block, value_block, logsum, delta, key_first, query_first
):
    scores, causal = block_scores(query_heads, key_block, key_first, query_first)
    key_count = key_block.shape[0]
    key_view = key_block.reshape(key_count, query_heads.shape[1], HEAD)
    value_view = value_block.reshape(key_count, query_heads.shape[1], HEAD)
    weights = jnp.where(causal, jnp.exp(scores - logsum[..., None]), 0.0)
    value_part = jnp.einsum(
        "hgij,ihgd->jhd",
        weights.astype(jnp.bfloat16),
        grad_heads,
        preferred_element_type=jnp.float32,
    )
    prob_grad = jnp.einsum(
        "ihgd,jhd->hgij", grad_heads, value_view, preferred_element_type=jnp.float32
    )
    score_grad = (weights * (prob_grad - delta[..., None])).astype(jnp.bfloat16)
    query_part = jnp.einsum(
        "hgij,jhd->ihgd", score_grad, key_view, preferred_element_type=jnp.float32
    )
    key_part = jnp.einsum(
        "hgij,ihgd->jhd", score_grad, query_heads, preferred_element_type=jnp.float32
    )
    return (
        query_part,
        key_part.reshape(key_count, -1) * score_scale,
        value_part.reshape(key_count, -1),
    )


def attention_grads(queries, key_rows, value_rows, out_grad):
    length = queries.shape[1]
    kv_width = key_rows.shape[2]
    head_count = kv_width // HEAD
    group_size = queries.shape[2] // kv_width
    query_heads = queries[0].reshape(length, head_count, group_size, HEAD)
    grad_heads = out_grad[0].reshape(length, head_count, group_size, HEAD)
    cycle_size = lax.axis_size("ctx")
    cycle_index = lax.axis_index("ctx")
    query_first = cycle_index * length
    paired = jnp.stack([key_rows[0], value_rows[0]])
    stat_shape = (head_count, group_size, length)
    state = (
        jnp.full(stat_shape, masked_score, jnp.float32),
        jnp.zeros(stat_shape, jnp.float32),
        jnp.zeros(stat_shape, jnp.float32),
    )
    visiting = paired
    for cycle_step in range(cycle_size):
        source = (cycle_index - cycle_step) % cycle_size
        state = forward_block(
            state, query_heads, grad_heads, visiting[0], visiting[1], source * length, query_first
        )
        if cycle_step + 1 < cycle_size:
            visiting = from_behind(visiting, "ctx", 1)
    logsum = state[0] + jnp.log(state[1])
    delta = state[2] / state[1]
    visiting = paired
    query_total = jnp.zeros((length, head_count, group_size, HEAD), jnp.float32)
    carried = jnp.zeros((2, length, kv_width), jnp.float32)
    for cycle_step in range(cycle_size):
        source = (cycle_index - cycle_step) % cycle_size
        query_part, key_part, value_part = backward_block(
            query_heads,
            grad_heads,
            visiting[0],
            visiting[1],
            logsum,
            delta,
            source * length,
            query_first,
        )
        query_total = query_total + query_part
        carried = carried + jnp.stack([key_part, value_part])
        if cycle_step + 1 < cycle_size:
            visiting = from_behind(visiting, "ctx", 1)
        carried = from_behind_2(carried, "ctx", 1)
    key_total = carried[0]
    value_total = carried[1]
    query_grad = (query_total * score_scale).reshape(1, length, -1).astype(jnp.bfloat16)
    return (
        query_grad,
        key_total.astype(jnp.bfloat16)[None],
        value_total.astype(jnp.bfloat16)[None],
    )


def expert_grads(tokens, token_grad, route_ids, route_probs, entry_weight, exit_weight):
    hidden_rows = tokens[0]
    upstream = token_grad[0]
    routes = route_ids[0]
    shares = route_probs[0]
    width = hidden_rows.shape[1]
    experts_here = lax.axis_size("exp")
    slot_count = experts_here * CAP
    matched = routes[:, :, None] == jnp.arange(experts_here)[None, None, :]
    token_hits = jnp.any(matched, axis=1).astype(jnp.int32)
    earlier = jnp.cumsum(token_hits, axis=0) - token_hits
    slot_index = jnp.sum(
        jnp.where(matched, earlier[:, None, :] + routes[:, :, None] * CAP, 0), axis=2
    )
    in_window = jnp.any(matched, axis=2)
    placed = (slot_index[:, :, None] == jnp.arange(slot_count)[None, None, :]) & in_window[
        :, :, None
    ]
    selector = jnp.any(placed, axis=1).astype(jnp.bfloat16)
    slot_share = jnp.sum(jnp.where(placed, shares[:, :, None], 0.0), axis=(0, 1))
    sent_rows = jnp.dot(selector.T, hidden_rows, preferred_element_type=jnp.float32).astype(
        jnp.bfloat16
    )
    picked = jnp.dot(selector.T, upstream, preferred_element_type=jnp.float32)
    sent_grads = (picked * slot_share[:, None]).astype(jnp.bfloat16)
    sent_rows = sent_rows.reshape(experts_here, CAP, width)
    sent_grads = sent_grads.reshape(experts_here, CAP, width)
    entry_local = entry_weight[0].reshape(width, -1)
    exit_local = exit_weight[0]
    hidden_part = exit_local.shape[0]
    arrived = (
        lax.all_to_all(sent_rows, "exp", split_axis=0, concat_axis=0, tiled=True),
        lax.all_to_all(sent_grads, "exp", split_axis=0, concat_axis=0, tiled=True),
    )
    rows_in = lax.all_gather(arrived[0].reshape(slot_count, width), "ctx", axis=0, tiled=True)
    grads_in = lax.all_gather(arrived[1].reshape(slot_count, width), "ctx", axis=0, tiled=True)
    projected = jnp.dot(rows_in, entry_local, preferred_element_type=jnp.float32)
    gate = projected[:, :hidden_part]
    upward = projected[:, hidden_part:]
    sigma = jax.nn.sigmoid(gate)
    swish = gate * sigma
    activation = (swish * upward).astype(jnp.bfloat16)
    act_grad = jnp.dot(grads_in, exit_local.T, preferred_element_type=jnp.float32)
    slope = sigma * (1.0 + gate * (1.0 - sigma))
    score_rows = jnp.concatenate([act_grad * upward * slope, act_grad * swish], axis=1).astype(
        jnp.bfloat16
    )
    entry_sum = jnp.dot(rows_in.T, score_rows, preferred_element_type=jnp.float32)
    exit_sum = jnp.dot(activation.T, grads_in, preferred_element_type=jnp.float32)
    carried = (entry_sum, exit_sum, score_rows)
    entry_sum, exit_sum, score_buffer = carried
    summed = lax.psum_scatter(
        jnp.dot(score_buffer, entry_local.T, preferred_element_type=jnp.float32).astype(
            jnp.bfloat16
        ),
        "ctx",
        scatter_dimension=0,
        tiled=True,
    )
    returned = lax.all_to_all(
        summed.reshape(experts_here, CAP, width), "exp", split_axis=0, concat_axis=0, tiled=True
    )
    row_grad = returned.reshape(slot_count, width)
    input_grad = jnp.dot(selector, row_grad, preferred_element_type=jnp.float32).astype(
        jnp.bfloat16
    )
    entry_grad = entry_sum.astype(jnp.bfloat16).reshape(1, width, 2, hidden_part)
    return (input_grad[None], entry_grad, exit_sum.astype(jnp.bfloat16)[None])


def per_device(
    queries,
    key_rows,
    value_rows,
    out_grad,
    tokens,
    token_grad,
    route_ids,
    route_probs,
    entry_weight,
    exit_weight,
):
    input_grad, entry_grad, exit_grad = expert_grads(
        tokens, token_grad, route_ids, route_probs, entry_weight, exit_weight
    )
    query_grad, key_grad, value_grad = attention_grads(queries, key_rows, value_rows, out_grad)
    return (query_grad, key_grad, value_grad, input_grad, entry_grad, exit_grad)


def solution(mesh):
    return jax.shard_map(
        per_device,
        mesh=mesh,
        in_specs=(
            P("exp", "ctx", None),
            P("exp", "ctx", None),
            P("exp", "ctx", None),
            P("exp", "ctx", None),
            P("exp", "ctx", None),
            P("exp", "ctx", None),
            P("exp", "ctx", None),
            P("exp", "ctx", None),
            P("exp", None, None, "ctx"),
            P("exp", "ctx", None),
        ),
        out_specs=(
            P("exp", "ctx", None),
            P("exp", "ctx", None),
            P("exp", "ctx", None),
            P("exp", "ctx", None),
            P("exp", None, None, "ctx"),
            P("exp", "ctx", None),
        ),
        check_vma=False,
    )
```

profile of v0, /device:TPU:1, one launch (start us, length us, event | category | flops | bytes accessed | tf_op | source)
XLA Modules:
  0.0 736.7 jit_solution(15636822952502831941)
XLA Ops:
  9.9 2.5 convolution_convert_fusion.3
  13.8 48.0 %all_to_all.15 = bf16[32,5,2880]{2,1,0:T(8,128)(2,1)} all-to-all(bf16[32,5,2880]{2,1,0:T(8,128)(2,1)S(1)} %reshape.423), channel_id=1, replica_groups=mesh['ctx'=8,'exp'=32] {'exp'}, dimensions={0} | all-to-all | bytes 1843200 | tf_op jit(solution)/shard_map/all_to_all | solution.py:174
  61.8 2.6 reshape.424
  67.5 61.7 %all_to_all.16 = bf16[32,5,2880]{2,1,0:T(8,128)(2,1)} all-to-all(bf16[32,5,2880]{2,1,0:T(8,128)(2,1)S(1)} %reshape.421), channel_id=1, replica_groups=mesh['ctx'=8,'exp'=32] {'exp'}, dimensions={0} | all-to-all | bytes 1843200 | tf_op jit(solution)/shard_map/all_to_all | solution.py:175
  129.2 2.7 reshape.422
  131.9 3.1 collective-permute-start
  136.0 1.8 fusion.62
  138.2 3.1 copy.234
  141.4 3.9 reshape_squeeze.88
  145.4 3.1 collective-permute-start.1
  148.5 1.8 fusion.57
  151.0 4.2 collective-permute-start.2
  155.3 1.8 fusion.52
  157.2 1.8 collective-permute-done.2
  159.1 4.2 collective-permute-start.3
  163.3 1.8 fusion.47
  165.4 13.9 %collective-permute-start.4 = (bf16[2,128,256]{2,1,0:T(8,128)(2,1)S(1)}, bf16[2,128,256]{2,1,0:T(8,128)(2,1)S(1)}, u32[]{:S(2)}, u32[]{:S(2)}) collective-permute-start(bf16[2,128,256]{2,1,0:T(8,128)(2,1)S(1)} %collective-permute-done.3), channel_id=1, source_target_pairs={{0,32},{32,64},{64,96},{96,128},{128,160},{160,192},{192,224},{1,3... | collective-permute-start | bytes 393224 | tf_op jit(solution)/shard_map/ppermute | solution.py:17
  179.3 1.8 fusion.42
  181.4 20.9 %collective-permute-start.5 = (bf16[2,128,256]{2,1,0:T(8,128)(2,1)S(1)}, bf16[2,128,256]{2,1,0:T(8,128)(2,1)}, u32[]{:S(2)}, u32[]{:S(2)}) collective-permute-start(bf16[2,128,256]{2,1,0:T(8,128)(2,1)S(1)} %collective-permute-done.4), channel_id=1, source_target_pairs={{0,32},{32,64},{64,96},{96,128},{128,160},{160,192},{192,224},{1,3... | collective-permute-start | bytes 393224 | tf_op jit(solution)/shard_map/ppermute | solution.py:17
  202.3 32.6 %all-gather.5.cloned.1.call-done = bf16[1280,2880]{1,0:T(8,128)(2,1)} async-done(((bf16[160,2880]{1,0:T(8,128)(2,1)}), bf16[1280,2880]{1,0:T(8,128)(2,1)}) %all-gather.5.cloned.1.call-update) | async-done | bytes 7372816 | tf_op jit(solution)/shard_map/all_gather | solution.py:177
  234.9 8.0 %fusion.164 = f32[1280,360]{0,1:T(8,128)} fusion(bf16[1280,2880]{1,0:T(8,128)(2,1)} %all-gather.5.cloned.1.call-done, bf16[2880,360]{0,1:T(8,128)(2,1)} %reshape_squeeze.88), kind=kOutput, calls=%fused_computation.265 | convolution fusion | flops 2654208000 | bytes 11289600 | tf_op jit(solution)/shard_map/dot_general | solution.py:179
  242.9 182.0 %all-gather.3.cloned.1.call-done = bf16[1280,2880]{1,0:T(8,128)(2,1)} async-done(((bf16[160,2880]{1,0:T(8,128)(2,1)}), bf16[1280,2880]{1,0:T(8,128)(2,1)}) %all-gather.3.cloned.1.call-update) | async-done | bytes 7372816 | tf_op jit(solution)/shard_map/all_gather | solution.py:178
  424.9 6.6 multiply_convert_fusion.2
  432.4 6.4 convolution_convert_fusion
  438.9 1.9 fusion.37
  441.9 2.1 collective-permute-start.6
  444.0 1.8 fusion.32
  448.4 2.0 fusion.6
  450.4 2.0 fusion.3
  452.4 2.0 fusion.9
  454.4 2.0 fusion.12
  456.5 2.0 fusion.15
  458.5 2.0 fusion.18
  460.5 2.0 fusion.21
  462.6 2.1 fusion.24
  466.1 6.4 fusion.8
  478.0 2.0 collective-permute-start.7
  480.0 2.8 fusion.114
  484.5 11.1 %fusion.5 = (bf16[4,8,128,128]{2,3,1,0:T(8,128)(2,1)}, bf16[4,8,128,128]{2,3,1,0:T(8,128)(2,1)S(1)}, bf16[4,8,128,128]{2,3,1,0:T(8,128)(2,1)}, bf16[4,8,128,128]{2,3,1,0:T(8,128)(2,1)}, bf16[4,8,128,128]{2,3,1,0:T(8,128)(2,1)}) fusion(f32[4,128,128,8]{2,1,3,0:T(8,128)} %get-tuple-element.102, f32[4,128,128,8]{2,1,3,0:T(8,128)} %copy-done.9, ...), kind=kLoop, calls=%fused_computation.13 | loop fusion | flops 15728640 | bytes 26329088 | tf_op jit(solution)/shard_map/convert_element_type | solution.py:72
  499.3 2.8 fusion.112
  503.8 2.4 fusion.94
  507.8 2.8 fusion.110
  512.3 2.4 fusion.95
  516.3 2.8 fusion.108
  520.7 2.3 fusion.96
  524.7 2.8 fusion.106
  531.9 2.8 fusion.104
  539.2 2.8 fusion.102
  543.0 1.7 fusion.99
  550.0 15.7 %collective-permute-done.8 = f32[2,128,256]{2,1,0:T(8,128)S(1)} collective-permute-done((f32[2,128,256]{2,1,0:T(8,128)S(1)}, f32[2,128,256]{2,1,0:T(8,128)S(1)}, u32[]{:S(2)}, u32[]{:S(2)}) %collective-permute-start.8) | collective-permute-done | bytes 262176 | tf_op jit(solution)/shard_map/ppermute | solution.py:22
  566.2 12.3 %collective-permute-done.9 = f32[2,128,256]{2,1,0:T(8,128)S(1)} collective-permute-done((f32[2,128,256]{2,1,0:T(8,128)S(1)}, f32[2,128,256]{2,1,0:T(8,128)S(1)}, u32[]{:S(2)}, u32[]{:S(2)}) %collective-permute-start.9) | collective-permute-done | bytes 262176 | tf_op jit(solution)/shard_map/ppermute | solution.py:22
  579.0 11.9 %collective-permute-done.10 = f32[2,128,256]{2,1,0:T(8,128)S(1)} collective-permute-done((f32[2,128,256]{2,1,0:T(8,128)S(1)}, f32[2,128,256]{2,1,0:T(8,128)S(1)}, u32[]{:S(2)}, u32[]{:S(2)}) %collective-permute-start.10) | collective-permute-done | bytes 262176 | tf_op jit(solution)/shard_map/ppermute | solution.py:22
  591.4 15.9 %collective-permute-done.11 = f32[2,128,256]{2,1,0:T(8,128)S(1)} collective-permute-done((f32[2,128,256]{2,1,0:T(8,128)S(1)}, f32[2,128,256]{2,1,0:T(8,128)S(1)}, u32[]{:S(2)}, u32[]{:S(2)}) %collective-permute-start.11) | collective-permute-done | bytes 262176 | tf_op jit(solution)/shard_map/ppermute | solution.py:22
  607.9 36.3 %collective-permute-done.12 = f32[2,128,256]{2,1,0:T(8,128)S(1)} collective-permute-done((f32[2,128,256]{2,1,0:T(8,128)S(1)}, f32[2,128,256]{2,1,0:T(8,128)S(1)}, u32[]{:S(2)}, u32[]{:S(2)}) %collective-permute-start.12) | collective-permute-done | bytes 262176 | tf_op jit(solution)/shard_map/ppermute | solution.py:22
  645.6 13.0 %collective-permute-done.13 = f32[2,128,256]{2,1,0:T(8,128)S(1)} collective-permute-done((f32[2,128,256]{2,1,0:T(8,128)S(1)}, f32[2,128,256]{2,1,0:T(8,128)S(1)}, u32[]{:S(2)}, u32[]{:S(2)}) %collective-permute-start.13) | collective-permute-done | bytes 262176 | tf_op jit(solution)/shard_map/ppermute | solution.py:22
  658.7 4.9 reduce-scatter.2.cloned.1.call-done
  663.7 2.3 reshape.425
  666.0 22.2 %all-to-all-start.2 = ((bf16[32,5,2880]{2,1,0:T(8,128)(2,1)}), bf16[32,5,2880]{2,1,0:T(8,128)(2,1)S(1)}, u32[]{:S(2)}, u32[]{:S(2)}) async-start(bf16[32,5,2880]{2,1,0:T(8,128)(2,1)} %reshape.425), calls=%async_computation.3 | async-start | bytes 3014656 | tf_op jit(solution)/shard_map/all_to_all | solution.py:202
  691.5 7.7 %convolution_convert_fusion.1 = bf16[2880,360]{0,1:T(8,128)(2,1)} fusion(bf16[1280,2880]{1,0:T(8,128)(2,1)} %all-gather.5.cloned.1.call-done, bf16[1280,180]{0,1:T(8,128)(2,1)} %copy-done.54, bf16[1280,180]{0,1:T(8,128)(2,1)} %copy-done.53), kind=kOutput, calls=%fused_computation.1 | convolution fusion | flops 2657088000 | bytes 10368000 | tf_op jit(solution)/shard_map/dot_general | solution.py:190
  699.1 3.5 reshape.427
  702.6 4.7 copy.236
  707.3 6.0 fusion.1
  713.3 12.5 %all-to-all-done.2 = bf16[32,5,2880]{2,1,0:T(8,128)(2,1)S(1)} async-done(((bf16[32,5,2880]{2,1,0:T(8,128)(2,1)}), bf16[32,5,2880]{2,1,0:T(8,128)(2,1)S(1)}, u32[]{:S(2)}, u32[]{:S(2)}) %all-to-all-start.2) | async-done | bytes 921632 | tf_op jit(solution)/shard_map/all_to_all | solution.py:202
  727.2 2.8 fusion.2
  (220 shorter events, 59.8 us)
Async XLA Ops:
  7.2 417.7 %copy-start = (bf16[1,180,2880]{2,1,0:T(8,128)(2,1)S(1)}, bf16[1,180,2880]{2,1,0:T(8,128)(2,1)}, u32[]{:S(2)}) copy-start(bf16[1,180,2880]{2,1,0:T(8,128)(2,1)} %param.19) | copy-start | bytes 3110404
  7.2 227.7 %all-gather.5.cloned.1.call-start = ((), (), s32[]{:S(2)}) async-start(), calls=%async_computation.5 | async-start | bytes 8478720 | tf_op jit(solution)/shard_map/all_gather | solution.py:177
  61.8 2.7 copy-start.51
  61.8 2.9 copy-start.17
  64.5 360.4 %all-gather.3.cloned.1.call-start = ((), (), s32[]{:S(2)}) async-start(), calls=%async_computation.4 | async-start | bytes 8478720 | tf_op jit(solution)/shard_map/all_gather | solution.py:178
  129.2 2.8 copy-start.40
  129.2 2.8 copy-start.41
  129.2 6.2 copy-start.24
  131.9 531.8 %reduce-scatter.2.cloned.1.call-start = ((), (), s32[]{:S(2)}) async-start(), calls=%async_computation.6 | async-start | bytes 8478720 | tf_op jit(solution)/shard_map/reduce_scatter | solution.py:194
  131.9 13.3 %collective-permute-start = (bf16[2,128,256]{2,1,0:T(8,128)(2,1)S(1)}, bf16[2,128,256]{2,1,0:T(8,128)(2,1)S(1)}, u32[]{:S(2)}, u32[]{:S(2)}) collective-permute-start(bf16[2,128,256]{2,1,0:T(8,128)(2,1)S(1)} %pad_maximum_fusion.4), channel_id=1, source_target_pairs={{0,32},{32,64},{64,96},{96,128},{128,160},{160,192},{192,224},{1,3... | collective-permute-start | bytes 393224 | tf_op jit(solution)/shard_map/ppermute | solution.py:17
  135.2 2.7 copy-start.25
  135.9 314.5 %copy-start.42 = (pred[128,128]{0,1:T(8,128)(4,1)}, pred[128,128]{0,1:T(8,128)(4,1)S(1)}, u32[]{:S(2)}) copy-start(pred[128,128]{0,1:T(8,128)(4,1)S(1)} %get-tuple-element.85) | copy-start | bytes 49156
  135.9 316.5 %copy-start.37 = (pred[128,128]{0,1:T(8,128)(4,1)}, pred[128,128]{0,1:T(8,128)(4,1)S(1)}, u32[]{:S(2)}) copy-start(pred[128,128]{0,1:T(8,128)(4,1)S(1)} %get-tuple-element.83) | copy-start | bytes 49156
  135.9 318.5 %copy-start.44 = (pred[128,128]{0,1:T(8,128)(4,1)}, pred[128,128]{0,1:T(8,128)(4,1)S(1)}, u32[]{:S(2)}) copy-start(pred[128,128]{0,1:T(8,128)(4,1)S(1)} %get-tuple-element.82) | copy-start | bytes 49156
  135.9 320.5 %copy-start.45 = (pred[128,128]{0,1:T(8,128)(4,1)}, pred[128,128]{0,1:T(8,128)(4,1)S(1)}, u32[]{:S(2)}) copy-start(pred[128,128]{0,1:T(8,128)(4,1)S(1)} %get-tuple-element.81) | copy-start | bytes 49156
  136.0 322.5 %copy-start.46 = (pred[128,128]{0,1:T(8,128)(4,1)}, pred[128,128]{0,1:T(8,128)(4,1)S(1)}, u32[]{:S(2)}) copy-start(pred[128,128]{0,1:T(8,128)(4,1)S(1)} %get-tuple-element.80) | copy-start | bytes 49156
  136.0 324.5 %copy-start.47 = (pred[128,128]{0,1:T(8,128)(4,1)}, pred[128,128]{0,1:T(8,128)(4,1)S(1)}, u32[]{:S(2)}) copy-start(pred[128,128]{0,1:T(8,128)(4,1)S(1)} %get-tuple-element.79) | copy-start | bytes 49156
  136.0 328.7 %copy-start.39 = (pred[128,128]{0,1:T(8,128)(4,1)}, pred[128,128]{0,1:T(8,128)(4,1)S(1)}, u32[]{:S(2)}) copy-start(pred[128,128]{0,1:T(8,128)(4,1)S(1)} %get-tuple-element.78) | copy-start | bytes 49156
  145.4 5.5 collective-permute-start.1
  151.0 7.9 %collective-permute-start.2 = (bf16[2,128,256]{2,1,0:T(8,128)(2,1)S(1)}, bf16[2,128,256]{2,1,0:T(8,128)(2,1)S(1)}, u32[]{:S(2)}, u32[]{:S(2)}) collective-permute-start(bf16[2,128,256]{2,1,0:T(8,128)(2,1)S(1)} %collective-permute-done.1), channel_id=1, source_target_pairs={{0,32},{32,64},{64,96},{96,128},{128,160},{160,192},{192,224},{1,3... | collective-permute-start | bytes 393224 | tf_op jit(solution)/shard_map/ppermute | solution.py:17
  159.1 6.2 collective-permute-start.3
  165.4 15.8 %collective-permute-start.4 = (bf16[2,128,256]{2,1,0:T(8,128)(2,1)S(1)}, bf16[2,128,256]{2,1,0:T(8,128)(2,1)S(1)}, u32[]{:S(2)}, u32[]{:S(2)}) collective-permute-start(bf16[2,128,256]{2,1,0:T(8,128)(2,1)S(1)} %collective-permute-done.3), channel_id=1, source_target_pairs={{0,32},{32,64},{64,96},{96,128},{128,160},{160,192},{192,224},{1,3... | collective-permute-start | bytes 393224 | tf_op jit(solution)/shard_map/ppermute | solution.py:17
  181.4 257.5 %copy-start.18 = (bf16[1,128,256]{1,2,0:T(8,128)(2,1)}, bf16[1,128,256]{1,2,0:T(8,128)(2,1)S(1)}, u32[]{:S(2)}) copy-start(bf16[1,128,256]{1,2,0:T(8,128)(2,1)S(1)} %copy.180) | copy-start | bytes 196612
  181.4 259.5 %collective-permute-start.5 = (bf16[2,128,256]{2,1,0:T(8,128)(2,1)S(1)}, bf16[2,128,256]{2,1,0:T(8,128)(2,1)}, u32[]{:S(2)}, u32[]{:S(2)}) collective-permute-start(bf16[2,128,256]{2,1,0:T(8,128)(2,1)S(1)} %collective-permute-done.4), channel_id=1, source_target_pairs={{0,32},{32,64},{64,96},{96,128},{128,160},{160,192},{192,224},{1,3... | collective-permute-start | bytes 393224 | tf_op jit(solution)/shard_map/ppermute | solution.py:17
  424.9 7.5 %copy-start.16 = (bf16[2880,360]{0,1:T(8,128)(2,1)S(1)}, bf16[2880,360]{0,1:T(8,128)(2,1)}, u32[]{:S(2)}) copy-start(bf16[2880,360]{0,1:T(8,128)(2,1)} %reshape_squeeze.88) | copy-start | bytes 6220804
  441.9 5.0 copy-start.20
  441.9 4.2 collective-permute-start.6
  446.2 4.2 copy-start.22
  446.3 2.1 copy-start.8
  446.8 3.6 copy-start.9
  456.5 2.0 copy-start.3
  460.5 2.0 copy-start.4
  466.0 6.5 copy-start.50
  476.3 8.2 %copy-start.43 = (pred[128,128]{0,1:T(8,128)(4,1)S(1)}, pred[128,128]{0,1:T(8,128)(4,1)}, u32[]{:S(2)}) copy-start(pred[128,128]{0,1:T(8,128)(4,1)} %copy-done.42) | copy-start | bytes 49156
  478.0 68.4 %collective-permute-start.7 = (f32[2,128,256]{2,1,0:T(8,128)}, f32[2,128,256]{2,1,0:T(8,128)}, u32[]{:S(2)}, u32[]{:S(2)}) collective-permute-start(f32[2,128,256]{2,1,0:T(8,128)} %pad_maximum_fusion.3), channel_id=1, source_target_pairs={{0,32},{32,64},{64,96},{96,128},{128,160},{160,192},{192,224},{224... | collective-permute-start | bytes 786440 | tf_op jit(solution)/shard_map/ppermute | solution.py:22
  527.5 4.4 copy-start.49
  543.0 3.4 copy-start.32
  546.3 19.4 %copy-start.35 = (f32[1,128,256]{2,1,0:T(8,128)S(1)}, f32[1,128,256]{2,1,0:T(8,128)}, u32[]{:S(2)}) copy-start(f32[1,128,256]{2,1,0:T(8,128)} %copy.211) | copy-start | bytes 393220
  546.3 19.4 %copy-start.36 = (f32[1,128,256]{2,1,0:T(8,128)S(1)}, f32[1,128,256]{2,1,0:T(8,128)}, u32[]{:S(2)}) copy-start(f32[1,128,256]{2,1,0:T(8,128)} %copy.210) | copy-start | bytes 393220
  547.5 18.4 %copy-start.12 = (bf16[4,8,128,128]{2,3,1,0:T(8,128)(2,1)S(1)}, bf16[4,8,128,128]{2,3,1,0:T(8,128)(2,1)}, u32[]{:S(2)}) copy-start(bf16[4,8,128,128]{2,3,1,0:T(8,128)(2,1)} %get-tuple-element.71) | copy-start | bytes 3145732
  547.5 18.3 %collective-permute-start.8 = (f32[2,128,256]{2,1,0:T(8,128)S(1)}, f32[2,128,256]{2,1,0:T(8,128)S(1)}, u32[]{:S(2)}, u32[]{:S(2)}) collective-permute-start(f32[2,128,256]{2,1,0:T(8,128)S(1)} %maximum_add_fusion), channel_id=1, source_target_pairs={{0,32},{32,64},{64,96},{96,128},{128,160},{160,192},{192,224},{224... | collective-permute-start | bytes 786440 | tf_op jit(solution)/shard_map/ppermute | solution.py:22
  550.0 28.5 %copy-start.33 = (f32[1,128,256]{2,1,0:T(8,128)S(1)}, f32[1,128,256]{2,1,0:T(8,128)}, u32[]{:S(2)}) copy-start(f32[1,128,256]{2,1,0:T(8,128)} %copy.215) | copy-start | bytes 393220
  550.0 28.5 %copy-start.34 = (f32[1,128,256]{2,1,0:T(8,128)S(1)}, f32[1,128,256]{2,1,0:T(8,128)}, u32[]{:S(2)}) copy-start(f32[1,128,256]{2,1,0:T(8,128)} %copy.214) | copy-start | bytes 393220
  565.8 12.9 %copy-start.11 = (bf16[4,8,128,128]{2,3,1,0:T(8,128)(2,1)S(1)}, bf16[4,8,128,128]{2,3,1,0:T(8,128)(2,1)}, u32[]{:S(2)}) copy-start(bf16[4,8,128,128]{2,3,1,0:T(8,128)(2,1)} %get-tuple-element.72) | copy-start | bytes 3145732
  565.8 12.7 %collective-permute-start.9 = (f32[2,128,256]{2,1,0:T(8,128)S(1)}, f32[2,128,256]{2,1,0:T(8,128)S(1)}, u32[]{:S(2)}, u32[]{:S(2)}) collective-permute-start(f32[2,128,256]{2,1,0:T(8,128)S(1)} %maximum_add_fusion.1), channel_id=1, source_target_pairs={{0,32},{32,64},{64,96},{96,128},{128,160},{160,192},{192,224},{224... | collective-permute-start | bytes 786440 | tf_op jit(solution)/shard_map/ppermute | solution.py:22
  566.2 24.7 %copy-start.30 = (f32[1,128,256]{2,1,0:T(8,128)S(1)}, f32[1,128,256]{2,1,0:T(8,128)}, u32[]{:S(2)}) copy-start(f32[1,128,256]{2,1,0:T(8,128)} %copy.219) | copy-start | bytes 393220
  566.2 24.7 %copy-start.31 = (f32[1,128,256]{2,1,0:T(8,128)S(1)}, f32[1,128,256]{2,1,0:T(8,128)}, u32[]{:S(2)}) copy-start(f32[1,128,256]{2,1,0:T(8,128)} %copy.218) | copy-start | bytes 393220
  578.6 12.5 %copy-start.10 = (bf16[4,8,128,128]{2,3,1,0:T(8,128)(2,1)S(1)}, bf16[4,8,128,128]{2,3,1,0:T(8,128)(2,1)}, u32[]{:S(2)}) copy-start(bf16[4,8,128,128]{2,3,1,0:T(8,128)(2,1)} %get-tuple-element.73) | copy-start | bytes 3145732
  578.6 12.3 %collective-permute-start.10 = (f32[2,128,256]{2,1,0:T(8,128)S(1)}, f32[2,128,256]{2,1,0:T(8,128)S(1)}, u32[]{:S(2)}, u32[]{:S(2)}) collective-permute-start(f32[2,128,256]{2,1,0:T(8,128)S(1)} %maximum_add_fusion.2), channel_id=1, source_target_pairs={{0,32},{32,64},{64,96},{96,128},{128,160},{160,192},{192,224},{224... | collective-permute-start | bytes 786440 | tf_op jit(solution)/shard_map/ppermute | solution.py:22
  579.0 28.3 %copy-start.28 = (f32[1,128,256]{2,1,0:T(8,128)S(1)}, f32[1,128,256]{2,1,0:T(8,128)}, u32[]{:S(2)}) copy-start(f32[1,128,256]{2,1,0:T(8,128)} %copy.223) | copy-start | bytes 393220
  579.0 28.3 %copy-start.29 = (f32[1,128,256]{2,1,0:T(8,128)S(1)}, f32[1,128,256]{2,1,0:T(8,128)}, u32[]{:S(2)}) copy-start(f32[1,128,256]{2,1,0:T(8,128)} %copy.222) | copy-start | bytes 393220
  591.0 16.6 %copy-start.19 = (bf16[1,128,256]{1,2,0:T(8,128)(2,1)S(1)}, bf16[1,128,256]{1,2,0:T(8,128)(2,1)}, u32[]{:S(2)}) copy-start(bf16[1,128,256]{1,2,0:T(8,128)(2,1)} %copy-done.18) | copy-start | bytes 196612
  591.0 16.3 %collective-permute-start.11 = (f32[2,128,256]{2,1,0:T(8,128)S(1)}, f32[2,128,256]{2,1,0:T(8,128)S(1)}, u32[]{:S(2)}, u32[]{:S(2)}) collective-permute-start(f32[2,128,256]{2,1,0:T(8,128)S(1)} %maximum_add_fusion.3), channel_id=1, source_target_pairs={{0,32},{32,64},{64,96},{96,128},{128,160},{160,192},{192,224},{224... | collective-permute-start | bytes 786440 | tf_op jit(solution)/shard_map/ppermute | solution.py:22
  591.4 52.9 %copy-start.26 = (f32[1,128,256]{2,1,0:T(8,128)S(1)}, f32[1,128,256]{2,1,0:T(8,128)}, u32[]{:S(2)}) copy-start(f32[1,128,256]{2,1,0:T(8,128)} %copy.227) | copy-start | bytes 393220
  591.4 52.9 %copy-start.27 = (f32[1,128,256]{2,1,0:T(8,128)S(1)}, f32[1,128,256]{2,1,0:T(8,128)}, u32[]{:S(2)}) copy-start(f32[1,128,256]{2,1,0:T(8,128)} %copy.226) | copy-start | bytes 393220
  607.3 37.1 %copy-start.21 = (bf16[1,128,256]{1,2,0:T(8,128)(2,1)S(1)}, bf16[1,128,256]{1,2,0:T(8,128)(2,1)}, u32[]{:S(2)}) copy-start(bf16[1,128,256]{1,2,0:T(8,128)(2,1)} %copy-done.20) | copy-start | bytes 196612
  607.3 36.9 %collective-permute-start.12 = (f32[2,128,256]{2,1,0:T(8,128)S(1)}, f32[2,128,256]{2,1,0:T(8,128)S(1)}, u32[]{:S(2)}, u32[]{:S(2)}) collective-permute-start(f32[2,128,256]{2,1,0:T(8,128)S(1)} %maximum_add_fusion.4), channel_id=1, source_target_pairs={{0,32},{32,64},{64,96},{96,128},{128,160},{160,192},{192,224},{224... | collective-permute-start | bytes 786440 | tf_op jit(solution)/shard_map/ppermute | solution.py:22
  644.3 14.3 %collective-permute-start.13 = (f32[2,128,256]{2,1,0:T(8,128)S(1)}, f32[2,128,256]{2,1,0:T(8,128)S(1)}, u32[]{:S(2)}, u32[]{:S(2)}) collective-permute-start(f32[2,128,256]{2,1,0:T(8,128)S(1)} %maximum_add_fusion.5), channel_id=1, source_target_pairs={{0,32},{32,64},{64,96},{96,128},{128,160},{160,192},{192,224},{224... | collective-permute-start | bytes 786440 | tf_op jit(solution)/shard_map/ppermute | solution.py:22
  658.6 32.2 %collective-permute-start.14 = (bf16[2,128,256]{2,1,0:T(8,128)(2,1)S(1)}, bf16[2,128,256]{2,1,0:T(8,128)(2,1)S(1)}, u32[]{:S(2)}, u32[]{:S(2)}) collective-permute-start(bf16[2,128,256]{2,1,0:T(8,128)(2,1)S(1)} %maximum_add_fusion.6), channel_id=1, source_target_pairs={{0,32},{32,64},{64,96},{96,128},{128,160},{160,192},{192,224},{224... | collective-permute-start | bytes 393224 | tf_op jit(solution)/shard_map/ppermute | solution.py:22
  666.0 22.2 %copy-start.15 = (bf16[4,8,128,128]{2,3,1,0:T(8,128)(2,1)S(1)}, bf16[4,8,128,128]{2,3,1,0:T(8,128)(2,1)}, u32[]{:S(2)}) copy-start(bf16[4,8,128,128]{2,3,1,0:T(8,128)(2,1)} %get-tuple-element.69) | copy-start | bytes 3145732
  666.0 22.2 %copy-start.23 = (bf16[1,128,256]{1,2,0:T(8,128)(2,1)S(1)}, bf16[1,128,256]{1,2,0:T(8,128)(2,1)}, u32[]{:S(2)}) copy-start(bf16[1,128,256]{1,2,0:T(8,128)(2,1)} %copy-done.22) | copy-start | bytes 196612
  666.0 59.7 %all-to-all-start.2 = ((bf16[32,5,2880]{2,1,0:T(8,128)(2,1)}), bf16[32,5,2880]{2,1,0:T(8,128)(2,1)S(1)}, u32[]{:S(2)}, u32[]{:S(2)}) async-start(bf16[32,5,2880]{2,1,0:T(8,128)(2,1)} %reshape.425), calls=%async_computation.3 | async-start | bytes 3014656 | tf_op jit(solution)/shard_map/all_to_all | solution.py:202
  702.6 4.7 copy-start.52
  707.3 22.7 %copy-start.1 = (bf16[1,180,2880]{2,1,0:T(8,128)(2,1)S(1)}, bf16[1,180,2880]{2,1,0:T(8,128)(2,1)}, u32[]{:S(2)}) copy-start(bf16[1,180,2880]{2,1,0:T(8,128)(2,1)} %param.19) | copy-start | bytes 3110404
  (10 other events, 14.5 us)
Sparse Core Ops, SparseCore 0:
  64.6 170.2 all-gather.4
  237.5 187.3 all-gather.2
  439.0 224.6 reduce-scatter.1
where the time goes:
time: 748 us; the launch traced here: 737 us
  waiting for transfers between devices  340 us (45%)
  matrix products  111 us (15%)
  blocking collectives  110 us (15%)
  starting transfers between devices  77.7 us (10%)
  local copies, waits for them, and re-layouts  60.2 us (8%)
  other arithmetic  23.4 us (3%)
  between operations  15.1 us (2%)
    all_gather x1, waiting for transfers between devices, expert_grads(): lax.all_gather(arrived[1].reshape(slot_count, width), 'ctx', axis=0, tile...  182 us
    ppermute x8, waiting for transfers between devices, from_behind_2(): lax.ppermute(shard, axis, [(i, (i + by) % length) for i in range(length)])  105 us
    all_to_all x1, blocking collectives, expert_grads(): lax.all_to_all(sent_grads, 'exp', split_axis=0, concat_axis=0, tiled=True)  61.7 us
    ppermute x7, starting transfers between devices, from_behind(): return lax.ppermute(shard, axis, pairs)  51.6 us
    all_to_all x1, blocking collectives, expert_grads(): lax.all_to_all(sent_rows, 'exp', split_axis=0, concat_axis=0, tiled=True)  48 us
    all_gather x1, waiting for transfers between devices, expert_grads(): lax.all_gather(arrived[0].reshape(slot_count, width), 'ctx', axis=0, tile...  32.6 us
    all_to_all x1, starting transfers between devices, expert_grads(): lax.all_to_all(summed.reshape(experts_here, CAP, width), 'exp', split_axi...  22.2 us
    dot_general x8, matrix products, backward_block(): jnp.einsum('hgij,ihgd->jhd', weights.astype(jnp.bfloat16), grad_heads, pr...  20.1 us
  transfers between devices with their start and end apart: 19, of which 13 were waited for; matrix products, arithmetic and copies ran while one was open for 24% of the time, Pallas kernels for 0%

commit v1 on v0

v1 whole, which is shorter than its diff:
```python
import functools

import jax
import jax.numpy as jnp
import numpy as np
from jax import lax
from jax.experimental import pallas as pl
from jax.experimental.pallas import tpu as pltpu
from jax.sharding import PartitionSpec as P

HEAD = 64
CAP = 5
TOK = 128
WIDTH = 2880
FOLD = 1920
BACK = 1024
PAD = 192
EXPERTS = 32
MESH = pl.DeviceIdType.MESH
MIB = 1024 * 1024
SCALE = 0.125
EXP_SCALE = 0.125 * 1.4426950408889634


def nt(a, b):
    return lax.dot_general(a, b, (((1,), (1,)), ((), ())), preferred_element_type=jnp.float32)


def tn(a, b):
    return lax.dot_general(a, b, (((0,), (0,)), ((), ())), preferred_element_type=jnp.float32)


def nn(a, b):
    return lax.dot_general(a, b, (((1,), (0,)), ((), ())), preferred_element_type=jnp.float32)


def attention_body(c, q_ref, g_ref, kv_ref, dq_ref, dkv_ref, s_ref, p_ref, kz_ref, vz_ref, q4, g4, dk2, dv2, dq4):
    length = q_ref.shape[0]
    lane = lax.broadcasted_iota(jnp.int32, (length, 128), 1)
    low = lane < HEAD
    krow = lax.broadcasted_iota(jnp.int32, (2 * length, 512), 0) % length
    qcol = lax.broadcasted_iota(jnp.int32, (2 * length, 512), 1) % length
    diag = krow <= qcol

    def spread(tile, h):
        tile = tile.astype(jnp.float32)
        swapped = pltpu.roll(tile, HEAD, 1)
        first, second = (tile, swapped) if h % 2 == 0 else (swapped, tile)
        return jnp.concatenate([jnp.where(low, first, 0.0), jnp.where(low, 0.0, second)], axis=0).astype(jnp.bfloat16)

    def halves(stat):
        return jnp.concatenate([jnp.broadcast_to(stat[0:1], (length, 512)), jnp.broadcast_to(stat[1:2], (length, 512))], axis=0)

    def by_half(x, op):
        return jnp.concatenate([op(x[:length], axis=0, keepdims=True), op(x[length:], axis=0, keepdims=True)], axis=0)

    for h in range(4):
        t = h // 2
        for i in range(4):
            cols = slice(h * 512 + i * 128, h * 512 + (i + 1) * 128)
            q4[i * length : (i + 1) * length, :] = q_ref[:, cols]
            g4[i * length : (i + 1) * length, :] = g_ref[:, cols]

        def score_step(j, top, masked):
            keys = spread(kv_ref[j, :, t * 128 : (t + 1) * 128], h)
            kz_ref[j] = keys
            vz_ref[j] = spread(kv_ref[j, :, 256 + t * 128 : 256 + (t + 1) * 128], h)
            s = nt(keys, q4[...])
            if masked:
                s = jnp.where(diag, s, -1e30)
            s_ref[j] = s
            return jnp.maximum(top, by_half(s, jnp.max))

        top = lax.fori_loop(0, c, lambda j, m: score_step(j, m, False), jnp.full((2, 512), -1e30, jnp.float32))
        top = score_step(c, top, True)
        top_wide = halves(top)

        def sum_step(j, state):
            total, dot = state
            p = jnp.exp2((s_ref[j] - top_wide) * EXP_SCALE)
            dp = nt(vz_ref[j], g4[...])
            s_ref[j] = p
            p_ref[j] = dp
            return total + by_half(p, jnp.sum), dot + by_half(p * dp, jnp.sum)

        zero = jnp.zeros((2, 512), jnp.float32)
        total, dot = lax.fori_loop(0, c + 1, sum_step, (zero, zero))
        inverse = 1.0 / total
        inverse_wide = halves(inverse)
        delta_wide = halves(dot * inverse)
        dq4[...] = jnp.zeros_like(dq4)

        def grad_step(j, carry):
            p = s_ref[j] * inverse_wide
            ds = (p * (p_ref[j] - delta_wide)).astype(jnp.bfloat16)
            dv2[j] = nn(p.astype(jnp.bfloat16), g4[...])
            dk2[j] = nn(ds, q4[...])
            dq4[...] += tn(ds, kz_ref[j])
            return carry

        lax.fori_loop(0, c + 1, grad_step, 0)
        for i in range(4):
            cols = slice(h * 512 + i * 128, h * 512 + (i + 1) * 128)
            dq_ref[:, cols] = (dq4[i * length : (i + 1) * length, :] * SCALE).astype(jnp.bfloat16)

        def out_step(j, carry):
            for ref, base, scale in ((dk2, 0, SCALE), (dv2, 256, 1.0)):
                even, odd = ref[j, :length, :], ref[j, length:, :]
                if h % 2 == 0:
                    whole = even + pltpu.roll(odd, HEAD, 1)
                else:
                    whole = pltpu.roll(even, HEAD, 1) + odd
                whole = (whole * scale).astype(jnp.bfloat16)
                cols = slice(base + t * 128, base + (t + 1) * 128)
                if h % 2 == 0:
                    dkv_ref[j, :, cols] = whole
                else:
                    dkv_ref[j, :, cols] = jnp.where(low, dkv_ref[j, :, cols], whole)
            return carry

        lax.fori_loop(0, c + 1, out_step, 0)


ATTENTION_SCRATCH = [
    pltpu.VMEM((8, 256, 512), jnp.float32),
    pltpu.VMEM((8, 256, 512), jnp.float32),
    pltpu.VMEM((8, 256, 128), jnp.bfloat16),
    pltpu.VMEM((8, 256, 128), jnp.bfloat16),
    pltpu.VMEM((512, 128), jnp.bfloat16),
    pltpu.VMEM((512, 128), jnp.bfloat16),
    pltpu.VMEM((8, 256, 128), jnp.float32),
    pltpu.VMEM((8, 256, 128), jnp.float32),
    pltpu.VMEM((512, 128), jnp.float32),
]


def attention_kernel(*refs):
    attention_body(lax.axis_index("ctx"), *refs)


def attention_call(queries, out_grad, kv_all):
    vmem = pl.BlockSpec(memory_space=pltpu.VMEM)
    return pl.pallas_call(
        attention_kernel,
        out_shape=(
            jax.ShapeDtypeStruct(queries.shape, jnp.bfloat16),
            jax.ShapeDtypeStruct(kv_all.shape, jnp.bfloat16),
        ),
        in_specs=[vmem] * 3,
        out_specs=(vmem, vmem),
        scratch_shapes=ATTENTION_SCRATCH,
        compiler_params=pltpu.CompilerParams(vmem_limit_bytes=40 * MIB),
    )(queries, out_grad, kv_all)


def place():
    c, e = lax.axis_index("ctx"), lax.axis_index("exp")
    zh, x = c // 4, c % 4
    zl = (e // 2) % 4
    yc = (e // 8) * 2 + e % 2
    return c, e, zh, x, zh * 4 + zl, yc


def at(z, yc, x):
    return ((z // 4) * 4 + x, (yc // 2) * 8 + (z % 4) * 2 + yc % 2)


def greet(x, z, yc, c, e):
    barrier = pltpu.get_barrier_semaphore()

    def peer(i, carry):
        pl.semaphore_signal(barrier, inc=1, device_id=at((z + i // 8) % 8, (yc + i % 8) % 8, x), device_id_type=MESH)
        return carry

    lax.fori_loop(1, 64, peer, 0)
    return barrier


ORDER = (4, 3, 5, 2, 6, 1, 7, 0)


def send_kernel(pk, kv, w3, ra, rb, kv_all, w6, s_send, s_recv, f_send, f_recv, w_sem, k_send, k_recv, local):
    c, e, zh, x, z, yc = place()
    wx = x + 1 - 2 * (x % 2)
    rx = 3 - x
    barrier = greet(x, z, yc, c, e)
    for i in range(1, 4):
        pl.semaphore_signal(barrier, inc=1, device_id=(zh * 4 + (x + i) % 4, e), device_id_type=MESH)
    own_kv = pltpu.make_async_copy(kv, kv_all.at[c], local.at[0])
    own_kv.start()
    own_w = pltpu.make_async_copy(w3, w6.at[:, 0], local.at[1])
    own_w.start()
    own_rows = pltpu.make_async_copy(pk.at[e], ra.at[z * 8 + yc], local.at[2])
    own_rows.start()
    pl.semaphore_wait(barrier, 66)

    def kv_copy(src, block, i, to):
        return pltpu.make_async_remote_copy(src, kv_all.at[block], k_send.at[i], k_recv.at[block], device_id=to, device_id_type=MESH)

    other = (4 + x, e)

    @pl.when(zh == 0)
    def _():
        kv_copy(kv, c, 0, other).start()

    for i in range(1, 4):
        kv_copy(kv, c, i, (zh * 4 + (x + i) % 4, e)).start()

    weights = pltpu.make_async_remote_copy(w3, w6.at[:, 1], w_sem.at[0], w_sem.at[1], device_id=(zh * 4 + wx, e), device_id_type=MESH)
    weights.start()

    for dz in ORDER:
        zt = (z + dz) % 8

        def send_one(d, carry, zt=zt):
            yt = (yc + d) % 8
            to = at(zt, yt, x)
            pltpu.make_async_remote_copy(
                pk.at[to[1]], ra.at[z * 8 + yc], s_send, s_recv.at[z], device_id=to, device_id_type=MESH
            ).start()
            return carry

        lax.fori_loop(1 if dz == 0 else 0, 8, send_one, 0)

    @pl.when(zh == 1)
    def _():
        kv_copy(kv, x, 0, other).wait_recv()
        for i in range(1, 4):
            kv_copy(kv_all.at[x], x, 3 + i, (4 + (x + i) % 4, e)).start()

    def forward(zs):
        return pltpu.make_async_remote_copy(
            ra.at[pl.ds(zs * 8, 8)], rb.at[pl.ds(zs * 8, 8)], f_send.at[zs], f_recv.at[zs], device_id=(zh * 4 + rx, e), device_id_type=MESH
        )

    for dz in (0, 1, 7, 2, 6, 3, 5, 4):
        zs = (z + dz) % 8
        if dz == 0:
            own_rows.wait()
            pltpu.make_async_copy(ra.at[pl.ds(0, 7)], ra.at[pl.ds(0, 7)], s_recv.at[zs]).wait()
        else:
            pltpu.make_async_copy(ra.at[pl.ds(0, 8)], ra.at[pl.ds(0, 8)], s_recv.at[zs]).wait()
        forward(zs).start()

    own_kv.wait()
    own_w.wait()
    weights.wait()
    for i in range(1, 4):
        kv_copy(kv, c, i, (zh * 4 + (x + i) % 4, e)).wait_send()
        block = zh * 4 + (x + i) % 4
        kv_copy(kv, block, i, other).wait_recv()

    @pl.when(zh == 0)
    def _():
        kv_copy(kv, c, 0, other).wait_send()

    @pl.when(zh == 1)
    def _():
        for i in range(1, 4):
            kv_copy(kv, x, 3 + i, other).wait_send()
            kv_copy(kv, (x + i) % 4, 3 + i, other).wait_recv()

    most = ra.at[pl.ds(0, 63)]
    pltpu.make_async_copy(most, most, s_send).wait()
    for zs in range(8):
        forward(zs).wait()


def send_call(pk, kv, w3):
    hbm = pl.BlockSpec(memory_space=pl.ANY)
    rows = jax.ShapeDtypeStruct((64, 16, FOLD), jnp.bfloat16)
    return pl.pallas_call(
        send_kernel,
        out_shape=(
            rows,
            rows,
            jax.ShapeDtypeStruct((8, TOK, 512), jnp.bfloat16),
            jax.ShapeDtypeStruct((3, 2, PAD, WIDTH), jnp.bfloat16),
        ),
        in_specs=[hbm] * 3,
        out_specs=(hbm,) * 4,
        scratch_shapes=[
            pltpu.SemaphoreType.DMA,
            pltpu.SemaphoreType.DMA((8,)),
            pltpu.SemaphoreType.DMA((8,)),
            pltpu.SemaphoreType.DMA((8,)),
            pltpu.SemaphoreType.DMA((2,)),
            pltpu.SemaphoreType.DMA((7,)),
            pltpu.SemaphoreType.DMA((8,)),
            pltpu.SemaphoreType.DMA((3,)),
        ],
        compiler_params=pltpu.CompilerParams(collective_id=0, has_side_effects=True),
    )(pk, kv, w3)


def return_kernel(rows, eg, xg, dkv, back, w_in, dkv_in, own, theirs, r_send, r_recv, b_send, b_recv, w_sem, k_send, k_recv, local):
    c, e, zh, x, z, yc = place()
    wx = x + 1 - 2 * (x % 2)
    rx = 3 - x
    barrier = greet(x, z, yc, c, e)
    for i in range(1, 4):
        pl.semaphore_signal(barrier, inc=1, device_id=(zh * 4 + (x + i) % 4, e), device_id_type=MESH)
    for i in range(1, 4):
        pl.semaphore_signal(barrier, inc=1, device_id=((1 - zh) * 4 + (x + i) % 4, e), device_id_type=MESH)

    def load(zs):
        return pltpu.make_async_copy(rows.at[0, zs], own.at[zs], local.at[zs])

    for dz in range(8):
        load((z + dz) % 8).start()
    pl.semaphore_wait(barrier, 69)

    def swap(zs):
        return pltpu.make_async_remote_copy(
            rows.at[1, zs], theirs.at[zs], r_send.at[zs], r_recv.at[zs], device_id=(zh * 4 + rx, e), device_id_type=MESH
        )

    for dz in ORDER:
        swap((z + dz) % 8).start()
    wto = (zh * 4 + wx, e)
    w_copies = (
        pltpu.make_async_remote_copy(eg.at[:, 1], w_in.at[pl.ds(0, 2)], w_sem.at[0], w_sem.at[1], device_id=wto, device_id_type=MESH),
        pltpu.make_async_remote_copy(xg.at[1], w_in.at[2], w_sem.at[2], w_sem.at[3], device_id=wto, device_id_type=MESH),
    )
    for copy in w_copies:
        copy.start()

    def kv_copy(i, home, source):
        return pltpu.make_async_remote_copy(
            dkv.at[home], dkv_in.at[source], k_send.at[i], k_recv.at[source], device_id=(home, e), device_id_type=MESH
        )

    for i in range(1, 8):
        home = (c + i) % 8

        @pl.when(home < c)
        def _(i=i, home=home):
            kv_copy(i, home, c).start()

    own_kv = pltpu.make_async_copy(dkv.at[c], dkv_in.at[c], local.at[8])
    own_kv.start()

    for dz in ORDER:
        zs = (z + dz) % 8
        load(zs).wait()
        swap(zs).wait_recv()

        def add(d, carry, zs=zs):
            total = own[zs, d].astype(jnp.float32) + theirs[zs, d].astype(jnp.float32)
            own[zs, d] = total.astype(jnp.bfloat16)
            return carry

        lax.fori_loop(0, 8, add, 0)

        def send_one(d, carry, zs=zs):
            ys = (yc + d) % 8
            to = at(zs, ys, x)
            pltpu.make_async_remote_copy(
                own.at[zs, ys], back.at[zh * EXPERTS + e], b_send, b_recv, device_id=to, device_id_type=MESH
            ).start()
            return carry

        lax.fori_loop(1 if dz == 0 else 0, 8, send_one, 0)
        if dz == 0:
            own_back = pltpu.make_async_copy(own.at[z, yc], back.at[zh * EXPERTS + e], local.at[9])
            own_back.start()

    own_kv.wait()
    for copy in w_copies:
        copy.wait()
    for i in range(1, 8):
        partner = (c + i) % 8

        @pl.when(partner < c)
        def _(i=i, partner=partner):
            kv_copy(i, partner, c).wait_send()

        @pl.when(partner > c)
        def _(i=i, partner=partner):
            kv_copy(i, partner, partner).wait_recv()

    for zs in range(8):
        swap(zs).wait_send()
    own_back.wait()
    most = back.at[pl.ds(0, 63)]
    for sem in (b_send, b_recv):
        pltpu.make_async_copy(most, most, sem).wait()


def return_call(rows, eg, xg, dkv):
    hbm = pl.BlockSpec(memory_space=pl.ANY)
    return pl.pallas_call(
        return_kernel,
        out_shape=(
            jax.ShapeDtypeStruct((2 * EXPERTS, 16, BACK), jnp.bfloat16),
            jax.ShapeDtypeStruct((3, PAD, WIDTH), jnp.bfloat16),
            jax.ShapeDtypeStruct((8, TOK, 512), jnp.bfloat16),
        ),
        in_specs=[hbm] * 4,
        out_specs=(hbm,) * 3,
        scratch_shapes=[
            pltpu.VMEM((8, 8, 16, BACK), jnp.bfloat16),
            pltpu.VMEM((8, 8, 16, BACK), jnp.bfloat16),
            pltpu.SemaphoreType.DMA((8,)),
            pltpu.SemaphoreType.DMA((8,)),
            pltpu.SemaphoreType.DMA,
            pltpu.SemaphoreType.DMA,
            pltpu.SemaphoreType.DMA((4,)),
            pltpu.SemaphoreType.DMA((8,)),
            pltpu.SemaphoreType.DMA((8,)),
            pltpu.SemaphoreType.DMA((10,)),
        ],
        compiler_params=pltpu.CompilerParams(collective_id=1, has_side_effects=True, vmem_limit_bytes=16 * MIB),
    )(rows, eg, xg, dkv)


def pick_rows(routes, shares):
    matched = routes[:, :, None] == jnp.arange(EXPERTS)[None, None, :]
    hits = jnp.any(matched, axis=1)
    share = jnp.sum(jnp.where(matched, shares[:, :, None], 0.0), axis=1)
    before = jnp.asarray(np.tril(np.ones((TOK, TOK), np.float32), -1), jnp.bfloat16)
    earlier = jnp.dot(before, hits.astype(jnp.bfloat16), preferred_element_type=jnp.float32).astype(jnp.int32)
    row = jnp.arange(16)[None, None, :]
    chosen = hits[:, :, None] & (earlier[:, :, None] == row % CAP) & (row < 3 * CAP)
    slot_share = jnp.sum(jnp.where(chosen, share[:, :, None], 0.0), axis=0)
    return chosen, slot_share


def unfold_matrix():
    out = np.zeros((3 * 80, 256), np.float32)
    for p in range(16):
        for k in range(3):
            for s in range(CAP):
                out[k * 80 + p * CAP + s, p * 16 + k * CAP + s] = 1
    return out


UNFOLD = unfold_matrix()


def per_device(queries, key_rows, value_rows, out_grad, tokens, token_grad, route_ids, route_probs, entry_weight, exit_weight):
    f32, bf16 = jnp.float32, jnp.bfloat16
    x, g = tokens[0], token_grad[0]
    chosen, slot_share = pick_rows(route_ids[0], route_probs[0])
    part = jnp.arange(16) // CAP
    chosen3 = [(chosen & (part == k)[None, None, :]).reshape(TOK, 512).astype(bf16) for k in range(3)]

    chunks = (x[:, :FOLD], jnp.concatenate([x[:, FOLD:], g[:, FOLD:]], axis=1), g[:, :FOLD])
    packed = sum(tn(s, m) for s, m in zip(chosen3, chunks)).reshape(EXPERTS, 16, FOLD)
    is_grad = (part[:, None] == 2) | ((part[:, None] == 1) & (jnp.arange(FOLD)[None, :] >= WIDTH - FOLD))
    packed = jnp.where(is_grad[None], packed * slot_share[:, :, None], packed).astype(bf16)

    entry = entry_weight[0].transpose(1, 2, 0)
    w3 = jnp.concatenate([entry, exit_weight], axis=0)
    w3 = jnp.pad(w3, ((0, 0), (0, PAD - w3.shape[1]), (0, 0)))
    kv = jnp.concatenate([key_rows[0], value_rows[0]], axis=1)

    ra, rb, kv_all, w6 = send_call(packed, kv, w3)

    query_grad, dkv = attention_call(queries[0], out_grad[0], kv_all)

    unfold = jnp.asarray(UNFOLD, bf16)
    arrived = jnp.concatenate([ra.reshape(4, 256, FOLD), rb.reshape(4, 256, FOLD)], axis=0)
    slots = jnp.einsum("uv,bvc->buc", unfold, arrived, preferred_element_type=f32).astype(bf16)
    rest = WIDTH - FOLD
    xr = jnp.concatenate([slots[:, :80], slots[:, 80:160, :rest]], axis=2).reshape(640, WIDTH)
    gr = jnp.concatenate([slots[:, 160:], slots[:, 80:160, rest:]], axis=2).reshape(640, WIDTH)

    up_down = w6[:2].reshape(4 * PAD, WIDTH)
    leave = w6[2].reshape(2 * PAD, WIDTH)
    projected = nt(xr, up_down)
    gate, upward = projected[:, : 2 * PAD], projected[:, 2 * PAD :]
    sigma = jax.nn.sigmoid(gate)
    swish = gate * sigma
    activation = (swish * upward).astype(bf16)
    act_grad = nt(gr, leave)
    slope = sigma * (1.0 + gate * (1.0 - sigma))
    score_rows = jnp.concatenate([act_grad * upward * slope, act_grad * swish], axis=1).astype(bf16)
    row_part = nn(score_rows, up_down).astype(bf16)
    eg = tn(score_rows, xr).astype(bf16).reshape(2, 2, PAD, WIDTH)
    xg = tn(activation, gr).astype(bf16).reshape(2, PAD, WIDTH)

    row_part = jnp.pad(row_part, ((0, 0), (0, 3 * BACK - WIDTH))).reshape(8, 80, 3, BACK)
    fold = jnp.asarray(UNFOLD.reshape(3, 80, 256), bf16)
    folded = jnp.einsum("kuv,bukc->bvc", fold, row_part, preferred_element_type=f32).astype(bf16)
    folded = folded.reshape(2, 8, 8, 16, BACK)

    back, w_in, dkv_in = return_call(folded, eg, xg, dkv)

    back = back.reshape(2 * 512, BACK)
    input_grad = jnp.concatenate(
        [nn(jnp.concatenate([s, s], axis=1), back) for s in chosen3], axis=1
    )[:, :WIDTH].astype(bf16)

    c = lax.axis_index("ctx")
    later = jnp.arange(8)[:, None, None] >= c
    dkv_sum = jnp.sum(jnp.where(later, dkv_in.astype(f32), 0.0), axis=0).astype(bf16)

    hidden = exit_weight.shape[1]
    entry_grad = (eg[:, 0].astype(f32) + w_in[:2].astype(f32)).astype(bf16)[:, :hidden]
    exit_grad = (xg[0].astype(f32) + w_in[2].astype(f32)).astype(bf16)[:hidden]
    return (
        query_grad[None],
        dkv_sum[None, :, :256],
        dkv_sum[None, :, 256:],
        input_grad[None],
        entry_grad.transpose(2, 0, 1)[None],
        exit_grad[None],
    )


def solution(mesh):
    row = P("exp", "ctx", None)
    entry = P("exp", None, None, "ctx")
    return jax.shard_map(
        per_device,
        mesh=mesh,
        in_specs=(row,) * 8 + (entry, row),
        out_specs=(row,) * 4 + (entry, row),
        check_vma=False,
    )
```

time: 748 us -> 421 us (0.56); the launches traced: 737 us -> 418 us
  waiting for transfers between devices: 340 us -> 0 us
  Pallas kernels: 0 us -> 326 us
  blocking collectives: 110 us -> 0 us
  starting transfers between devices: 77.7 us -> 0 us
  matrix products: 111 us -> 34.5 us
  local copies, waits for them, and re-layouts: 60.2 us -> 43.1 us
  between operations: 15.1 us -> 1.05 us
  other arithmetic: 23.4 us -> 12.7 us
    pallas_call x0 -> x3, Pallas kernels: none -> 326 us  [the longest x1 200 us: send_call(): pl.pallas_call(send_kernel, out_shape=(rows, rows, jax.ShapeDtypeStruct((...]
    all_gather x2 -> x0, waiting for transfers between devices: 215 us -> none  [the longest x1 182 us: expert_grads(): lax.all_gather(arrived[1].reshape(slot_count, width), 'ctx', axis=0, tile...]
    all_to_all x2 -> x0, blocking collectives: 110 us -> none  [the longest x1 61.7 us: expert_grads(): lax.all_to_all(sent_grads, 'exp', split_axis=0, concat_axis=0, tiled=True)]
    ppermute x15 -> x0, waiting for transfers between devices: 108 us -> none  [the longest x8 105 us: from_behind_2(): lax.ppermute(shard, axis, [(i, (i + by) % length) for i in range(length)])]
    dot_general x48 -> x14, matrix products: 111 us -> 34.5 us  [the longest x5 9.57 us: tn(): lax.dot_general(a, b, (((0,), (0,)), ((), ())), preferred_element_type=jn...]
    ppermute x15 -> x0, starting transfers between devices: 55.3 us -> none  [the longest x7 51.6 us: from_behind(): return lax.ppermute(shard, axis, pairs)]
    all_to_all x1 -> x0, starting transfers between devices: 22.2 us -> none  [expert_grads(): lax.all_to_all(summed.reshape(experts_here, CAP, width), 'exp', split_axi...]
    convert_element_type x3 -> x1, other arithmetic: 17.5 us -> 1.68 us  [per_device(): jnp.where(is_grad[None], packed * slot_share[:, :, None], packed)]
  transfers between devices with their start and end apart: 19 -> 0, of which waited for: 13 -> 0; matrix products, arithmetic and copies ran while one was open for 24% -> 0% of each run, Pallas kernels for 0% -> 0%
where the time goes in v1:
time: 421 us; the launch traced here: 418 us
  Pallas kernels  326 us (77%)
  local copies, waits for them, and re-layouts  43.1 us (10%)
  matrix products  34.5 us (8%)
  other arithmetic  12.7 us (3%)
    pallas_call x1, Pallas kernels, send_call(): pl.pallas_call(send_kernel, out_shape=(rows, rows, jax.ShapeDtypeStruct((...  200 us
    pallas_call x1, Pallas kernels, return_call(): pl.pallas_call(return_kernel, out_shape=(jax.ShapeDtypeStruct((2 * EXPERT...  121 us
    reshape x1, local copies, waits for them, and re-layouts, per_device(): jnp.pad(row_part, ((0, 0), (0, 3 * BACK - WIDTH))).reshape(8, 80, 3, BACK)  11 us
    unnamed x39, local copies, waits for them, and re-layouts  10.5 us
    dot_general x5, matrix products, tn(): lax.dot_general(a, b, (((0,), (0,)), ((), ())), preferred_element_type=jn...  9.57 us

profile of v1, /device:TPU:1, one launch (start us, length us, event | category | flops | bytes accessed | tf_op | source)
XLA Modules:
  0.0 417.7 jit_solution(18323657881508579966)
XLA Ops:
  0.6 0.0 copy-start.8
  0.7 0.1 and.142
  0.8 0.8 fusion.43
  1.7 0.1 and.150
  1.7 0.1 and.146
  1.8 0.1 and.138
  1.9 0.9 fusion.17
  2.8 0.1 eq.89
  2.9 0.7 select_reduce_fusion.2
  3.7 0.2 select_reduce_fusion.1
  3.9 0.1 and_or_fusion
  4.0 1.5 pad_maximum_fusion.7.kv
  5.5 0.6 fusion.39
  6.1 1.0 slice.87
  7.1 1.0 slice.88
  8.1 1.8 copy.60
  9.9 0.0 copy-done.8
  9.9 2.0 fusion.12.w3
  11.9 0.7 fusion.33
  12.6 0.4 copy-done.9
  13.0 0.7 fusion.31
  13.7 0.0 copy-done.10
  13.7 0.7 add_add_fusion
  14.4 1.7 fusion.11.pk
  16.1 200.3 %shard_map.172 = (bf16[64,16,1920]{2,1,0:T(8,128)(2,1)}, bf16[64,16,1920]{2,1,0:T(8,128)(2,1)}, bf16[8,128,512]{2,1,0:T(8,128)(2,1)}, bf16[3,2,192,2880]{3,2,1,0:T(8,128)(2,1)}) custom-call(bf16[32,16,1920]{2,1,0:T(8,128)(2,1)} %fusion.11.pk, bf16[128,512]{1,0:T(8,128)(2,1)} %pad_maximum_fusion.7.kv, bf16[3,192,2880]{2,1,0:T(8,128)(2,1)} %fusion.12.w3), custom_call_target="tpu_custom_call" | custom-call | tf_op jit(solution)/shard_map/pallas_call | solution.py:272
  216.4 0.0 copy-done.12
  216.4 0.0 copy-start.4
  216.4 0.0 copy-start.5
  216.4 0.0 copy-start.6
  216.5 5.5 %convert_bitcast_fusion = bf16[8,240,1920]{2,1,0:T(8,128)(2,1)S(1)} fusion(bf16[240,256,1]{1,0,2:T(8,128)(2,1)S(1)} %copy-done.12, bf16[4,256,1920]{2,1,0:T(8,128)(2,1)} %bitcast.125, bf16[4,256,1920]{2,1,0:T(8,128)(2,1)} %bitcast.124), kind=kOutput, calls=%fused_computation.5 | convolution fusion | flops 1906851840 | bytes 15360000 | tf_op jit(solution)/shard_map/uv,bvc->buc/dot_general | solution.py:464
  222.0 0.0 copy-done.4
  222.0 0.0 copy-done.5
  222.0 0.0 copy-done.6
  222.0 5.4 %shard_map.173 = (bf16[128,2048]{1,0:T(8,128)(2,1)}, bf16[8,128,512]{2,1,0:T(8,128)(2,1)S(1)}) custom-call(bf16[128,2048]{1,0:T(8,128)(2,1)S(1)} %bitcast.104, bf16[128,2048]{1,0:T(8,128)(2,1)S(1)} %bitcast.105, bf16[8,128,512]{2,1,0:T(8,128)(2,1)S(1)} %copy-done.4), custom_call_target="tpu_custom_call" | custom-call | tf_op jit(solution)/shard_map/pallas_call | solution.py:143
  227.4 2.2 slice.71
  229.6 2.6 slice.74
  232.2 0.7 fusion.53
  232.9 0.4 fusion.52
  233.3 0.3 pad_maximum_fusion.1
  233.6 0.3 pad_maximum_fusion
  233.9 3.8 fusion.54
  237.7 2.1 multiply_convert_fusion.2
  239.8 2.0 convolution_convert_fusion.2
  241.8 5.7 %convolution_convert_fusion.1 = bf16[640,2880]{0,1:T(8,128)(2,1)} fusion(bf16[768,2880]{1,0:T(8,128)(2,1)S(1)} %bitcast.109, bf16[640,384]{0,1:T(8,128)(2,1)S(1)} %get-tuple-element.47, bf16[640,384]{0,1:T(8,128)(2,1)S(1)} %get-tuple-element.46), kind=kOutput, calls=%fused_computation.13 | convolution fusion | flops 2834964480 | bytes 9093120 | tf_op jit(solution)/shard_map/dot_general | solution.py:34
  247.5 5.5 %convolution_convert_fusion = bf16[768,2880]{0,1:T(8,128)(2,1)} fusion(bf16[640,2880]{1,0:T(8,128)(2,1)S(1)} %bitcast.111, bf16[640,384]{0,1:T(8,128)(2,1)S(1)} %get-tuple-element.47, bf16[640,384]{0,1:T(8,128)(2,1)S(1)} %get-tuple-element.46), kind=kOutput, calls=%fused_computation.12 | convolution fusion | flops 2835333120 | bytes 9093120 | tf_op jit(solution)/shard_map/dot_general | solution.py:30
  253.0 6.6 %copy.46 = bf16[768,2880]{1,0:T(8,128)(2,1)} copy(bf16[768,2880]{0,1:T(8,128)(2,1)} %convolution_convert_fusion) | data formatting | bytes 8847360 | tf_op jit(solution)/shard_map/convert_element_type | solution.py:480
  259.7 4.5 %pad.9 = bf16[640,3072]{0,1:T(8,128)(2,1)} pad(bf16[640,2880]{0,1:T(8,128)(2,1)} %convolution_convert_fusion.1, bf16[]{:T(256)} %constant.47.clone.1), padding=0_0x0_192 | pad | bytes 7618562 | tf_op jit(solution)/shard_map/jit(_pad)/pad | solution.py:483
  264.2 1.1 slice.101
  265.2 1.5 slice_bitcast_fusion
  266.8 11.0 %reshape.200 = bf16[8,80,3,1024]{1,0,3,2:T(8,128)(2,1)} reshape(bf16[640,3072]{0,1:T(8,128)(2,1)} %pad.9) | data formatting | bytes 7864320 | tf_op jit(solution)/shard_map/reshape | solution.py:483
  277.8 5.5 %bitcast_convert_fusion = bf16[8,1024,256]{1,2,0:T(8,128)(2,1)S(1)} fusion(bf16[3,80,256,1]{2,1,0,3:T(8,128)(2,1)S(1)} %copy-done.11, bf16[8,80,3,1024]{1,0,3,2:T(8,128)(2,1)} %reshape.200), kind=kOutput, calls=%fused_computation | convolution fusion | flops 1008730112 | bytes 8249344 | tf_op jit(solution)/shard_map/kuv,bukc->bvc/dot_general | solution.py:485
  283.3 120.6 %shard_map.174 = (bf16[64,16,1024]{2,1,0:T(8,128)(2,1)S(1)}, bf16[3,192,2880]{2,1,0:T(8,128)(2,1)S(1)}, bf16[8,128,512]{2,1,0:T(8,128)(2,1)S(1)}) custom-call(bf16[2,8,8,16,1024]{4,3,2,1,0:T(8,128)(2,1)S(1)} %bitcast.103, bf16[2,2,192,2880]{3,2,1,0:T(8,128)(2,1)S(1)} %bitcast.98, bf16[2,192,2880]{2,1,0:T(8,128)(2,1)S(1)} %bitcast.102, ...), custom_call_target="tpu_custom_call" | custom-call | tf_op jit(solution)/shard_map/pallas_call | solution.py:392
  404.0 0.3 select_reduce_fusion
  404.3 0.9 slice_bitcast_fusion.2
  405.2 0.5 convolution_convert_fusion.3
  405.7 0.5 convolution_convert_fusion.4
  406.2 0.5 convolution_convert_fusion.5
  406.7 0.9 fusion.20
  407.6 2.4 copy.48
  410.0 1.3 slice_bitcast_fusion.1
  411.4 2.7 fusion.18
  414.0 0.2 slice.81
  414.2 0.5 fusion.15
  414.7 3.0 copy.49
  (36 shorter events, 0.1 us)
Async XLA Ops:
  0.6 9.2 %copy-start.8 = (bf16[1,180,2880]{2,1,0:T(8,128)(2,1)S(1)}, bf16[1,180,2880]{2,1,0:T(8,128)(2,1)}, u32[]{:S(2)}) copy-start(bf16[1,180,2880]{2,1,0:T(8,128)(2,1)} %param.22) | copy-start | bytes 3110404
  11.9 1.1 copy-start.9
  11.9 1.8 copy-start.10
  16.1 200.3 %copy-start.12 = (bf16[240,256,1]{1,0,2:T(8,128)(2,1)S(1)}, bf16[240,256,1]{1,0,2:T(8,128)(2,1)}, u32[]{:S(2)}) copy-start(bf16[240,256,1]{1,0,2:T(8,128)(2,1)} %constant.68) | copy-start | bytes 368644
  216.4 5.6 %copy-start.4 = (bf16[8,128,512]{2,1,0:T(8,128)(2,1)S(1)}, bf16[8,128,512]{2,1,0:T(8,128)(2,1)}, u32[]{:S(2)}) copy-start(bf16[8,128,512]{2,1,0:T(8,128)(2,1)} %get-tuple-element.15.refs_2_) | copy-start | bytes 3145732
  216.4 5.6 %copy-start.5 = (bf16[1,128,2048]{2,1,0:T(8,128)(2,1)S(1)}, bf16[1,128,2048]{2,1,0:T(8,128)(2,1)}, u32[]{:S(2)}) copy-start(bf16[1,128,2048]{2,1,0:T(8,128)(2,1)} %param.13) | copy-start | bytes 1572868
  216.4 5.6 %copy-start.6 = (bf16[1,128,2048]{2,1,0:T(8,128)(2,1)S(1)}, bf16[1,128,2048]{2,1,0:T(8,128)(2,1)}, u32[]{:S(2)}) copy-start(bf16[1,128,2048]{2,1,0:T(8,128)(2,1)} %param.16) | copy-start | bytes 1572868
  227.4 4.8 %copy-start.2 = (bf16[8,128,512]{2,1,0:T(8,128)(2,1)}, bf16[8,128,512]{2,1,0:T(8,128)(2,1)S(1)}, u32[]{:S(2)}) copy-start(bf16[8,128,512]{2,1,0:T(8,128)(2,1)S(1)} %get-tuple-element.20.dkv) | copy-start | bytes 3145732
  259.7 5.6 %slice-start = ((s8[4521984]{0:T(1024)(128)(4,1)}), s8[4194304]{0:T(1024)(128)(4,1)S(1)}, s32[]{:S(2)}) async-start(s8[4521984]{0:T(1024)(128)(4,1)} %bitcast.93), calls=%async_computation | async-start | bytes 8388608
  259.7 5.6 %slice-start.1 = ((s8[4521984]{0:T(1024)(128)(4,1)}), s8[327680]{0:T(1024)(128)(4,1)S(1)}, s32[]{:S(2)}) async-start(s8[4521984]{0:T(1024)(128)(4,1)} %bitcast.93), calls=%async_computation.1 | async-start | bytes 655360
  266.8 11.0 %copy-start.11 = (bf16[3,80,256,1]{2,1,0,3:T(8,128)(2,1)S(1)}, bf16[3,80,256,1]{2,1,0,3:T(8,128)(2,1)}, u32[]{:S(2)}) copy-start(bf16[3,80,256,1]{2,1,0,3:T(8,128)(2,1)} %constant.69) | copy-start | bytes 368644
  266.8 16.5 %slice-start.2 = ((s8[4521984]{0:T(1024)(128)(4,1)}), s8[327680]{0:T(1024)(128)(4,1)S(1)}, s32[]{:S(2)}) async-start(s8[4521984]{0:T(1024)(128)(4,1)} %bitcast.96), calls=%async_computation.2 | async-start | bytes 655360
  277.8 5.5 %slice-start.3 = ((s8[4521984]{0:T(1024)(128)(4,1)}), s8[4194304]{0:T(1024)(128)(4,1)S(1)}, s32[]{:S(2)}) async-start(s8[4521984]{0:T(1024)(128)(4,1)} %bitcast.96), calls=%async_computation.3 | async-start | bytes 8388608
  277.8 5.5 %copy-start.3 = (bf16[8,128,512]{2,1,0:T(8,128)(2,1)S(1)}, bf16[8,128,512]{2,1,0:T(8,128)(2,1)}, u32[]{:S(2)}) copy-start(bf16[8,128,512]{2,1,0:T(8,128)(2,1)} %copy-done.2) | copy-start | bytes 3145732
  404.0 2.7 copy-start
  407.6 6.4 %copy-start.1 = (bf16[3,192,2880]{2,1,0:T(8,128)(2,1)S(1)}, bf16[3,192,2880]{2,1,0:T(8,128)(2,1)}, u32[]{:S(2)}) copy-start(bf16[3,192,2880]{2,1,0:T(8,128)(2,1)} %copy-done) | copy-start | bytes 9953284
  411.4 2.9 copy-start.7

commit v2 on v1

v2 whole, which is shorter than its diff:
```python
import functools

import jax
import jax.numpy as jnp
import numpy as np
from jax import lax
from jax.experimental import pallas as pl
from jax.experimental.pallas import tpu as pltpu
from jax.sharding import PartitionSpec as P

HEAD = 64
CAP = 5
TOK = 128
WIDTH = 2880
FOLD = 1920
BACK = 1024
PAD = 192
EXPERTS = 32
MESH = pl.DeviceIdType.MESH
MIB = 1024 * 1024
SCALE = 0.125
EXP_SCALE = 0.125 * 1.4426950408889634


def nt(a, b):
    return lax.dot_general(a, b, (((1,), (1,)), ((), ())), preferred_element_type=jnp.float32)


def tn(a, b):
    return lax.dot_general(a, b, (((0,), (0,)), ((), ())), preferred_element_type=jnp.float32)


def nn(a, b):
    return lax.dot_general(a, b, (((1,), (0,)), ((), ())), preferred_element_type=jnp.float32)


def attention_body(c, q_ref, g_ref, kv_ref, dq_ref, dkv_ref, s_ref, p_ref, kz_ref, vz_ref, q4, g4, dk2, dv2, dq4, heads=range(4)):
    length = q_ref.shape[0]
    lane = lax.broadcasted_iota(jnp.int32, (length, 128), 1)
    low = lane < HEAD
    krow = lax.broadcasted_iota(jnp.int32, (2 * length, 512), 0) % length
    qcol = lax.broadcasted_iota(jnp.int32, (2 * length, 512), 1) % length
    diag = krow <= qcol

    def spread(tile, h):
        tile = tile.astype(jnp.float32)
        swapped = pltpu.roll(tile, HEAD, 1)
        first, second = (tile, swapped) if h % 2 == 0 else (swapped, tile)
        return jnp.concatenate([jnp.where(low, first, 0.0), jnp.where(low, 0.0, second)], axis=0).astype(jnp.bfloat16)

    def halves(stat):
        return jnp.concatenate([jnp.broadcast_to(stat[0:1], (length, 512)), jnp.broadcast_to(stat[1:2], (length, 512))], axis=0)

    def by_half(x, op):
        return jnp.concatenate([op(x[:length], axis=0, keepdims=True), op(x[length:], axis=0, keepdims=True)], axis=0)

    for h in heads:
        t = h // 2
        for i in range(4):
            cols = slice(h * 512 + i * 128, h * 512 + (i + 1) * 128)
            q4[i * length : (i + 1) * length, :] = q_ref[:, cols]
            g4[i * length : (i + 1) * length, :] = g_ref[:, cols]

        def score_step(j, top, masked):
            keys = spread(kv_ref[j, :, t * 128 : (t + 1) * 128], h)
            kz_ref[j] = keys
            vz_ref[j] = spread(kv_ref[j, :, 256 + t * 128 : 256 + (t + 1) * 128], h)
            s = nt(keys, q4[...])
            if masked:
                s = jnp.where(diag, s, -1e30)
            s_ref[j] = s
            return jnp.maximum(top, by_half(s, jnp.max))

        top = lax.fori_loop(0, c, lambda j, m: score_step(j, m, False), jnp.full((2, 512), -1e30, jnp.float32))
        top = score_step(c, top, True)
        top_wide = halves(top)

        def sum_step(j, state):
            total, dot = state
            p = jnp.exp2((s_ref[j] - top_wide) * EXP_SCALE)
            dp = nt(vz_ref[j], g4[...])
            s_ref[j] = p
            p_ref[j] = dp
            return total + by_half(p, jnp.sum), dot + by_half(p * dp, jnp.sum)

        zero = jnp.zeros((2, 512), jnp.float32)
        total, dot = lax.fori_loop(0, c + 1, sum_step, (zero, zero))
        inverse = 1.0 / total
        inverse_wide = halves(inverse)
        delta_wide = halves(dot * inverse)
        dq4[...] = jnp.zeros_like(dq4)

        def grad_step(j, carry):
            p = s_ref[j] * inverse_wide
            ds = (p * (p_ref[j] - delta_wide)).astype(jnp.bfloat16)
            dv2[j] = nn(p.astype(jnp.bfloat16), g4[...])
            dk2[j] = nn(ds, q4[...])
            dq4[...] += tn(ds, kz_ref[j])
            return carry

        lax.fori_loop(0, c + 1, grad_step, 0)
        for i in range(4):
            cols = slice(h * 512 + i * 128, h * 512 + (i + 1) * 128)
            dq_ref[:, cols] = (dq4[i * length : (i + 1) * length, :] * SCALE).astype(jnp.bfloat16)

        def out_step(j, carry):
            for ref, base, scale in ((dk2, 0, SCALE), (dv2, 256, 1.0)):
                even, odd = ref[j, :length, :], ref[j, length:, :]
                if h % 2 == 0:
                    whole = even + pltpu.roll(odd, HEAD, 1)
                else:
                    whole = pltpu.roll(even, HEAD, 1) + odd
                whole = (whole * scale).astype(jnp.bfloat16)
                cols = slice(base + t * 128, base + (t + 1) * 128)
                if h % 2 == 0:
                    dkv_ref[j, :, cols] = whole
                else:
                    dkv_ref[j, :, cols] = jnp.where(low, dkv_ref[j, :, cols], whole)
            return carry

        lax.fori_loop(0, c + 1, out_step, 0)


ATTENTION_SCRATCH = [
    pltpu.VMEM((8, 256, 512), jnp.float32),
    pltpu.VMEM((8, 256, 512), jnp.float32),
    pltpu.VMEM((8, 256, 128), jnp.bfloat16),
    pltpu.VMEM((8, 256, 128), jnp.bfloat16),
    pltpu.VMEM((512, 128), jnp.bfloat16),
    pltpu.VMEM((512, 128), jnp.bfloat16),
    pltpu.VMEM((8, 256, 128), jnp.float32),
    pltpu.VMEM((8, 256, 128), jnp.float32),
    pltpu.VMEM((512, 128), jnp.float32),
]


def place():
    c, e = lax.axis_index("ctx"), lax.axis_index("exp")
    zh, x = c // 4, c % 4
    zl = (e // 2) % 4
    yc = (e // 8) * 2 + e % 2
    return c, e, zh, x, zh * 4 + zl, yc


def at(z, yc, x):
    return ((z // 4) * 4 + x, (yc // 2) * 8 + (z % 4) * 2 + yc % 2)


def greet(x, z, yc, c, e):
    barrier = pltpu.get_barrier_semaphore()

    def peer(i, carry):
        pl.semaphore_signal(barrier, inc=1, device_id=at((z + i // 8) % 8, (yc + i % 8) % 8, x), device_id_type=MESH)
        return carry

    lax.fori_loop(1, 64, peer, 0)
    return barrier


def pairs(x, e):
    core = e % 2
    near = x + 1 - 2 * (x % 2)
    far = 3 - x
    return near + core * (far - near), far + core * (near - far)


GROUPS = (1, 7, 2, 6, 0, 3, 5, 4)
SLOT = {dz: r for r, dz in enumerate(GROUPS)}
ROWS = 640


def send_kernel(
    pk, kv, gu, ex, q, g, unfold,
    xr, gr, gu2, ex2, dq, dkv,
    ra, rb, kv_all, xv, gv, s_send, s_recv, f_send, f_recv, w_sem, k_send, k_recv, local, o_sem, *scratch
):
    c, e, zh, x, z, yc = place()
    wx, rx = pairs(x, e)
    barrier = greet(x, z, yc, c, e)
    for i in range(1, 4):
        pl.semaphore_signal(barrier, inc=1, device_id=(zh * 4 + (x + i) % 4, e), device_id_type=MESH)
    own = (
        pltpu.make_async_copy(pk.at[e], ra.at[SLOT[0] * 8 + yc], local.at[0]),
        pltpu.make_async_copy(kv, kv_all.at[c], local.at[1]),
        pltpu.make_async_copy(gu, gu2.at[:, 0], local.at[2]),
        pltpu.make_async_copy(ex, ex2.at[0], local.at[3]),
    )
    for copy in own:
        copy.start()
    pl.semaphore_wait(barrier, 66)

    def kv_copy(src, block, i, to):
        return pltpu.make_async_remote_copy(src, kv_all.at[block], k_send.at[i], k_recv.at[block], device_id=to, device_id_type=MESH)

    other = (4 + x, e)

    @pl.when(zh == 0)
    def _():
        kv_copy(kv, c, 0, other).start()

    for i in range(1, 4):
        kv_copy(kv, c, i, (zh * 4 + (x + i) % 4, e)).start()

    wto = (zh * 4 + wx, e)
    weights = (
        pltpu.make_async_remote_copy(gu, gu2.at[:, 1], w_sem.at[0], w_sem.at[1], device_id=wto, device_id_type=MESH),
        pltpu.make_async_remote_copy(ex, ex2.at[1], w_sem.at[2], w_sem.at[3], device_id=wto, device_id_type=MESH),
    )
    for copy in weights:
        copy.start()

    for dz in GROUPS:
        slot = SLOT[(8 - dz) % 8]

        def send_one(d, carry, dz=dz, slot=slot):
            to = at((z + dz) % 8, (yc + d) % 8, x)
            pltpu.make_async_remote_copy(
                pk.at[to[1]], ra.at[slot * 8 + yc], s_send, s_recv.at[slot], device_id=to, device_id_type=MESH
            ).start()
            return carry

        lax.fori_loop(1 if dz == 0 else 0, 8, send_one, 0)

    @pl.when(zh == 1)
    def _():
        kv_copy(kv, x, 0, other).wait_recv()
        for i in range(1, 4):
            kv_copy(kv_all.at[x], x, 3 + i, (4 + (x + i) % 4, e)).start()

    def forward(r):
        block = pl.ds(r * 8, 8)
        return pltpu.make_async_remote_copy(
            ra.at[block], rb.at[block], f_send.at[r], f_recv.at[r], device_id=(zh * 4 + rx, e), device_id_type=MESH
        )

    def arrive(r):
        count = 8
        if GROUPS[r] == 0:
            own[0].wait()
            count = 7
        pltpu.make_async_copy(ra.at[pl.ds(0, count)], ra.at[pl.ds(0, count)], s_recv.at[r]).wait()
        forward(r).start()

    def out_copies(b):
        rows = pl.ds(b * 80, 80)
        return (
            pltpu.make_async_copy(xv.at[rows], xr.at[rows], o_sem.at[b, 0]),
            pltpu.make_async_copy(gv.at[rows], gr.at[rows], o_sem.at[b, 1]),
        )

    def spread_rows(ref, b, half):
        packets = ref[b * 16 : (b + 1) * 16].reshape(256, FOLD)
        slots = nn(unfold[...], packets)
        rest = WIDTH - FOLD
        b = b + 4 * half
        rows = slice(b * 80, (b + 1) * 80)
        xv[rows, :FOLD] = slots[:80].astype(jnp.bfloat16)
        gv[rows, :FOLD] = slots[160:].astype(jnp.bfloat16)
        xv[rows, FOLD:] = slots[80:160, :rest].astype(jnp.bfloat16)
        gv[rows, FOLD:] = slots[80:160, rest:].astype(jnp.bfloat16)
        for copy in out_copies(b):
            copy.start()

    own[1].wait()
    for i in range(1, 4):
        kv_copy(kv, zh * 4 + (x + i) % 4, i, other).wait_recv()

    @pl.when(zh == 1)
    def _():
        for i in range(1, 4):
            kv_copy(kv, (x + i) % 4, 3 + i, other).wait_recv()

    def attend(heads):
        attention_body(c, q, g, kv_all, dq, dkv, *scratch, heads=heads)

    arrive(0)
    arrive(1)
    attend((0, 1))
    arrive(2)
    arrive(3)
    attend((2, 3))
    spread_rows(ra, 0, 0)
    spread_rows(ra, 1, 0)
    arrive(4)
    arrive(5)
    spread_rows(ra, 2, 0)
    arrive(6)
    arrive(7)
    spread_rows(ra, 3, 0)
    for b in range(4):
        forward(2 * b).wait_recv()
        forward(2 * b + 1).wait_recv()
        spread_rows(rb, b, 1)

    for copy in own[2:]:
        copy.wait()
    for copy in weights:
        copy.wait()
    for i in range(1, 4):
        kv_copy(kv, c, i, other).wait_send()

    @pl.when(zh == 0)
    def _():
        kv_copy(kv, c, 0, other).wait_send()

    @pl.when(zh == 1)
    def _():
        for i in range(1, 4):
            kv_copy(kv, x, 3 + i, other).wait_send()

    most = ra.at[pl.ds(0, 63)]
    pltpu.make_async_copy(most, most, s_send).wait()
    for r in range(8):
        forward(r).wait_send()
    for b in range(8):
        for copy in out_copies(b):
            copy.wait()


def send_call(pk, kv, gu, ex, queries, out_grad):
    hbm = pl.BlockSpec(memory_space=pl.ANY)
    vmem = pl.BlockSpec(memory_space=pltpu.VMEM)
    bf16 = jnp.bfloat16
    rows = jax.ShapeDtypeStruct((ROWS, WIDTH), bf16)
    return pl.pallas_call(
        send_kernel,
        out_shape=(
            rows,
            rows,
            jax.ShapeDtypeStruct((2, 2, PAD, WIDTH), bf16),
            jax.ShapeDtypeStruct((2, PAD, WIDTH), bf16),
            jax.ShapeDtypeStruct(queries.shape, bf16),
            jax.ShapeDtypeStruct((8, TOK, 512), bf16),
        ),
        in_specs=[hbm] * 4 + [vmem] * 3,
        out_specs=(hbm,) * 4 + (vmem,) * 2,
        scratch_shapes=[
            pltpu.VMEM((64, 16, FOLD), bf16),
            pltpu.VMEM((64, 16, FOLD), bf16),
            pltpu.VMEM((8, TOK, 512), bf16),
            pltpu.VMEM((ROWS, WIDTH), bf16),
            pltpu.VMEM((ROWS, WIDTH), bf16),
            pltpu.SemaphoreType.DMA,
            pltpu.SemaphoreType.DMA((8,)),
            pltpu.SemaphoreType.DMA((8,)),
            pltpu.SemaphoreType.DMA((8,)),
            pltpu.SemaphoreType.DMA((4,)),
            pltpu.SemaphoreType.DMA((7,)),
            pltpu.SemaphoreType.DMA((8,)),
            pltpu.SemaphoreType.DMA((4,)),
            pltpu.SemaphoreType.DMA((8, 2)),
        ]
        + ATTENTION_SCRATCH,
        compiler_params=pltpu.CompilerParams(collective_id=0, has_side_effects=True, vmem_limit_bytes=52 * MIB),
    )(pk, kv, gu, ex, queries, out_grad, jnp.asarray(UNFOLD, bf16))


HOMEWARD = (7, 5, 6, 2, 3, 4, 0, 1)


def return_kernel(
    rows, eg, xg, dkv, fold,
    back, eg_in, xg_in, dkv_out,
    own, mine, theirs, kv_in, cross, r_send, r_recv, b_send, b_recv, w_sem, k_send, k_recv, local
):
    c, e, zh, x, z, yc = place()
    wx, rx = pairs(x, e)
    barrier = greet(x, z, yc, c, e)
    for i in range(1, 4):
        pl.semaphore_signal(barrier, inc=1, device_id=(zh * 4 + (x + i) % 4, e), device_id_type=MESH)

    def fold_rows(ref, b, half):
        block = slice((b + 4 * half) * 80, (b + 4 * half + 1) * 80)
        total = jnp.zeros((256, BACK), jnp.float32)
        for k in range(3):
            part = rows[block, k * BACK : min((k + 1) * BACK, WIDTH)]
            placed = nn(fold[k], part)
            if placed.shape[1] < BACK:
                placed = jnp.concatenate([placed, jnp.zeros((256, BACK - placed.shape[1]), jnp.float32)], axis=1)
            total = total + placed
        ref[b * 16 : (b + 1) * 16] = total.astype(jnp.bfloat16).reshape(16, 16, BACK)

    for b in range(4):
        fold_rows(own, b, 1)
    pl.semaphore_wait(barrier, 66)

    def swap(r):
        block = pl.ds(r * 8, 8)
        return pltpu.make_async_remote_copy(
            own.at[block], theirs.at[block], r_send.at[r], r_recv.at[r], device_id=(zh * 4 + rx, e), device_id_type=MESH
        )

    for r in HOMEWARD:
        swap(r).start()
    wto = (zh * 4 + wx, e)
    weights = (
        pltpu.make_async_remote_copy(eg.at[:, 1], eg_in, w_sem.at[0], w_sem.at[1], device_id=wto, device_id_type=MESH),
        pltpu.make_async_remote_copy(xg.at[1], xg_in, w_sem.at[2], w_sem.at[3], device_id=wto, device_id_type=MESH),
    )

    def kv_copy(i, home, slot, half):
        return pltpu.make_async_remote_copy(
            dkv.at[home], kv_in.at[slot], k_send.at[i + 3 * half], k_recv.at[slot],
            device_id=(zh * 4 + home % 4, e), device_id_type=MESH,
        )

    cross_copy = pltpu.make_async_remote_copy(
        cross, kv_in.at[8], k_send.at[0], k_recv.at[8], device_id=(x, e), device_id_type=MESH
    )

    @pl.when(zh == 1)
    def _():
        for i in range(1, 4):
            kv_copy(i, (x + i) % 4, 4 + x, 1).start()

    for i in range(1, 4):
        to = (x + i) % 4

        @pl.when(to < x)
        def _(i=i, to=to):
            kv_copy(i, zh * 4 + to, x, 0).start()

    for copy in weights:
        copy.start()

    for b in range(4):
        fold_rows(mine, b, 0)

    @pl.when(zh == 1)
    def _():
        total = dkv[x].astype(jnp.float32)
        for i in range(1, 4):
            source = 4 + (x + i) % 4
            kv_copy(i, 0, source, 1).wait_recv()
            total = total + kv_in[source].astype(jnp.float32)
        cross[...] = total.astype(jnp.bfloat16)
        cross_copy.start()

    own_back = pltpu.make_async_copy(mine.at[SLOT[0] * 8 + yc], back.at[zh * EXPERTS + e], local.at[0])
    for r in HOMEWARD:
        dz = GROUPS[r]
        swap(r).wait_recv()

        def add(d, carry, r=r):
            total = mine[r * 8 + d].astype(jnp.float32) + theirs[r * 8 + d].astype(jnp.float32)
            mine[r * 8 + d] = total.astype(jnp.bfloat16)
            return carry

        lax.fori_loop(0, 8, add, 0)

        def send_one(d, carry, r=r, dz=dz):
            ys = (yc + d) % 8
            pltpu.make_async_remote_copy(
                mine.at[r * 8 + ys], back.at[zh * EXPERTS + e], b_send, b_recv,
                device_id=at((z + dz) % 8, ys, x), device_id_type=MESH,
            ).start()
            return carry

        lax.fori_loop(1 if dz == 0 else 0, 8, send_one, 0)
        if dz == 0:
            own_back.start()

    total = [dkv[c].astype(jnp.float32)]
    for i in range(1, 4):
        source = (x + i) % 4

        @pl.when(source > x)
        def _(i=i, source=source):
            kv_copy(i, 0, source, 0).wait_recv()

        @pl.when(source < x)
        def _(i=i, source=source):
            kv_copy(i, 0, source, 0).wait_send()
            kv_in[source] = jnp.zeros((TOK, 512), jnp.bfloat16)

        total.append(kv_in[source].astype(jnp.float32))

    @pl.when(zh == 0)
    def _():
        cross_copy.wait_recv()

    @pl.when(zh == 1)
    def _():
        cross_copy.wait_send()
        for i in range(1, 4):
            kv_copy(i, 0, 0, 1).wait_send()
        kv_in[8] = jnp.zeros((TOK, 512), jnp.bfloat16)

    total.append(kv_in[8].astype(jnp.float32))
    dkv_out[...] = sum(total).astype(jnp.bfloat16)

    for copy in weights:
        copy.wait()
    for r in range(8):
        swap(r).wait_send()
    own_back.wait()
    most = back.at[pl.ds(0, 63)]
    for sem in (b_send, b_recv):
        pltpu.make_async_copy(most, most, sem).wait()


def return_call(rows, eg, xg, dkv):
    hbm = pl.BlockSpec(memory_space=pl.ANY)
    vmem = pl.BlockSpec(memory_space=pltpu.VMEM)
    bf16 = jnp.bfloat16
    packets = pltpu.VMEM((64, 16, BACK), bf16)
    return pl.pallas_call(
        return_kernel,
        out_shape=(
            jax.ShapeDtypeStruct((2 * EXPERTS, 16, BACK), bf16),
            jax.ShapeDtypeStruct((2, PAD, WIDTH), bf16),
            jax.ShapeDtypeStruct((PAD, WIDTH), bf16),
            jax.ShapeDtypeStruct((TOK, 512), bf16),
        ),
        in_specs=[vmem, hbm, hbm, vmem, vmem],
        out_specs=(hbm,) * 3 + (vmem,),
        scratch_shapes=[
            packets,
            packets,
            packets,
            pltpu.VMEM((9, TOK, 512), bf16),
            pltpu.VMEM((TOK, 512), bf16),
            pltpu.SemaphoreType.DMA((8,)),
            pltpu.SemaphoreType.DMA((8,)),
            pltpu.SemaphoreType.DMA,
            pltpu.SemaphoreType.DMA,
            pltpu.SemaphoreType.DMA((4,)),
            pltpu.SemaphoreType.DMA((7,)),
            pltpu.SemaphoreType.DMA((9,)),
            pltpu.SemaphoreType.DMA((1,)),
        ],
        compiler_params=pltpu.CompilerParams(collective_id=1, has_side_effects=True, vmem_limit_bytes=32 * MIB),
    )(rows, eg, xg, dkv, jnp.asarray(FOLDING, bf16))


def pick_rows(routes, shares):
    matched = routes[:, :, None] == jnp.arange(EXPERTS)[None, None, :]
    hits = jnp.any(matched, axis=1)
    share = jnp.sum(jnp.where(matched, shares[:, :, None], 0.0), axis=1)
    before = jnp.asarray(np.tril(np.ones((TOK, TOK), np.float32), -1), jnp.bfloat16)
    earlier = jnp.dot(before, hits.astype(jnp.bfloat16), preferred_element_type=jnp.float32).astype(jnp.int32)
    row = jnp.arange(16)[None, None, :]
    chosen = hits[:, :, None] & (earlier[:, :, None] == row % CAP) & (row < 3 * CAP)
    slot_share = jnp.sum(jnp.where(chosen, share[:, :, None], 0.0), axis=0)
    return chosen, slot_share


def unfold_matrix():
    out = np.zeros((3 * 80, 256), np.float32)
    for p in range(16):
        for k in range(3):
            for s in range(CAP):
                out[k * 80 + p * CAP + s, p * 16 + k * CAP + s] = 1
    return out


UNFOLD = unfold_matrix()
FOLDING = UNFOLD.reshape(3, 80, 256).transpose(0, 2, 1)


def per_device(queries, key_rows, value_rows, out_grad, tokens, token_grad, route_ids, route_probs, entry_weight, exit_weight):
    f32, bf16 = jnp.float32, jnp.bfloat16
    x, g = tokens[0], token_grad[0]
    chosen, slot_share = pick_rows(route_ids[0], route_probs[0])
    part = jnp.arange(16) // CAP
    chosen3 = [(chosen & (part == k)[None, None, :]).reshape(TOK, 512).astype(bf16) for k in range(3)]

    chunks = (x[:, :FOLD], jnp.concatenate([x[:, FOLD:], g[:, FOLD:]], axis=1), g[:, :FOLD])
    packed = sum(tn(s, m) for s, m in zip(chosen3, chunks)).reshape(EXPERTS, 16, FOLD)
    is_grad = (part[:, None] == 2) | ((part[:, None] == 1) & (jnp.arange(FOLD)[None, :] >= WIDTH - FOLD))
    packed = jnp.where(is_grad[None], packed * slot_share[:, :, None], packed).astype(bf16)

    hidden = exit_weight.shape[1]
    gu = jnp.pad(entry_weight[0].transpose(1, 2, 0), ((0, 0), (0, PAD - hidden), (0, 0)))
    ex = jnp.pad(exit_weight[0], ((0, PAD - hidden), (0, 0)))
    kv = jnp.concatenate([key_rows[0], value_rows[0]], axis=1)

    xr, gr, gu2, ex2, query_grad, dkv = send_call(packed, kv, gu, ex, queries[0], out_grad[0])

    up_down = gu2.reshape(4 * PAD, WIDTH)
    leave = ex2.reshape(2 * PAD, WIDTH)
    projected = nt(xr, up_down)
    gate, upward = projected[:, : 2 * PAD], projected[:, 2 * PAD :]
    sigma = jax.nn.sigmoid(gate)
    swish = gate * sigma
    activation = (swish * upward).astype(bf16)
    act_grad = nt(gr, leave)
    slope = sigma * (1.0 + gate * (1.0 - sigma))
    score_rows = jnp.concatenate([act_grad * upward * slope, act_grad * swish], axis=1).astype(bf16)
    row_part = nn(score_rows, up_down).astype(bf16)
    eg = tn(score_rows, xr).astype(bf16).reshape(2, 2, PAD, WIDTH)
    xg = tn(activation, gr).astype(bf16).reshape(2, PAD, WIDTH)

    back, eg_in, xg_in, dkv_sum = return_call(row_part, eg, xg, dkv)

    back = back.reshape(2 * 512, BACK)
    input_grad = jnp.concatenate(
        [nn(jnp.concatenate([s, s], axis=1), back) for s in chosen3], axis=1
    )[:, :WIDTH].astype(bf16)

    entry_grad = (eg[:, 0].astype(f32) + eg_in.astype(f32)).astype(bf16)[:, :hidden]
    exit_grad = (xg[0].astype(f32) + xg_in.astype(f32)).astype(bf16)[:hidden]
    return (
        query_grad[None],
        dkv_sum[None, :, :256],
        dkv_sum[None, :, 256:],
        input_grad[None],
        entry_grad.transpose(2, 0, 1)[None],
        exit_grad[None],
    )


def solution(mesh):
    row = P("exp", "ctx", None)
    entry = P("exp", None, None, "ctx")
    return jax.shard_map(
        per_device,
        mesh=mesh,
        in_specs=(row,) * 8 + (entry, row),
        out_specs=(row,) * 4 + (entry, row),
        check_vma=False,
    )
```

time: 421 us -> 307 us (0.73)
  Pallas kernels: 326 us -> 239 us
  local copies, waits for them, and re-layouts: 43.1 us -> 31.2 us
  matrix products: 34.5 us -> 26.8 us
  other arithmetic: 12.7 us -> 7.77 us
    pallas_call x1, Pallas kernels: 200 us -> 115 us  [send_call(): pl.pallas_call(send_kernel, out_shape=(rows, rows, jax.ShapeDtypeStruct((...]
    reshape x1 -> x0, local copies, waits for them, and re-layouts: 11 us -> none  [per_device(): jnp.pad(row_part, ((0, 0), (0, 3 * BACK - WIDTH))).reshape(8, 80, 3, BACK)]
    dot_general x2 -> x0, matrix products: 11 us -> none  [the longest x1 5.52 us: per_device(): jnp.einsum('uv,bvc->buc', unfold, arrived, preferred_element_type=f32)]
    slice x6 -> x1, local copies, waits for them, and re-layouts: 7.08 us -> 0.08 us  [per_device(): exit_grad = (xg[0].astype(f32) + xg_in.astype(f32)).astype(bf16)[:hidden]]
    convert_element_type x0 -> x1, local copies, waits for them, and re-layouts: none -> 6.19 us  [per_device(): row_part = nn(score_rows, up_down).astype(bf16)]
    pallas_call x1 -> x0, Pallas kernels: 5.36 us -> none  [attention_call(): pl.pallas_call(attention_kernel, out_shape=(jax.ShapeDtypeStruct(queries....]
    unnamed x39 -> x57, local copies, waits for them, and re-layouts: 10.5 us -> 12.5 us
where the time goes in v2:
time: 307 us; the launch traced here: 306 us
  Pallas kernels  239 us (78%)
  local copies, waits for them, and re-layouts  31.2 us (10%)
  matrix products  26.8 us (9%)
  other arithmetic  7.77 us (3%)
    pallas_call x1, Pallas kernels, return_call(): pl.pallas_call(return_kernel, out_shape=(jax.ShapeDtypeStruct((2 * EXPERT...  124 us
    pallas_call x1, Pallas kernels, send_call(): pl.pallas_call(send_kernel, out_shape=(rows, rows, jax.ShapeDtypeStruct((...  115 us
    unnamed x57, local copies, waits for them, and re-layouts  12.5 us
    dot_general x5, matrix products, tn(): lax.dot_general(a, b, (((0,), (0,)), ((), ())), preferred_element_type=jn...  9.61 us
    dot_general x2, matrix products, nt(): lax.dot_general(a, b, (((1,), (1,)), ((), ())), preferred_element_type=jn...  9.44 us
    dot_general x4, matrix products, nn(): lax.dot_general(a, b, (((1,), (0,)), ((), ())), preferred_element_type=jn...  6.89 us
    convert_element_type x1, local copies, waits for them, and re-layouts, per_device(): eg = tn(score_rows, xr).astype(bf16).reshape(2, 2, PAD, WIDTH)  6.6 us
    convert_element_type x1, local copies, waits for them, and re-layouts, per_device(): row_part = nn(score_rows, up_down).astype(bf16)  6.19 us

profile of v2, /device:TPU:1, one launch (start us, length us, event | category | flops | bytes accessed | tf_op | source)
XLA Modules:
  0.0 306.0 jit_solution(16626843797015313305)
XLA Ops:
  0.6 0.0 copy-start.12
  0.7 0.1 and.141
  0.8 0.8 fusion.29
  1.7 0.1 and.149
  1.8 0.1 and.145
  1.9 0.1 and.137
  2.0 0.9 fusion.3
  2.9 0.1 eq.89
  3.0 0.7 select_reduce_fusion.1
  3.7 0.2 select_reduce_fusion
  3.9 0.1 and_or_fusion
  4.0 0.9 pad_maximum_fusion.5.kv
  4.9 0.6 fusion.25
  5.5 0.0 copy-start.17
  5.6 0.0 copy-start.19
  5.6 1.0 slice.55
  6.6 1.0 slice.56
  7.6 1.1 pad.9.ex
  8.7 0.2 copy.59
  8.9 1.6 pad.8.gu
  10.4 0.7 fusion.19
  11.1 0.4 copy-done.13
  11.6 0.7 fusion.17
  12.3 0.4 copy-done.14
  12.7 0.7 add_add_fusion
  13.4 0.0 copy-start.5
  13.4 0.0 copy-start.6
  13.4 0.0 copy-start.10
  13.4 1.7 fusion.1.pk
  15.1 115.4 %shard_map.172 = (bf16[640,2880]{1,0:T(8,128)(2,1)}, bf16[640,2880]{1,0:T(8,128)(2,1)}, bf16[2,2,192,2880]{3,2,1,0:T(8,128)(2,1)}, bf16[2,192,2880]{2,1,0:T(8,12...) custom-call(bf16[32,16,1920]{2,1,0:T(8,128)(2,1)} %fusion.1.pk, ...), custom_call_target="tpu_custom_call" | custom-call | tf_op jit(solution)/shard_map/pallas_call | solution.py:325
  130.5 0.0 copy-start.7
  130.6 0.0 slice-start
  130.6 7.3 %fusion.37 = f32[640,768]{0,1:T(8,128)S(1)} fusion(bf16[640,2880]{1,0:T(8,128)(2,1)} %get-tuple-element.19, bf16[768,2880]{1,0:T(8,128)(2,1)} %bitcast.94), kind=kOutput, calls=%fused_computation.74 | convolution fusion | flops 2831155200 | bytes 10076160 | tf_op jit(solution)/shard_map/dot_general | solution.py:26
  137.9 0.0 slice-start.1
  137.9 2.1 multiply_convert_fusion.2
  140.1 2.0 convolution_convert_fusion.2
  142.1 0.0 slice-done
  142.1 0.0 slice-done.1
  142.1 0.0 copy-start.21
  142.1 5.4 %convolution_convert_fusion.1 = bf16[640,2880]{0,1:T(8,128)(2,1)} fusion(bf16[768,2880]{1,0:T(8,128)(2,1)S(1)} %bitcast.97, bf16[640,384]{0,1:T(8,128)(2,1)S(1)} %get-tuple-element.51, bf16[640,384]{0,1:T(8,128)(2,1)S(1)} %get-tuple-element.50), kind=kOutput, calls=%fused_computation.2 | convolution fusion | flops 2834964480 | bytes 9093120 | tf_op jit(solution)/shard_map/dot_general | solution.py:34
  147.5 0.0 copy-done.21
  147.5 5.6 %convolution_convert_fusion = bf16[768,2880]{0,1:T(8,128)(2,1)} fusion(bf16[640,2880]{1,0:T(8,128)(2,1)S(1)} %copy-done.21, bf16[640,384]{0,1:T(8,128)(2,1)S(1)} %get-tuple-element.51, bf16[640,384]{0,1:T(8,128)(2,1)S(1)} %get-tuple-element.50), kind=kOutput, calls=%fused_computation.1 | convolution fusion | flops 2835333120 | bytes 9093120 | tf_op jit(solution)/shard_map/dot_general | solution.py:30
  153.1 6.2 %copy.53.rows = bf16[640,2880]{1,0:T(8,128)(2,1)} copy(bf16[640,2880]{0,1:T(8,128)(2,1)} %convolution_convert_fusion.1) | data formatting | bytes 7372800 | tf_op jit(solution)/shard_map/convert_element_type | solution.py:590
  159.3 6.6 %copy.51 = bf16[768,2880]{1,0:T(8,128)(2,1)} copy(bf16[768,2880]{0,1:T(8,128)(2,1)} %convolution_convert_fusion) | data formatting | bytes 8847360 | tf_op jit(solution)/shard_map/convert_element_type | solution.py:591
  165.9 0.0 copy-done.2
  165.9 2.3 copy-done
  168.2 2.1 copy-done.1
  170.2 123.8 %shard_map.173 = (bf16[64,16,1024]{2,1,0:T(8,128)(2,1)S(1)}, bf16[2,192,2880]{2,1,0:T(8,128)(2,1)S(1)}, bf16[192,2880]{1,0:T(8,128)(2,1)S(1)}, bf16[128,512]{1,0:T(8,128)(2,1)S(1)}) custom-call(bf16[640,2880]{1,0:T(8,128)(2,1)S(1)} %copy-done.1, bf16[2,2,192,2880]{3,2,1,0:T(8,128)(2,1)S(1)} %bitcast.73, bf16[2,192,2880]{2,1,0:T(8,128)(2,1)S(1)} %bitcast.78, ...), custom_call_target="tpu_custom_call" | custom-call | tf_op jit(solution)/shard_map/pallas_call | solution.py:507
  294.0 0.0 copy-start.3
  294.0 0.2 slice_bitcast_fusion
  294.2 0.8 copy-done.3
  295.0 0.5 fusion.2
  295.5 0.0 copy-start.20
  295.5 3.0 copy.55
  298.5 0.7 slice_bitcast_fusion.1
  299.2 0.5 convolution_convert_fusion.3
  299.7 0.5 convolution_convert_fusion.4
  300.2 0.5 convolution_convert_fusion.5
  300.7 0.9 fusion.6
  301.6 2.3 copy.54
  303.9 0.1 slice.63
  304.0 0.0 copy-done.4
  304.0 1.2 fusion.4
  305.2 0.8 copy.70
  (41 shorter events, 0.1 us)
Async XLA Ops:
  0.6 6.9 %copy-start.12 = (bf16[1,180,2880]{2,1,0:T(8,128)(2,1)S(1)}, bf16[1,180,2880]{2,1,0:T(8,128)(2,1)}, u32[]{:S(2)}) copy-start(bf16[1,180,2880]{2,1,0:T(8,128)(2,1)} %param.22) | copy-start | bytes 3110404
  0.6 8.0 %copy-start.11 = (bf16[1,2880,2,180]{1,2,3,0:T(2,128)(2,1)S(1)}, bf16[1,2880,2,180]{1,2,3,0:T(2,128)(2,1)}, u32[]{:S(2)}) copy-start(bf16[1,2880,2,180]{1,2,3,0:T(2,128)(2,1)} %param.21) | copy-start | bytes 6220804
  5.5 4.9 %copy-start.17 = (pred[128,512]{0,1:T(32,128)(4,1)}, pred[128,512]{0,1:T(32,128)(4,1)S(1)}, u32[]{:S(2)}) copy-start(pred[128,512]{0,1:T(32,128)(4,1)S(1)} %get-tuple-element.55) | copy-start | bytes 196612
  5.5 5.6 %copy-start.15 = (pred[128,512]{0,1:T(32,128)(4,1)}, pred[128,512]{0,1:T(32,128)(4,1)S(1)}, u32[]{:S(2)}) copy-start(pred[128,512]{0,1:T(32,128)(4,1)S(1)} %get-tuple-element.56) | copy-start | bytes 196612
  5.6 6.7 %copy-start.19 = (pred[128,512]{0,1:T(32,128)(4,1)}, pred[128,512]{0,1:T(32,128)(4,1)S(1)}, u32[]{:S(2)}) copy-start(pred[128,512]{0,1:T(32,128)(4,1)S(1)} %get-tuple-element.54) | copy-start | bytes 196612
  10.4 1.1 copy-start.13
  11.6 1.1 copy-start.14
  13.4 1.7 copy-start.5
  13.4 1.7 copy-start.6
  13.4 1.7 copy-start.10
  130.5 7.4 %copy-start.7 = (bf16[128,2048]{1,0:T(8,128)(2,1)}, bf16[128,2048]{1,0:T(8,128)(2,1)S(1)}, u32[]{:S(2)}) copy-start(bf16[128,2048]{1,0:T(8,128)(2,1)S(1)} %get-tuple-element.16) | copy-start | bytes 1572868
  130.5 7.4 %copy-start.22 = (bf16[640,2880]{1,0:T(8,128)(2,1)S(1)}, bf16[640,2880]{1,0:T(8,128)(2,1)}, u32[]{:S(2)}) copy-start(bf16[640,2880]{1,0:T(8,128)(2,1)} %get-tuple-element.17) | copy-start | bytes 11059204
  130.6 7.4 %copy-start.23 = (bf16[2,192,2880]{2,1,0:T(8,128)(2,1)S(1)}, bf16[2,192,2880]{2,1,0:T(8,128)(2,1)}, u32[]{:S(2)}) copy-start(bf16[2,192,2880]{2,1,0:T(8,128)(2,1)} %get-tuple-element.18) | copy-start | bytes 6635524
  130.6 11.5 %slice-start = ((s8[4521984]{0:T(1024)(128)(4,1)}), s8[4194304]{0:T(1024)(128)(4,1)S(1)}, s32[]{:S(2)}) async-start(s8[4521984]{0:T(1024)(128)(4,1)} %bitcast.95), calls=%async_computation | async-start | bytes 8388608
  137.9 4.1 %slice-start.1 = ((s8[4521984]{0:T(1024)(128)(4,1)}), s8[327680]{0:T(1024)(128)(4,1)S(1)}, s32[]{:S(2)}) async-start(s8[4521984]{0:T(1024)(128)(4,1)} %bitcast.95), calls=%async_computation.1 | async-start | bytes 655360
  142.1 5.4 %copy-start.21 = (bf16[640,2880]{1,0:T(8,128)(2,1)S(1)}, bf16[640,2880]{1,0:T(8,128)(2,1)}, u32[]{:S(2)}) copy-start(bf16[640,2880]{1,0:T(8,128)(2,1)} %get-tuple-element.19) | copy-start | bytes 11059204
  159.3 6.6 %copy-start.2 = (bf16[8,128,512]{2,1,0:T(8,128)(2,1)S(1)}, bf16[8,128,512]{2,1,0:T(8,128)(2,1)}, u32[]{:S(2)}) copy-start(bf16[8,128,512]{2,1,0:T(8,128)(2,1)} %get-tuple-element.21.dkv) | copy-start | bytes 3145732
  159.3 6.6 %copy-start.9 = (bf16[3,256,80]{2,1,0:T(8,128)(2,1)S(1)}, bf16[3,256,80]{2,1,0:T(8,128)(2,1)}, u32[]{:S(2)}) copy-start(bf16[3,256,80]{2,1,0:T(8,128)(2,1)} %constant.47.clone.fold) | copy-start | bytes 368644
  165.9 2.3 copy-start
  168.2 2.1 copy-start.1
  294.0 1.0 copy-start.3
  295.5 3.6 %copy-start.20 = (pred[128,512]{0,1:T(32,128)(4,1)S(1)}, pred[128,512]{0,1:T(32,128)(4,1)}, u32[]{:S(2)}) copy-start(pred[128,512]{0,1:T(32,128)(4,1)} %copy-done.19) | copy-start | bytes 196612
  298.5 1.2 copy-start.18
  299.2 1.0 copy-start.16
  300.7 3.3 %copy-start.4 = (bf16[192,2880]{1,0:T(8,128)(2,1)S(1)}, bf16[192,2880]{1,0:T(8,128)(2,1)}, u32[]{:S(2)}) copy-start(bf16[192,2880]{1,0:T(8,128)(2,1)} %copy-done.3) | copy-start | bytes 3317764
  303.9 1.3 copy-start.8

commit v3 on v2

v3 whole, which is shorter than its diff:
```python
import functools

import jax
import jax.numpy as jnp
import numpy as np
from jax import lax
from jax.experimental import pallas as pl
from jax.experimental.pallas import tpu as pltpu
from jax.sharding import PartitionSpec as P

HEAD = 64
CAP = 5
TOK = 128
WIDTH = 2880
FOLD = 1920
BACK = 1024
PAD = 192
EXPERTS = 32
MESH = pl.DeviceIdType.MESH
MIB = 1024 * 1024
SCALE = 0.125
EXP_SCALE = 0.125 * 1.4426950408889634


def nt(a, b):
    return lax.dot_general(a, b, (((1,), (1,)), ((), ())), preferred_element_type=jnp.float32)


def tn(a, b):
    return lax.dot_general(a, b, (((0,), (0,)), ((), ())), preferred_element_type=jnp.float32)


def nn(a, b):
    return lax.dot_general(a, b, (((1,), (0,)), ((), ())), preferred_element_type=jnp.float32)


def attention_body(c, q_ref, g_ref, kv_ref, dq_ref, dkv_ref, s_ref, p_ref, kz_ref, vz_ref, q4, g4, dk2, dv2, dq4, heads=range(4)):
    length = q_ref.shape[0]
    lane = lax.broadcasted_iota(jnp.int32, (length, 128), 1)
    low = lane < HEAD
    krow = lax.broadcasted_iota(jnp.int32, (2 * length, 512), 0) % length
    qcol = lax.broadcasted_iota(jnp.int32, (2 * length, 512), 1) % length
    diag = krow <= qcol

    def spread(tile, h):
        tile = tile.astype(jnp.float32)
        swapped = pltpu.roll(tile, HEAD, 1)
        first, second = (tile, swapped) if h % 2 == 0 else (swapped, tile)
        return jnp.concatenate([jnp.where(low, first, 0.0), jnp.where(low, 0.0, second)], axis=0).astype(jnp.bfloat16)

    def halves(stat):
        return jnp.concatenate([jnp.broadcast_to(stat[0:1], (length, 512)), jnp.broadcast_to(stat[1:2], (length, 512))], axis=0)

    def by_half(x, op):
        return jnp.concatenate([op(x[:length], axis=0, keepdims=True), op(x[length:], axis=0, keepdims=True)], axis=0)

    for h in heads:
        t = h // 2
        for i in range(4):
            cols = slice(h * 512 + i * 128, h * 512 + (i + 1) * 128)
            q4[i * length : (i + 1) * length, :] = q_ref[:, cols]
            g4[i * length : (i + 1) * length, :] = g_ref[:, cols]

        def score_step(j, top, masked):
            keys = spread(kv_ref[j, :, t * 128 : (t + 1) * 128], h)
            kz_ref[j] = keys
            vz_ref[j] = spread(kv_ref[j, :, 256 + t * 128 : 256 + (t + 1) * 128], h)
            s = nt(keys, q4[...])
            if masked:
                s = jnp.where(diag, s, -1e30)
            s_ref[j] = s
            return jnp.maximum(top, by_half(s, jnp.max))

        top = lax.fori_loop(0, c, lambda j, m: score_step(j, m, False), jnp.full((2, 512), -1e30, jnp.float32))
        top = score_step(c, top, True)
        top_wide = halves(top)

        def sum_step(j, state):
            total, dot = state
            p = jnp.exp2((s_ref[j] - top_wide) * EXP_SCALE)
            dp = nt(vz_ref[j], g4[...])
            s_ref[j] = p
            p_ref[j] = dp
            return total + by_half(p, jnp.sum), dot + by_half(p * dp, jnp.sum)

        zero = jnp.zeros((2, 512), jnp.float32)
        total, dot = lax.fori_loop(0, c + 1, sum_step, (zero, zero))
        inverse = 1.0 / total
        inverse_wide = halves(inverse)
        delta_wide = halves(dot * inverse)
        dq4[...] = jnp.zeros_like(dq4)

        def grad_step(j, carry):
            p = s_ref[j] * inverse_wide
            ds = (p * (p_ref[j] - delta_wide)).astype(jnp.bfloat16)
            dv2[j] = nn(p.astype(jnp.bfloat16), g4[...])
            dk2[j] = nn(ds, q4[...])
            dq4[...] += tn(ds, kz_ref[j])
            return carry

        lax.fori_loop(0, c + 1, grad_step, 0)
        for i in range(4):
            cols = slice(h * 512 + i * 128, h * 512 + (i + 1) * 128)
            dq_ref[:, cols] = (dq4[i * length : (i + 1) * length, :] * SCALE).astype(jnp.bfloat16)

        def out_step(j, carry):
            for ref, base, scale in ((dk2, 0, SCALE), (dv2, 256, 1.0)):
                even, odd = ref[j, :length, :], ref[j, length:, :]
                if h % 2 == 0:
                    whole = even + pltpu.roll(odd, HEAD, 1)
                else:
                    whole = pltpu.roll(even, HEAD, 1) + odd
                whole = (whole * scale).astype(jnp.bfloat16)
                cols = slice(base + t * 128, base + (t + 1) * 128)
                if h % 2 == 0:
                    dkv_ref[j, :, cols] = whole
                else:
                    dkv_ref[j, :, cols] = jnp.where(low, dkv_ref[j, :, cols], whole)
            return carry

        lax.fori_loop(0, c + 1, out_step, 0)


ATTENTION_SCRATCH = [
    pltpu.VMEM((8, 256, 512), jnp.float32),
    pltpu.VMEM((8, 256, 512), jnp.float32),
    pltpu.VMEM((8, 256, 128), jnp.bfloat16),
    pltpu.VMEM((8, 256, 128), jnp.bfloat16),
    pltpu.VMEM((512, 128), jnp.bfloat16),
    pltpu.VMEM((512, 128), jnp.bfloat16),
    pltpu.VMEM((8, 256, 128), jnp.float32),
    pltpu.VMEM((8, 256, 128), jnp.float32),
    pltpu.VMEM((512, 128), jnp.float32),
]


def place():
    c, e = lax.axis_index("ctx"), lax.axis_index("exp")
    zh, x = c // 4, c % 4
    zl = (e // 2) % 4
    yc = (e // 8) * 2 + e % 2
    return c, e, zh, x, zh * 4 + zl, yc


def at(z, yc, x):
    return ((z // 4) * 4 + x, (yc // 2) * 8 + (z % 4) * 2 + yc % 2)


def greet(x, z, yc, c, e):
    barrier = pltpu.get_barrier_semaphore()

    def peer(i, carry):
        pl.semaphore_signal(barrier, inc=1, device_id=at((z + i // 8) % 8, (yc + i % 8) % 8, x), device_id_type=MESH)
        return carry

    lax.fori_loop(1, 64, peer, 0)
    return barrier


def pairs(x, e):
    core = e % 2
    near = x + 1 - 2 * (x % 2)
    far = 3 - x
    return near + core * (far - near), far + core * (near - far)


GROUPS = (1, 7, 2, 6, 0, 3, 5, 4)
SLOT = {dz: r for r, dz in enumerate(GROUPS)}
ROWS = 640


HOMEWARD = ((3, 2, 1, 0), (7, 6, 5, 4))
PARTS = ((0, 1024), (1024, 1024), (2048, 896))
WIDE = 2944


def layer_kernel(
    pk, kv, gu, ex, q, g, unfold, fold,
    dq, dkv_out, back, w_out,
    ra, rb, kv_all, xv, gv, gu2, ex2, dkv, kv_in, cross, score, active, score_t, mine, own, theirs, w_own, w_in,
    s_send, s_recv, f_send, f_recv, w_sem, k_send, k_recv, d_send, d_recv,
    r_send, r_recv, b_send, b_recv, g_send, g_recv, local, *scratch
):
    f32, bf16 = jnp.float32, jnp.bfloat16
    c, e, zh, x, z, yc = place()
    wx, rx = pairs(x, e)
    rto, wto = (zh * 4 + rx, e), (zh * 4 + wx, e)
    other = (4 + x, e)
    barrier = greet(x, z, yc, c, e)
    for i in range(1, 4):
        pl.semaphore_signal(barrier, inc=1, device_id=(zh * 4 + (x + i) % 4, e), device_id_type=MESH)
    own_in = (
        pltpu.make_async_copy(pk.at[e], ra.at[SLOT[0] * 8 + yc], local.at[0]),
        pltpu.make_async_copy(kv, kv_all.at[c], local.at[1]),
        pltpu.make_async_copy(gu, gu2.at[:, 0], local.at[2]),
        pltpu.make_async_copy(ex, ex2.at[0], local.at[3]),
    )
    for copy in own_in:
        copy.start()
    pl.semaphore_wait(barrier, 66)

    def remote(src, dst, send, recv, to):
        return pltpu.make_async_remote_copy(src, dst, send, recv, device_id=to, device_id_type=MESH)

    def kv_copy(src, block, i, to):
        return remote(src, kv_all.at[block], k_send.at[i], k_recv.at[block], to)

    @pl.when(zh == 0)
    def _():
        kv_copy(kv, c, 0, other).start()

    for i in range(1, 4):
        kv_copy(kv, c, i, (zh * 4 + (x + i) % 4, e)).start()

    weights = (
        remote(gu, gu2.at[:, 1], w_sem.at[0], w_sem.at[1], wto),
        remote(ex, ex2.at[1], w_sem.at[2], w_sem.at[3], wto),
    )
    for copy in weights:
        copy.start()

    for dz in GROUPS:
        slot = SLOT[(8 - dz) % 8]

        def send_one(d, carry, dz=dz, slot=slot):
            to = at((z + dz) % 8, (yc + d) % 8, x)
            remote(pk.at[to[1]], ra.at[slot * 8 + yc], s_send, s_recv.at[slot], to).start()
            return carry

        lax.fori_loop(1 if dz == 0 else 0, 8, send_one, 0)

    @pl.when(zh == 1)
    def _():
        kv_copy(kv, x, 0, other).wait_recv()
        for i in range(1, 4):
            kv_copy(kv_all.at[x], x, 3 + i, (4 + (x + i) % 4, e)).start()

    def forward(r):
        block = pl.ds(r * 8, 8)
        return remote(ra.at[block], rb.at[block], f_send.at[r], f_recv.at[r], rto)

    def arrive(r):
        count = 8
        if GROUPS[r] == 0:
            own_in[0].wait()
            count = 7
        pltpu.make_async_copy(ra.at[pl.ds(0, count)], ra.at[pl.ds(0, count)], s_recv.at[r]).wait()
        forward(r).start()

    def spread_rows(ref, b, half):
        packets = ref[b * 16 : (b + 1) * 16].reshape(256, FOLD)
        slots = nn(unfold[...], packets)
        rest = WIDTH - FOLD
        b = b + 4 * half
        rows = slice(b * 80, (b + 1) * 80)
        xv[rows, :FOLD] = slots[:80].astype(bf16)
        gv[rows, :FOLD] = slots[160:].astype(bf16)
        xv[rows, FOLD:] = slots[80:160, :rest].astype(bf16)
        gv[rows, FOLD:] = slots[80:160, rest:].astype(bf16)

    def expert_rows(ref, b, half):
        rows = slice((b + 4 * half) * 80, (b + 4 * half + 2) * 80)
        gate = nt(xv[rows], gu2[0].reshape(2 * PAD, WIDTH))
        upward = nt(xv[rows], gu2[1].reshape(2 * PAD, WIDTH))
        act_grad = nt(gv[rows], ex2[...].reshape(2 * PAD, WIDTH))
        sigma = jax.nn.sigmoid(gate)
        swish = gate * sigma
        slope = sigma * (1.0 + gate * (1.0 - sigma))
        active[rows] = (swish * upward).astype(bf16)
        score[rows, : 2 * PAD] = (act_grad * upward * slope).astype(bf16)
        score[rows, 2 * PAD :] = (act_grad * swish).astype(bf16)
        totals = [jnp.zeros((256, BACK), f32) for _ in range(2)]
        for k in range(3):
            cols = slice(k * BACK, min((k + 1) * BACK, WIDTH))
            both = gu2[:, :, :, cols].reshape(4 * PAD, cols.stop - cols.start)
            part = nn(score[rows], both).astype(bf16)
            for i in range(2):
                placed = nn(fold[k], part[80 * i : 80 * (i + 1)])
                if placed.shape[1] < BACK:
                    placed = jnp.concatenate([placed, jnp.zeros((256, BACK - placed.shape[1]), f32)], axis=1)
                totals[i] = totals[i] + placed
        for i in range(2):
            ref[(b + i) * 16 : (b + i + 1) * 16] = totals[i].astype(bf16).reshape(16, 16, BACK)

    def swap(r):
        block = pl.ds(r * 8, 8)
        return remote(own.at[block], theirs.at[block], r_send.at[r], r_recv.at[r], rto)

    home = zh * EXPERTS + e
    own_back = pltpu.make_async_copy(mine.at[SLOT[0] * 8 + yc], back.at[home], local.at[0])

    def go_home(r):
        dz = GROUPS[r]
        swap(r).wait_recv()

        def add(d, carry):
            total = mine[r * 8 + d].astype(f32) + theirs[r * 8 + d].astype(f32)
            mine[r * 8 + d] = total.astype(bf16)
            return carry

        lax.fori_loop(0, 8, add, 0)

        def send_one(d, carry):
            ys = (yc + d) % 8
            remote(mine.at[r * 8 + ys], back.at[home], b_send, b_recv, at((z + dz) % 8, ys, x)).start()
            return carry

        lax.fori_loop(1 if dz == 0 else 0, 8, send_one, 0)
        if dz == 0:
            own_back.start()

    def dkv_copy(i, block, slot, half):
        return remote(dkv.at[block], kv_in.at[slot], d_send.at[i + 3 * half], d_recv.at[slot], (zh * 4 + block % 4, e))

    cross_copy = remote(cross, kv_in.at[8], d_send.at[0], d_recv.at[8], (x, e))

    def send_dkv():
        @pl.when(zh == 1)
        def _():
            for i in range(1, 4):
                dkv_copy(i, (x + i) % 4, 4 + x, 1).start()

        for i in range(1, 4):
            to = (x + i) % 4

            @pl.when(to < x)
            def _(i=i, to=to):
                dkv_copy(i, zh * 4 + to, x, 0).start()

    def cross_dkv():
        @pl.when(zh == 1)
        def _():
            total = dkv[x].astype(f32)
            for i in range(1, 4):
                source = 4 + (x + i) % 4
                dkv_copy(i, 0, source, 1).wait_recv()
                total = total + kv_in[source].astype(f32)
            cross[...] = total.astype(bf16)
            cross_copy.start()

    own_in[1].wait()
    for i in range(1, 4):
        kv_copy(kv, zh * 4 + (x + i) % 4, i, other).wait_recv()

    @pl.when(zh == 1)
    def _():
        for i in range(1, 4):
            kv_copy(kv, (x + i) % 4, 3 + i, other).wait_recv()

    def attend(heads):
        attention_body(c, q, g, kv_all, dq, dkv, *scratch, heads=heads)

    arrive(0)
    arrive(1)
    attend((0, 1))
    arrive(2)
    arrive(3)
    attend((2, 3))
    send_dkv()

    for copy in own_in[2:]:
        copy.wait()
    for copy in weights:
        copy.wait_recv()
    spread_rows(ra, 0, 0)
    spread_rows(ra, 1, 0)
    expert_rows(mine, 0, 0)
    for r in range(4):
        forward(r).wait_recv()
    spread_rows(rb, 0, 1)
    spread_rows(rb, 1, 1)
    expert_rows(own, 0, 1)
    for r in HOMEWARD[0]:
        swap(r).start()
    cross_dkv()
    arrive(4)
    arrive(5)
    spread_rows(ra, 2, 0)
    for r in HOMEWARD[0]:
        go_home(r)

    arrive(6)
    arrive(7)
    spread_rows(ra, 3, 0)
    expert_rows(mine, 2, 0)
    for r in range(4, 8):
        forward(r).wait_recv()
    spread_rows(rb, 2, 1)
    spread_rows(rb, 3, 1)
    expert_rows(own, 2, 1)
    for r in HOMEWARD[1]:
        swap(r).start()

    def grad_copy(t, n):
        cols = pl.ds(PARTS[n][0], PARTS[n][1])
        return remote(w_own.at[t, :, cols], w_in.at[t, :, cols], g_send.at[t, n], g_recv.at[t, n], wto)

    def weight_grads(t):
        if t < 2:
            score_t[...] = score[:, t * 2 * PAD : (t + 1) * 2 * PAD].T
        else:
            score_t[...] = active[...].T
        source = gv if t == 2 else xv
        for n, (first, count) in enumerate(PARTS):
            cols = slice(first, min(first + count, WIDTH))
            made = nn(score_t[...], source[:, cols]).astype(bf16)
            w_out[t, :, cols] = made[:PAD]
            w_own[t, :, cols] = made[PAD:]
            grad_copy(t, n).start()

    weight_grads(0)
    for r in HOMEWARD[1][:2]:
        go_home(r)
    weight_grads(1)
    for r in HOMEWARD[1][2:]:
        go_home(r)
    weight_grads(2)

    total = [dkv[c].astype(f32)]
    for i in range(1, 4):
        source = (x + i) % 4

        @pl.when(source > x)
        def _(i=i, source=source):
            dkv_copy(i, 0, source, 0).wait_recv()

        @pl.when(source < x)
        def _(i=i, source=source):
            dkv_copy(i, 0, source, 0).wait_send()
            kv_in[source] = jnp.zeros((TOK, 512), bf16)

        total.append(kv_in[source].astype(f32))

    @pl.when(zh == 0)
    def _():
        kv_copy(kv, c, 0, other).wait_send()
        cross_copy.wait_recv()

    @pl.when(zh == 1)
    def _():
        cross_copy.wait_send()
        for i in range(1, 4):
            kv_copy(kv, x, 3 + i, other).wait_send()
            dkv_copy(i, 0, 0, 1).wait_send()
        kv_in[8] = jnp.zeros((TOK, 512), bf16)

    total.append(kv_in[8].astype(f32))
    dkv_out[...] = sum(total).astype(bf16)

    for copy in weights:
        copy.wait_send()
    for i in range(1, 4):
        kv_copy(kv, c, i, other).wait_send()
    most = ra.at[pl.ds(0, 63)]
    pltpu.make_async_copy(most, most, s_send).wait()
    for r in range(8):
        forward(r).wait_send()
        swap(r).wait_send()
    for t in range(3):
        for n, (first, count) in enumerate(PARTS):
            cols = slice(first, min(first + count, WIDTH))
            grad_copy(t, n).wait()
            w_out[t, :, cols] = (w_out[t, :, cols].astype(f32) + w_in[t, :, cols].astype(f32)).astype(bf16)
    own_back.wait()
    most = back.at[pl.ds(0, 63)]
    for sem in (b_send, b_recv):
        pltpu.make_async_copy(most, most, sem).wait()


def layer_call(pk, kv, gu, ex, queries, out_grad):
    hbm = pl.BlockSpec(memory_space=pl.ANY)
    vmem = pl.BlockSpec(memory_space=pltpu.VMEM)
    bf16 = jnp.bfloat16
    dma = pltpu.SemaphoreType.DMA
    packets = pltpu.VMEM((64, 16, BACK), bf16)
    grads = pltpu.VMEM((3, PAD, WIDE), bf16)
    return pl.pallas_call(
        layer_kernel,
        out_shape=(
            jax.ShapeDtypeStruct(queries.shape, bf16),
            jax.ShapeDtypeStruct((TOK, 512), bf16),
            jax.ShapeDtypeStruct((2 * EXPERTS, 16, BACK), bf16),
            jax.ShapeDtypeStruct((3, PAD, WIDE), bf16),
        ),
        in_specs=[hbm] * 4 + [vmem] * 4,
        out_specs=(vmem, vmem, hbm, vmem),
        scratch_shapes=[
            pltpu.VMEM((64, 16, FOLD), bf16),
            pltpu.VMEM((64, 16, FOLD), bf16),
            pltpu.VMEM((8, TOK, 512), bf16),
            pltpu.VMEM((ROWS, WIDTH), bf16),
            pltpu.VMEM((ROWS, WIDTH), bf16),
            pltpu.VMEM((2, 2, PAD, WIDTH), bf16),
            pltpu.VMEM((2, PAD, WIDTH), bf16),
            pltpu.VMEM((8, TOK, 512), bf16),
            pltpu.VMEM((9, TOK, 512), bf16),
            pltpu.VMEM((TOK, 512), bf16),
            pltpu.VMEM((ROWS, 4 * PAD), bf16),
            pltpu.VMEM((ROWS, 2 * PAD), bf16),
            pltpu.VMEM((2 * PAD, ROWS), bf16),
            packets,
            packets,
            packets,
            grads,
            grads,
            dma,
            dma((8,)),
            dma((8,)),
            dma((8,)),
            dma((4,)),
            dma((7,)),
            dma((8,)),
            dma((7,)),
            dma((9,)),
            dma((8,)),
            dma((8,)),
            dma,
            dma,
            dma((3, 3)),
            dma((3, 3)),
            dma((4,)),
        ]
        + ATTENTION_SCRATCH,
        compiler_params=pltpu.CompilerParams(collective_id=0, has_side_effects=True, vmem_limit_bytes=61 * MIB),
    )(pk, kv, gu, ex, queries, out_grad, jnp.asarray(UNFOLD, bf16), jnp.asarray(FOLDING, bf16))


def pick_rows(routes, shares):
    matched = routes[:, :, None] == jnp.arange(EXPERTS)[None, None, :]
    hits = jnp.any(matched, axis=1)
    share = jnp.sum(jnp.where(matched, shares[:, :, None], 0.0), axis=1)
    before = jnp.asarray(np.tril(np.ones((TOK, TOK), np.float32), -1), jnp.bfloat16)
    earlier = jnp.dot(before, hits.astype(jnp.bfloat16), preferred_element_type=jnp.float32).astype(jnp.int32)
    row = jnp.arange(16)[None, None, :]
    chosen = hits[:, :, None] & (earlier[:, :, None] == row % CAP) & (row < 3 * CAP)
    slot_share = jnp.sum(jnp.where(chosen, share[:, :, None], 0.0), axis=0)
    return chosen, slot_share


def unfold_matrix():
    out = np.zeros((3 * 80, 256), np.float32)
    for p in range(16):
        for k in range(3):
            for s in range(CAP):
                out[k * 80 + p * CAP + s, p * 16 + k * CAP + s] = 1
    return out


UNFOLD = unfold_matrix()
FOLDING = UNFOLD.reshape(3, 80, 256).transpose(0, 2, 1)


def per_device(queries, key_rows, value_rows, out_grad, tokens, token_grad, route_ids, route_probs, entry_weight, exit_weight):
    f32, bf16 = jnp.float32, jnp.bfloat16
    x, g = tokens[0], token_grad[0]
    chosen, slot_share = pick_rows(route_ids[0], route_probs[0])
    part = jnp.arange(16) // CAP
    chosen3 = [(chosen & (part == k)[None, None, :]).reshape(TOK, 512).astype(bf16) for k in range(3)]

    chunks = (x[:, :FOLD], jnp.concatenate([x[:, FOLD:], g[:, FOLD:]], axis=1), g[:, :FOLD])
    packed = sum(tn(s, m) for s, m in zip(chosen3, chunks)).reshape(EXPERTS, 16, FOLD)
    is_grad = (part[:, None] == 2) | ((part[:, None] == 1) & (jnp.arange(FOLD)[None, :] >= WIDTH - FOLD))
    packed = jnp.where(is_grad[None], packed * slot_share[:, :, None], packed).astype(bf16)

    hidden = exit_weight.shape[1]
    gu = jnp.pad(entry_weight[0].transpose(1, 2, 0), ((0, 0), (0, PAD - hidden), (0, 0)))
    ex = jnp.pad(exit_weight[0], ((0, PAD - hidden), (0, 0)))
    kv = jnp.concatenate([key_rows[0], value_rows[0]], axis=1)

    query_grad, dkv_sum, back, w_out = layer_call(packed, kv, gu, ex, queries[0], out_grad[0])

    back = back.reshape(2 * 512, BACK)
    input_grad = jnp.concatenate(
        [nn(jnp.concatenate([s, s], axis=1), back) for s in chosen3], axis=1
    )[:, :WIDTH].astype(bf16)

    entry_grad = w_out[:2, :hidden, :WIDTH]
    exit_grad = w_out[2, :hidden, :WIDTH]
    return (
        query_grad[None],
        dkv_sum[None, :, :256],
        dkv_sum[None, :, 256:],
        input_grad[None],
        entry_grad.transpose(2, 0, 1)[None],
        exit_grad[None],
    )


def solution(mesh):
    row = P("exp", "ctx", None)
    entry = P("exp", None, None, "ctx")
    return jax.shard_map(
        per_device,
        mesh=mesh,
        in_specs=(row,) * 8 + (entry, row),
        out_specs=(row,) * 4 + (entry, row),
        check_vma=False,
    )
```

time: 307 us -> 214 us (0.70)
  Pallas kernels: 239 us -> 183 us
  matrix products: 26.8 us -> 6.03 us
  local copies, waits for them, and re-layouts: 31.2 us -> 15.2 us
    pallas_call x2 -> x1, Pallas kernels: 239 us -> 183 us  [layer_call(): pl.pallas_call(layer_kernel, out_shape=(jax.ShapeDtypeStruct(queries.shap...]
    convert_element_type x2 -> x0, local copies, waits for them, and re-layouts: 12.8 us -> none  [the longest x1 6.6 us: per_device(): eg = tn(score_rows, xr).astype(bf16).reshape(2, 2, PAD, WIDTH)]
    dot_general x2 -> x0, matrix products: 9.44 us -> none  [nt(): lax.dot_general(a, b, (((1,), (1,)), ((), ())), preferred_element_type=jn...]
    dot_general x5 -> x3, matrix products: 9.61 us -> 2.06 us  [tn(): lax.dot_general(a, b, (((0,), (0,)), ((), ())), preferred_element_type=jn...]
    unnamed x57 -> x18, local copies, waits for them, and re-layouts: 12.5 us -> 7.1 us
    dot_general x4 -> x3, matrix products: 6.89 us -> 3.08 us  [nn(): lax.dot_general(a, b, (((1,), (0,)), ((), ())), preferred_element_type=jn...]
where the time goes in v3:
time: 214 us; the launch traced here: 212 us
  Pallas kernels  183 us (86%)
  local copies, waits for them, and re-layouts  15.2 us (7%)
  other arithmetic  6.66 us (3%)
  matrix products  6.03 us (3%)
    pallas_call x1, Pallas kernels, layer_call(): pl.pallas_call(layer_kernel, out_shape=(jax.ShapeDtypeStruct(queries.shap...  183 us
    unnamed x18, local copies, waits for them, and re-layouts  7.1 us

profile of v3, /device:TPU:1, one launch (start us, length us, event | category | flops | bytes accessed | tf_op | source)
XLA Modules:
  0.0 211.6 jit_solution(7906582043983351808)
XLA Ops:
  0.6 0.0 copy-start.3
  0.6 0.0 copy-start.2
  0.7 0.1 and.141
  0.8 0.8 fusion.24
  1.7 0.1 and.149
  1.8 0.1 and.145
  1.9 0.1 and.137
  2.0 0.9 fusion.1
  2.9 0.1 eq.89
  3.0 0.7 select_reduce_fusion.1
  3.7 0.2 select_reduce_fusion
  3.9 0.1 and_or_fusion
  4.0 1.5 pad_maximum_fusion.2.kv
  5.5 0.6 fusion.21
  6.2 1.0 slice.38
  7.1 1.0 slice.39
  8.1 0.0 copy-done.3
  8.1 1.2 pad.9.ex
  9.3 0.0 copy-done.2
  9.3 0.2 copy.34
  9.5 1.6 pad.8.gu
  11.1 0.0 copy-start.4
  11.1 0.7 fusion.15
  11.8 0.4 copy-done.4
  12.2 0.0 copy-start.5
  12.2 0.7 fusion.13
  12.9 0.4 copy-done.5
  13.3 0.7 add_add_fusion
  14.0 1.7 fusion.pk
  15.7 182.9 %shard_map.172 = (bf16[128,2048]{1,0:T(8,128)(2,1)}, bf16[128,512]{1,0:T(8,128)(2,1)}, bf16[64,16,1024]{2,1,0:T(8,128)(2,1)}, bf16[3,192,2944]{2,1,0:T(8,128)(2,1)}) custom-call(bf16[32,16,1920]{2,1,0:T(8,128)(2,1)} %fusion.pk, bf16[128,512]{1,0:T(8,128)(2,1)} %pad_maximum_fusion.2.kv, bf16[2,192,2880]{2,1,0:T(8,128)(2,1)} %pad.8.gu, ...), custom_call_target="tpu_custom_call" | custom-call | tf_op jit(solution)/shard_map/pallas_call | solution.py:477
  198.6 0.0 copy-start
  198.6 1.7 slice_bitcast_fusion.1
  200.3 2.1 convolution_convert_fusion
  202.4 0.0 copy-done
  202.4 0.5 convolution_convert_fusion.1
  202.9 0.0 copy-start.1
  202.9 0.5 convolution_convert_fusion.2
  203.4 0.9 fusion.2
  204.4 2.3 %copy.31 = bf16[1,128,2880]{1,2,0:T(8,128)(2,1)} copy(bf16[1,128,2880]{2,1,0:T(8,128)(2,1)} %fusion.2) | data formatting | bytes 1474560
  206.6 0.0 copy-done.1
  206.6 1.1 slice.36
  207.7 0.1 slice_bitcast_fusion
  207.8 0.0 copy-start.6
  207.8 3.0 %copy.32 = bf16[1,2880,2,180]{1,2,3,0:T(2,128)(2,1)} copy(bf16[1,2880,2,180]{1,3,2,0:T(8,128)(2,1)S(1)} %slice_bitcast_fusion) | data formatting | bytes 4147200
  210.8 0.0 copy-done.6
  210.8 0.8 copy.45
  (10 shorter events, 0.1 us)
Async XLA Ops:
  0.6 7.5 %copy-start.3 = (bf16[1,180,2880]{2,1,0:T(8,128)(2,1)S(1)}, bf16[1,180,2880]{2,1,0:T(8,128)(2,1)}, u32[]{:S(2)}) copy-start(bf16[1,180,2880]{2,1,0:T(8,128)(2,1)} %param.22) | copy-start | bytes 3110404
  0.6 8.6 %copy-start.2 = (bf16[1,2880,2,180]{1,2,3,0:T(2,128)(2,1)S(1)}, bf16[1,2880,2,180]{1,2,3,0:T(2,128)(2,1)}, u32[]{:S(2)}) copy-start(bf16[1,2880,2,180]{1,2,3,0:T(2,128)(2,1)} %param.21) | copy-start | bytes 6220804
  11.1 1.1 copy-start.4
  12.2 1.1 copy-start.5
  198.6 3.8 %copy-start = (bf16[64,16,1024]{2,1,0:T(8,128)(2,1)S(1)}, bf16[64,16,1024]{2,1,0:T(8,128)(2,1)}, u32[]{:S(2)}) copy-start(bf16[64,16,1024]{2,1,0:T(8,128)(2,1)} %get-tuple-element.12) | copy-start | bytes 6291460
  202.9 3.7 %copy-start.1 = (bf16[3,192,2944]{2,1,0:T(8,128)(2,1)S(1)}, bf16[3,192,2944]{2,1,0:T(8,128)(2,1)}, u32[]{:S(2)}) copy-start(bf16[3,192,2944]{2,1,0:T(8,128)(2,1)} %get-tuple-element.13) | copy-start | bytes 10174468
  207.8 3.0 %copy-start.6 = (bf16[128,2048]{1,0:T(8,128)(2,1)S(1)}, bf16[128,2048]{1,0:T(8,128)(2,1)}, u32[]{:S(2)}) copy-start(bf16[128,2048]{1,0:T(8,128)(2,1)} %get-tuple-element.10) | copy-start | bytes 1572868

commit v4 on v3

v4 whole, which is shorter than its diff:
```python
import functools

import jax
import jax.numpy as jnp
import numpy as np
from jax import lax
from jax.experimental import pallas as pl
from jax.experimental.pallas import tpu as pltpu
from jax.sharding import PartitionSpec as P

HEAD = 64
CAP = 5
TOK = 128
WIDTH = 2880
FOLD = 1920
BACK = 1024
PAD = 192
EXPERTS = 32
MESH = pl.DeviceIdType.MESH
MIB = 1024 * 1024
SCALE = 0.125
EXP_SCALE = 0.125 * 1.4426950408889634


def nt(a, b):
    return lax.dot_general(a, b, (((1,), (1,)), ((), ())), preferred_element_type=jnp.float32)


def tn(a, b):
    return lax.dot_general(a, b, (((0,), (0,)), ((), ())), preferred_element_type=jnp.float32)


def nn(a, b):
    return lax.dot_general(a, b, (((1,), (0,)), ((), ())), preferred_element_type=jnp.float32)


def attention_body(c, q_ref, g_ref, kv_ref, dq_ref, dkv_ref, s_ref, kz_ref, vz_ref, q4, g4, dq4, heads=range(4)):
    length = q_ref.shape[0]
    lane = lax.broadcasted_iota(jnp.int32, (length, 128), 1)
    low = lane < HEAD
    krow = lax.broadcasted_iota(jnp.int32, (2 * length, 512), 0) % length
    qcol = lax.broadcasted_iota(jnp.int32, (2 * length, 512), 1) % length
    diag = krow <= qcol

    def spread(tile, h):
        tile = tile.astype(jnp.float32)
        swapped = pltpu.roll(tile, HEAD, 1)
        first, second = (tile, swapped) if h % 2 == 0 else (swapped, tile)
        return jnp.concatenate([jnp.where(low, first, 0.0), jnp.where(low, 0.0, second)], axis=0).astype(jnp.bfloat16)

    def halves(stat):
        return jnp.concatenate([jnp.broadcast_to(stat[0:1], (length, 512)), jnp.broadcast_to(stat[1:2], (length, 512))], axis=0)

    def by_half(x, op):
        return jnp.concatenate([op(x[:length], axis=0, keepdims=True), op(x[length:], axis=0, keepdims=True)], axis=0)

    for h in heads:
        t = h // 2
        for i in range(4):
            cols = slice(h * 512 + i * 128, h * 512 + (i + 1) * 128)
            q4[i * length : (i + 1) * length, :] = q_ref[:, cols]
            g4[i * length : (i + 1) * length, :] = g_ref[:, cols]

        def score_step(j, top, masked):
            keys = spread(kv_ref[j, :, t * 128 : (t + 1) * 128], h)
            kz_ref[j] = keys
            vz_ref[j] = spread(kv_ref[j, :, 256 + t * 128 : 256 + (t + 1) * 128], h)
            s = nt(keys, q4[...])
            if masked:
                s = jnp.where(diag, s, -1e30)
            s_ref[j] = s
            return jnp.maximum(top, by_half(s, jnp.max))

        top = lax.fori_loop(0, c, lambda j, m: score_step(j, m, False), jnp.full((2, 512), -1e30, jnp.float32))
        top = score_step(c, top, True)
        top_wide = halves(top)

        def sum_step(j, state):
            total, dot = state
            p = jnp.exp2((s_ref[j] - top_wide) * EXP_SCALE)
            dp = nt(vz_ref[j], g4[...])
            s_ref[j] = p
            return total + by_half(p, jnp.sum), dot + by_half(p * dp, jnp.sum)

        zero = jnp.zeros((2, 512), jnp.float32)
        total, dot = lax.fori_loop(0, c + 1, sum_step, (zero, zero))
        inverse = 1.0 / total
        inverse_wide = halves(inverse)
        delta_wide = halves(dot * inverse)
        dq4[...] = jnp.zeros_like(dq4)

        def place_heads(j, made, base, scale):
            even, odd = made[:length], made[length:]
            if h % 2 == 0:
                whole = even + pltpu.roll(odd, HEAD, 1)
            else:
                whole = pltpu.roll(even, HEAD, 1) + odd
            whole = (whole * scale).astype(jnp.bfloat16)
            cols = slice(base + t * 128, base + (t + 1) * 128)
            if h % 2 == 1:
                whole = jnp.where(low, dkv_ref[j, :, cols], whole)
            dkv_ref[j, :, cols] = whole

        def grad_step(j, carry):
            p = s_ref[j] * inverse_wide
            ds = (p * (nt(vz_ref[j], g4[...]) - delta_wide)).astype(jnp.bfloat16)
            place_heads(j, nn(p.astype(jnp.bfloat16), g4[...]), 256, 1.0)
            place_heads(j, nn(ds, q4[...]), 0, SCALE)
            dq4[...] += tn(ds, kz_ref[j])
            return carry

        lax.fori_loop(0, c + 1, grad_step, 0)
        for i in range(4):
            cols = slice(h * 512 + i * 128, h * 512 + (i + 1) * 128)
            dq_ref[:, cols] = (dq4[i * length : (i + 1) * length, :] * SCALE).astype(jnp.bfloat16)


ATTENTION_SCRATCH = [
    pltpu.VMEM((8, 256, 512), jnp.float32),
    pltpu.VMEM((8, 256, 128), jnp.bfloat16),
    pltpu.VMEM((8, 256, 128), jnp.bfloat16),
    pltpu.VMEM((512, 128), jnp.bfloat16),
    pltpu.VMEM((512, 128), jnp.bfloat16),
    pltpu.VMEM((512, 128), jnp.float32),
]


def place():
    c, e = lax.axis_index("ctx"), lax.axis_index("exp")
    zh, x = c // 4, c % 4
    zl = (e // 2) % 4
    yc = (e // 8) * 2 + e % 2
    return c, e, zh, x, zh * 4 + zl, yc


def at(z, yc, x):
    return ((z // 4) * 4 + x, (yc // 2) * 8 + (z % 4) * 2 + yc % 2)


def greet(x, z, yc, c, e):
    barrier = pltpu.get_barrier_semaphore()

    def peer(i, carry):
        pl.semaphore_signal(barrier, inc=1, device_id=at((z + i // 8) % 8, (yc + i % 8) % 8, x), device_id_type=MESH)
        return carry

    lax.fori_loop(1, 64, peer, 0)
    return barrier


def pairs(x, e):
    core = e % 2
    near = x + 1 - 2 * (x % 2)
    far = 3 - x
    return near + core * (far - near), far + core * (near - far)


GROUPS = (4, 0, 3, 5, 2, 6, 1, 7)
SLOT = {dz: r for r, dz in enumerate(GROUPS)}
ROWS = 640


def pack_rows(xt, gt, ids, probs, pk, chosen, wide, middle):
    f32, bf16 = jnp.float32, jnp.bfloat16
    expert = lax.broadcasted_iota(jnp.int32, (EXPERTS, TOK), 0)
    hits = jnp.zeros((EXPERTS, TOK), f32)
    share = jnp.zeros((EXPERTS, TOK), f32)
    for j in range(ids.shape[0]):
        matched = jnp.broadcast_to(ids[j : j + 1, :], (EXPERTS, TOK)) == expert
        hits = jnp.where(matched, 1.0, hits)
        share = share + jnp.where(matched, jnp.broadcast_to(probs[j : j + 1, :], (EXPERTS, TOK)), 0.0)
    before = lax.broadcasted_iota(jnp.int32, (TOK, TOK), 0) < lax.broadcasted_iota(jnp.int32, (TOK, TOK), 1)
    earlier = nn(hits.astype(bf16), jnp.where(before, 1.0, 0.0).astype(bf16))
    slot = jnp.where(hits > 0.5, earlier, -1.0)
    for e in range(EXPERTS):
        wide[0, e * 16 : (e + 1) * 16] = jnp.broadcast_to(slot[e : e + 1], (16, TOK))
        wide[1, e * 16 : (e + 1) * 16] = jnp.broadcast_to(share[e : e + 1], (16, TOK))
    row = lax.broadcasted_iota(jnp.int32, (512, TOK), 0) % 16
    slot, share = wide[0], wide[1]
    slot_share = jnp.zeros((512, TOK), f32)
    for k in range(3):
        wanted = (row - CAP * k).astype(f32)
        taken = (slot == wanted) & (row >= CAP * k) & (row < CAP * (k + 1))
        chosen[k] = jnp.where(taken, 1.0, 0.0).astype(bf16)
        slot_share = slot_share + jnp.where(taken, share, 0.0)
    wide[0] = jnp.broadcast_to(jnp.sum(slot_share, axis=1, keepdims=True), (512, TOK))
    rest = WIDTH - FOLD
    middle[:rest] = xt[FOLD:]
    middle[rest:] = gt[FOLD:]
    is_grad = lax.broadcasted_iota(jnp.int32, (TOK, FOLD), 1) >= rest
    for b in range(4):
        rows = slice(b * 128, (b + 1) * 128)
        factor = jnp.broadcast_to(wide[0, rows, :1], (TOK, FOLD))
        total = nt(chosen[0, rows], xt[:FOLD])
        total = total + nt(chosen[1, rows], middle[...]) * jnp.where(is_grad, factor, 1.0)
        total = total + nt(chosen[2, rows], gt[:FOLD]) * factor
        pk[b * 8 : (b + 1) * 8] = total.astype(bf16).reshape(8, 16, FOLD)


PARTS = ((0, 1024), (1024, 1024), (2048, 896))
WIDE = 2944


def layer_kernel(
    gu, ex, k_in, v_in, q, g, xt, gt, ids, probs, unfold, fold,
    dq, dk_out, dv_out, in_out, gu_out, ex_out,
    pk, chosen, wide, middle, back, ra, rb, kv_all, xv, gv, gu2, ex2, dkv, kv_in, cross, score, active, score_t, mine, own, theirs, w_own, w_in,
    s_send, s_recv, f_send, f_recv, w_sem, k_send, k_recv, d_send, d_recv,
    r_send, r_recv, b_send, b_recv, g_send, g_recv, local, *scratch
):
    f32, bf16 = jnp.float32, jnp.bfloat16
    c, e, zh, x, z, yc = place()
    wx, rx = pairs(x, e)
    rto, wto = (zh * 4 + rx, e), (zh * 4 + wx, e)
    other = (4 + x, e)
    barrier = greet(x, z, yc, c, e)
    for i in range(1, 4):
        pl.semaphore_signal(barrier, inc=1, device_id=(zh * 4 + (x + i) % 4, e), device_id_type=MESH)
    own_packet = pltpu.make_async_copy(pk.at[e], ra.at[SLOT[0] * 8], local.at[0])
    own_kv = (
        pltpu.make_async_copy(k_in, kv_all.at[c, :, pl.ds(0, 256)], local.at[1]),
        pltpu.make_async_copy(v_in, kv_all.at[c, :, pl.ds(256, 256)], local.at[2]),
    )
    own_in = (
        pltpu.make_async_copy(gu, gu_out, local.at[3]),
        pltpu.make_async_copy(ex, ex_out, local.at[4]),
    )
    for copy in own_kv + own_in:
        copy.start()
    kv = kv_all.at[c]
    pack_rows(xt, gt, ids, probs, pk, chosen, wide, middle)
    own_packet.start()
    hidden = ex_out.shape[0]
    gu2[:, 0, hidden:] = jnp.zeros((2, PAD - hidden, WIDTH), bf16)
    ex2[0, hidden:] = jnp.zeros((PAD - hidden, WIDTH), bf16)
    for copy in own_kv + own_in:
        copy.wait()
    gu2[:, 0, :hidden] = gu_out[...]
    ex2[0, :hidden] = ex_out[...]
    pl.semaphore_wait(barrier, 66)

    def remote(src, dst, send, recv, to):
        return pltpu.make_async_remote_copy(src, dst, send, recv, device_id=to, device_id_type=MESH)

    def kv_copy(src, block, i, to):
        return remote(src, kv_all.at[block], k_send.at[i], k_recv.at[block], to)

    @pl.when(zh == 0)
    def _():
        kv_copy(kv, c, 0, other).start()

    for i in range(1, 4):

        @pl.when((x + i) % 4 > x)
        def _(i=i):
            kv_copy(kv, c, i, (zh * 4 + (x + i) % 4, e)).start()

    weights = (
        remote(gu2.at[:, 0], gu2.at[:, 1], w_sem.at[0], w_sem.at[1], wto),
        remote(ex2.at[0], ex2.at[1], w_sem.at[2], w_sem.at[3], wto),
    )
    weights[1].start()

    for dz in GROUPS:
        slot = SLOT[(8 - dz) % 8]

        def send_one(d, carry, dz=dz, slot=slot):
            to = at((z + dz) % 8, (yc + d) % 8, x)
            remote(pk.at[to[1]], ra.at[slot * 8 + d], s_send, s_recv.at[slot * 2 + d // 4], to).start()
            return carry

        lax.fori_loop(1 if dz == 0 else 0, 8, send_one, 0)

    @pl.when(zh == 1)
    def _():
        kv_copy(kv, x, 0, other).wait_recv()
        for i in range(1, 4):
            kv_copy(kv_all.at[x], x, 3 + i, (4 + (x + i) % 4, e)).start()

    weights[0].start()

    def forward(r, half):
        block = pl.ds(r * 8 + half * 4, 4)
        i = r * 2 + half
        return remote(ra.at[block], rb.at[block], f_send.at[i], f_recv.at[i], rto)

    def arrive(r, half):
        count = 4
        if GROUPS[r] == 0 and half == 0:
            own_packet.wait()
            count = 3
        some = ra.at[pl.ds(0, count)]
        pltpu.make_async_copy(some, some, s_recv.at[r * 2 + half]).wait()
        forward(r, half).start()

    def spread_rows(ref, b, half):
        packets = ref[b * 16 : (b + 1) * 16].reshape(256, FOLD)
        slots = nn(unfold[...], packets)
        rest = WIDTH - FOLD
        b = b + 4 * half
        rows = slice(b * 80, (b + 1) * 80)
        xv[rows, :FOLD] = slots[:80].astype(bf16)
        gv[rows, :FOLD] = slots[160:].astype(bf16)
        xv[rows, FOLD:] = slots[80:160, :rest].astype(bf16)
        gv[rows, FOLD:] = slots[80:160, rest:].astype(bf16)

    def expert_rows(ref, blocks, half):
        b, size = blocks[0], len(blocks)
        rows = slice((b + 4 * half) * 80, (b + 4 * half + size) * 80)
        gate = nt(xv[rows], gu2[0].reshape(2 * PAD, WIDTH))
        upward = nt(xv[rows], gu2[1].reshape(2 * PAD, WIDTH))
        act_grad = nt(gv[rows], ex2[...].reshape(2 * PAD, WIDTH))
        sigma = jax.nn.sigmoid(gate)
        swish = gate * sigma
        slope = sigma * (1.0 + gate * (1.0 - sigma))
        active[rows] = (swish * upward).astype(bf16)
        score[rows, : 2 * PAD] = (act_grad * upward * slope).astype(bf16)
        score[rows, 2 * PAD :] = (act_grad * swish).astype(bf16)
        totals = [jnp.zeros((256, BACK), f32) for _ in range(size)]
        for k in range(3):
            cols = slice(k * BACK, min((k + 1) * BACK, WIDTH))
            both = gu2[:, :, :, cols].reshape(4 * PAD, cols.stop - cols.start)
            part = nn(score[rows], both).astype(bf16)
            for i in range(size):
                placed = nn(fold[k], part[80 * i : 80 * (i + 1)])
                if placed.shape[1] < BACK:
                    placed = jnp.concatenate([placed, jnp.zeros((256, BACK - placed.shape[1]), f32)], axis=1)
                totals[i] = totals[i] + placed
        for i in range(size):
            ref[(b + i) * 16 : (b + i + 1) * 16] = totals[i].astype(bf16).reshape(16, 16, BACK)

    def swap(r):
        block = pl.ds(r * 8, 8)
        return remote(own.at[block], theirs.at[block], r_send.at[r], r_recv.at[r], rto)

    home = zh * EXPERTS + e
    own_back = pltpu.make_async_copy(mine.at[SLOT[0] * 8], back.at[home], local.at[0])

    def go_home(r):
        dz = GROUPS[r]
        swap(r).wait_recv()

        def add(d, carry):
            total = mine[r * 8 + d].astype(f32) + theirs[r * 8 + d].astype(f32)
            mine[r * 8 + d] = total.astype(bf16)
            return carry

        lax.fori_loop(0, 8, add, 0)

        def send_one(d, carry):
            to = at((z + dz) % 8, (yc + 8 - d) % 8, x)
            remote(mine.at[r * 8 + d], back.at[home], b_send, b_recv, to).start()
            return carry

        lax.fori_loop(1 if dz == 0 else 0, 8, send_one, 0)
        if dz == 0:
            own_back.start()

    def dkv_copy(i, block, slot, half):
        return remote(dkv.at[block], kv_in.at[slot], d_send.at[i + 3 * half], d_recv.at[slot], (zh * 4 + block % 4, e))

    cross_copy = remote(cross, kv_in.at[8], d_send.at[0], d_recv.at[8], (x, e))

    def send_dkv():
        @pl.when(zh == 1)
        def _():
            for i in range(1, 4):
                dkv_copy(i, (x + i) % 4, 4 + x, 1).start()

        for i in range(1, 4):
            to = (x + i) % 4

            @pl.when(to < x)
            def _(i=i, to=to):
                dkv_copy(i, zh * 4 + to, x, 0).start()

    def cross_dkv():
        @pl.when(zh == 1)
        def _():
            total = dkv[x].astype(f32)
            for i in range(1, 4):
                source = 4 + (x + i) % 4
                dkv_copy(i, 0, source, 1).wait_recv()
                total = total + kv_in[source].astype(f32)
            cross[...] = total.astype(bf16)
            cross_copy.start()

    for i in range(1, 4):

        @pl.when((x + i) % 4 < x)
        def _(i=i):
            kv_copy(kv, zh * 4 + (x + i) % 4, i, other).wait_recv()

    @pl.when(zh == 1)
    def _():
        for i in range(1, 4):
            kv_copy(kv, (x + i) % 4, 3 + i, other).wait_recv()

    def attend(heads):
        attention_body(c, q, g, kv_all, dq, dkv, *scratch, heads=heads)

    def own_rows(b):
        spread_rows(ra, b, 0)
        expert_rows(mine, (b,), 0)

    def partner_rows(b):
        for r in (2 * b, 2 * b + 1):
            for half in range(2):
                forward(r, half).wait_recv()
        spread_rows(rb, b, 1)
        expert_rows(own, (b,), 1)
        for r in (2 * b, 2 * b + 1):
            swap(r).start()

    attend((0, 1))
    arrive(1, 0)
    arrive(1, 1)
    attend((2,))
    arrive(0, 0)
    arrive(0, 1)
    attend((3,))
    send_dkv()

    for copy in weights:
        copy.wait_recv()
    own_rows(0)
    partner_rows(0)
    for half in range(2):
        arrive(2, half)
        arrive(3, half)
    own_rows(1)
    cross_dkv()
    partner_rows(1)
    for half in range(2):
        arrive(4, half)
        arrive(5, half)
    own_rows(2)
    for r in range(4):
        go_home(r)
    for half in range(2):
        arrive(6, half)
        arrive(7, half)
    partner_rows(2)
    own_rows(3)
    for r in range(4, 6):
        go_home(r)
    partner_rows(3)

    def grad_copy(t, n):
        cols = pl.ds(PARTS[n][0], PARTS[n][1])
        return remote(w_own.at[t, :, cols], w_in.at[t, :, cols], g_send.at[t, n], g_recv.at[t, n], wto)

    def grad_out(t):
        return ex_out if t == 2 else gu_out.at[t]

    def weight_grads(t):
        if t < 2:
            score_t[...] = score[:, t * 2 * PAD : (t + 1) * 2 * PAD].T
        else:
            score_t[...] = active[...].T
        source = gv if t == 2 else xv
        for n, (first, count) in enumerate(PARTS):
            cols = slice(first, min(first + count, WIDTH))
            made = nn(score_t[...], source[:, cols]).astype(bf16)
            grad_out(t)[:, cols] = made[: gu_out.shape[1]]
            w_own[t, :, cols] = made[PAD:]
            grad_copy(t, n).start()

    weight_grads(0)
    for r in range(6, 8):
        go_home(r)
    weight_grads(1)
    weight_grads(2)

    total = [dkv[c].astype(f32)]
    for i in range(1, 4):
        source = (x + i) % 4

        @pl.when(source > x)
        def _(i=i, source=source):
            dkv_copy(i, 0, source, 0).wait_recv()

        @pl.when(source < x)
        def _(i=i, source=source):
            dkv_copy(i, 0, source, 0).wait_send()
            kv_in[source] = jnp.zeros((TOK, 512), bf16)

        total.append(kv_in[source].astype(f32))

    @pl.when(zh == 0)
    def _():
        kv_copy(kv, c, 0, other).wait_send()
        cross_copy.wait_recv()

    @pl.when(zh == 1)
    def _():
        cross_copy.wait_send()
        for i in range(1, 4):
            kv_copy(kv, x, 3 + i, other).wait_send()
            dkv_copy(i, 0, 0, 1).wait_send()
        kv_in[8] = jnp.zeros((TOK, 512), bf16)

    total.append(kv_in[8].astype(f32))
    total = sum(total).astype(bf16)
    dk_out[...] = total[:, :256]
    dv_out[...] = total[:, 256:]

    for copy in weights:
        copy.wait_send()
    for i in range(1, 4):

        @pl.when((x + i) % 4 > x)
        def _(i=i):
            kv_copy(kv, c, i, other).wait_send()

    most = ra.at[pl.ds(0, 63)]
    pltpu.make_async_copy(most, most, s_send).wait()
    for r in range(8):
        for half in range(2):
            forward(r, half).wait_send()
        swap(r).wait_send()
    own_back.wait()
    most = back.at[pl.ds(0, 63)]
    for sem in (b_recv, b_send):
        pltpu.make_async_copy(most, most, sem).wait()
    for k in range(3):
        cols = slice(k * BACK, min((k + 1) * BACK, WIDTH))
        count = cols.stop - cols.start
        both = [back[h * 32 : (h + 1) * 32, :, :count].reshape(512, count) for h in range(2)]
        in_out[cols] = (tn(chosen[k], both[0]) + tn(chosen[k], both[1])).T.astype(bf16)
    for t in range(3):
        for n, (first, count) in enumerate(PARTS):
            cols = slice(first, min(first + count, WIDTH))
            grad_copy(t, n).wait()
            made = grad_out(t)
            made[:, cols] = (made[:, cols].astype(f32) + w_in[t, : made.shape[0], cols].astype(f32)).astype(bf16)


def layer_call(gu, ex, key_rows, value_rows, queries, out_grad, xt, gt, ids, probs, hidden):
    hbm = pl.BlockSpec(memory_space=pl.ANY)
    vmem = pl.BlockSpec(memory_space=pltpu.VMEM)
    bf16 = jnp.bfloat16
    dma = pltpu.SemaphoreType.DMA
    packets = pltpu.VMEM((64, 16, BACK), bf16)
    grads = pltpu.VMEM((3, PAD, WIDE), bf16)
    return pl.pallas_call(
        layer_kernel,
        out_shape=(
            jax.ShapeDtypeStruct(queries.shape, bf16),
            jax.ShapeDtypeStruct(key_rows.shape, bf16),
            jax.ShapeDtypeStruct(key_rows.shape, bf16),
            jax.ShapeDtypeStruct(xt.shape, bf16),
            jax.ShapeDtypeStruct((2, hidden, WIDTH), bf16),
            jax.ShapeDtypeStruct((hidden, WIDTH), bf16),
        ),
        in_specs=[hbm] * 4 + [vmem] * 8,
        out_specs=(vmem,) * 6,
        scratch_shapes=[
            pltpu.VMEM((EXPERTS, 16, FOLD), bf16),
            pltpu.VMEM((3, 512, TOK), bf16),
            pltpu.VMEM((2, 512, TOK), jnp.float32),
            pltpu.VMEM((FOLD, TOK), bf16),
            packets,
            pltpu.VMEM((64, 16, FOLD), bf16),
            pltpu.VMEM((64, 16, FOLD), bf16),
            pltpu.VMEM((8, TOK, 512), bf16),
            pltpu.VMEM((ROWS, WIDTH), bf16),
            pltpu.VMEM((ROWS, WIDTH), bf16),
            pltpu.VMEM((2, 2, PAD, WIDTH), bf16),
            pltpu.VMEM((2, PAD, WIDTH), bf16),
            pltpu.VMEM((8, TOK, 512), bf16),
            pltpu.VMEM((9, TOK, 512), bf16),
            pltpu.VMEM((TOK, 512), bf16),
            pltpu.VMEM((ROWS, 4 * PAD), bf16),
            pltpu.VMEM((ROWS, 2 * PAD), bf16),
            pltpu.VMEM((2 * PAD, ROWS), bf16),
            packets,
            packets,
            packets,
            grads,
            grads,
            dma,
            dma((16,)),
            dma((16,)),
            dma((16,)),
            dma((4,)),
            dma((7,)),
            dma((8,)),
            dma((7,)),
            dma((9,)),
            dma((8,)),
            dma((8,)),
            dma,
            dma,
            dma((3, 3)),
            dma((3, 3)),
            dma((5,)),
        ]
        + ATTENTION_SCRATCH,
        compiler_params=pltpu.CompilerParams(collective_id=0, has_side_effects=True, vmem_limit_bytes=60 * MIB),
    )(
        gu, ex, key_rows, value_rows, queries, out_grad, xt, gt, ids, probs,
        jnp.asarray(UNFOLD, bf16), jnp.asarray(FOLDING, bf16),
    )


def unfold_matrix():
    out = np.zeros((3 * 80, 256), np.float32)
    for p in range(16):
        for k in range(3):
            for s in range(CAP):
                out[k * 80 + p * CAP + s, p * 16 + k * CAP + s] = 1
    return out


UNFOLD = unfold_matrix()
FOLDING = UNFOLD.reshape(3, 80, 256).transpose(0, 2, 1)


def per_device(queries, key_rows, value_rows, out_grad, tokens, token_grad, route_ids, route_probs, entry_weight, exit_weight):
    hidden = exit_weight.shape[1]
    query_grad, key_grad, value_grad, input_grad, entry_grad, exit_grad = layer_call(
        entry_weight[0].transpose(1, 2, 0), exit_weight[0], key_rows[0], value_rows[0], queries[0], out_grad[0],
        tokens[0].T, token_grad[0].T, route_ids[0].T, route_probs[0].T, hidden,
    )
    return (
        query_grad[None],
        key_grad[None],
        value_grad[None],
        input_grad.T[None],
        entry_grad.transpose(2, 0, 1)[None],
        exit_grad[None],
    )


def solution(mesh):
    row = P("exp", "ctx", None)
    entry = P("exp", None, None, "ctx")
    return jax.shard_map(
        per_device,
        mesh=mesh,
        in_specs=(row,) * 8 + (entry, row),
        out_specs=(row,) * 4 + (entry, row),
        check_vma=False,
    )
```

time: 214 us -> 202 us (0.944)
  other arithmetic: 6.66 us -> 0 us
  matrix products: 6.03 us -> 0 us
  local copies, waits for them, and re-layouts: 15.2 us -> 11.8 us
    dot_general x7 -> x0, matrix products: 6.03 us -> none  [the longest x3 3.08 us: nn(): lax.dot_general(a, b, (((1,), (0,)), ((), ())), preferred_element_type=jn...]
    unnamed x18 -> x17, local copies, waits for them, and re-layouts: 7.1 us -> 11.8 us
    slice x3 -> x0, local copies, waits for them, and re-layouts: 2.99 us -> none  [the longest x1 1.06 us: per_device(): exit_grad = w_out[2, :hidden, :WIDTH]]
    pad x2 -> x0, local copies, waits for them, and re-layouts: 2.78 us -> none  [the longest x1 1.61 us: per_device(): jnp.pad(entry_weight[0].transpose(1, 2, 0), ((0, 0), (0, PAD - hidden), (...]
    pallas_call x1, Pallas kernels: 183 us -> 185 us  [layer_call(): pl.pallas_call(layer_kernel, out_shape=(jax.ShapeDtypeStruct(queries.shap...]
where the time goes in v4:
time: 202 us; the launch traced here: 198 us
  Pallas kernels  185 us (92%)
  local copies, waits for them, and re-layouts  11.8 us (6%)
    pallas_call x1, Pallas kernels, layer_call(): pl.pallas_call(layer_kernel, out_shape=(jax.ShapeDtypeStruct(queries.shap...  185 us
    unnamed x17, local copies, waits for them, and re-layouts  11.8 us

profile of v4, /device:TPU:1, one launch (start us, length us, event | category | flops | bytes accessed | tf_op | source)
XLA Modules:
  0.0 197.9 jit_solution(8211558574142227901)
XLA Ops:
  0.6 3.2 %copy.21 = bf16[1,2880,2,180]{1,3,2,0:T(8,128)(2,1)} copy(bf16[1,2880,2,180]{1,2,3,0:T(2,128)(2,1)} %param.20) | data formatting | bytes 4147200 | tf_op args[8]
  3.8 185.4 %shard_map.163 = (bf16[128,2048]{1,0:T(8,128)(2,1)}, bf16[128,256]{1,0:T(8,128)(2,1)}, bf16[128,256]{1,0:T(8,128)(2,1)}, bf16[2880,128]{1,0:T(8,128)(2,1)}, bf16...) custom-call(bf16[2,180,2880]{2,1,0:T(8,128)(2,1)} %bitcast.32, bf16[180,2880]{1,0:T(8,128)(2,1)} %bitcast.35, ...), custom_call_target="tpu_custom_call" | custom-call | tf_op jit(solution)/shard_map/pallas_call | solution.py:546
  189.2 0.0 copy-start.2
  189.3 0.0 copy-start.4
  189.3 0.0 copy-start.3
  189.3 0.0 copy-start.1
  189.3 4.7 %copy.19 = bf16[1,2880,2,180]{1,2,3,0:T(2,128)(2,1)} copy(bf16[1,2880,2,180]{1,3,2,0:T(8,128)(2,1)} %bitcast.33) | data formatting | bytes 4147200
  194.0 0.0 copy-done.2
  194.0 0.0 copy-start
  194.0 0.8 copy.27
  194.8 0.0 copy-done.4
  194.8 0.6 copy.28
  195.4 0.0 copy-done.3
  195.4 0.6 copy.29
  196.0 0.0 copy-done.1
  196.0 0.9 copy.30
  196.9 0.0 copy-done
  196.9 1.0 copy.31
Async XLA Ops:
  189.2 4.7 %copy-start.2 = (bf16[128,2048]{1,0:T(8,128)(2,1)S(1)}, bf16[128,2048]{1,0:T(8,128)(2,1)}, u32[]{:S(2)}) copy-start(bf16[128,2048]{1,0:T(8,128)(2,1)} %get-tuple-element.12) | copy-start | bytes 1572868
  189.3 5.5 %copy-start.4 = (bf16[128,256]{1,0:T(8,128)(2,1)S(1)}, bf16[128,256]{1,0:T(8,128)(2,1)}, u32[]{:S(2)}) copy-start(bf16[128,256]{1,0:T(8,128)(2,1)} %get-tuple-element.13) | copy-start | bytes 196612
  189.3 6.1 %copy-start.3 = (bf16[128,256]{1,0:T(8,128)(2,1)S(1)}, bf16[128,256]{1,0:T(8,128)(2,1)}, u32[]{:S(2)}) copy-start(bf16[128,256]{1,0:T(8,128)(2,1)} %get-tuple-element.14) | copy-start | bytes 196612
  189.3 6.7 %copy-start.1 = (bf16[2880,128]{1,0:T(8,128)(2,1)S(1)}, bf16[2880,128]{1,0:T(8,128)(2,1)}, u32[]{:S(2)}) copy-start(bf16[2880,128]{1,0:T(8,128)(2,1)} %get-tuple-element.15) | copy-start | bytes 2211844
  194.0 2.9 %copy-start = (bf16[180,2880]{1,0:T(8,128)(2,1)S(1)}, bf16[180,2880]{1,0:T(8,128)(2,1)}, u32[]{:S(2)}) copy-start(bf16[180,2880]{1,0:T(8,128)(2,1)} %get-tuple-element.17) | copy-start | bytes 3110404

commit v5 on v4

--- a/solution.py
+++ b/solution.py
@@ -304,30 +304,46 @@
         xv[rows, FOLD:] = slots[80:160, :rest].astype(bf16)
         gv[rows, FOLD:] = slots[80:160, rest:].astype(bf16)
 
-    def expert_rows(ref, blocks, half):
-        b, size = blocks[0], len(blocks)
-        rows = slice((b + 4 * half) * 80, (b + 4 * half + size) * 80)
-        gate = nt(xv[rows], gu2[0].reshape(2 * PAD, WIDTH))
-        upward = nt(xv[rows], gu2[1].reshape(2 * PAD, WIDTH))
-        act_grad = nt(gv[rows], ex2[...].reshape(2 * PAD, WIDTH))
+    def rows_of(part):
+        b, half = part
+        return slice((b + 4 * half) * 80, (b + 4 * half + 1) * 80)
+
+    def rows_from(ref, parts):
+        return jnp.concatenate([ref[rows_of(part)] for part in parts], axis=0)
+
+    def expert_in(parts):
+        rows = rows_from(xv, parts)
+        gate = nt(rows, gu2[0].reshape(2 * PAD, WIDTH))
+        upward = nt(rows, gu2[1].reshape(2 * PAD, WIDTH))
+        act_grad = nt(rows_from(gv, parts), ex2[...].reshape(2 * PAD, WIDTH))
         sigma = jax.nn.sigmoid(gate)
         swish = gate * sigma
         slope = sigma * (1.0 + gate * (1.0 - sigma))
-        active[rows] = (swish * upward).astype(bf16)
-        score[rows, : 2 * PAD] = (act_grad * upward * slope).astype(bf16)
-        score[rows, 2 * PAD :] = (act_grad * swish).astype(bf16)
-        totals = [jnp.zeros((256, BACK), f32) for _ in range(size)]
+        made = (
+            (active, slice(0, 2 * PAD), swish * upward),
+            (score, slice(0, 2 * PAD), act_grad * upward * slope),
+            (score, slice(2 * PAD, 4 * PAD), act_grad * swish),
+        )
+        for ref, cols, value in made:
+            value = value.astype(bf16)
+            for i, part in enumerate(parts):
+                ref[rows_of(part), cols] = value[80 * i : 80 * (i + 1)]
+
+    def expert_back(parts):
+        rows = rows_from(score, parts)
+        totals = [jnp.zeros((256, BACK), f32) for _ in parts]
         for k in range(3):
             cols = slice(k * BACK, min((k + 1) * BACK, WIDTH))
             both = gu2[:, :, :, cols].reshape(4 * PAD, cols.stop - cols.start)
-            part = nn(score[rows], both).astype(bf16)
-            for i in range(size):
-                placed = nn(fold[k], part[80 * i : 80 * (i + 1)])
+            made = nn(rows, both).astype(bf16)
+            for i in range(len(parts)):
+                placed = nn(fold[k], made[80 * i : 80 * (i + 1)])
                 if placed.shape[1] < BACK:
                     placed = jnp.concatenate([placed, jnp.zeros((256, BACK - placed.shape[1]), f32)], axis=1)
                 totals[i] = totals[i] + placed
-        for i in range(size):
-            ref[(b + i) * 16 : (b + i + 1) * 16] = totals[i].astype(bf16).reshape(16, 16, BACK)
+        for (b, half), total in zip(parts, totals):
+            ref = own if half else mine
+            ref[b * 16 : (b + 1) * 16] = total.astype(bf16).reshape(16, 16, BACK)
 
     def swap(r):
         block = pl.ds(r * 8, 8)
@@ -399,16 +415,19 @@
     def attend(heads):
         attention_body(c, q, g, kv_all, dq, dkv, *scratch, heads=heads)
 
-    def own_rows(b):
-        spread_rows(ra, b, 0)
-        expert_rows(mine, (b,), 0)
-
-    def partner_rows(b):
-        for r in (2 * b, 2 * b + 1):
-            for half in range(2):
-                forward(r, half).wait_recv()
-        spread_rows(rb, b, 1)
-        expert_rows(own, (b,), 1)
+    def arrive_groups(b):
+        for half in range(2):
+            for r in (2 * b, 2 * b + 1):
+                arrive(r, half)
+
+    def take_rows(b, half):
+        if half:
+            for r in (2 * b, 2 * b + 1):
+                for i in range(2):
+                    forward(r, i).wait_recv()
+        spread_rows(rb if half else ra, b, half)
+
+    def swap_rows(b):
         for r in (2 * b, 2 * b + 1):
             swap(r).start()
 
@@ -423,28 +442,31 @@
 
     for copy in weights:
         copy.wait_recv()
-    own_rows(0)
-    partner_rows(0)
-    for half in range(2):
-        arrive(2, half)
-        arrive(3, half)
-    own_rows(1)
-    cross_dkv()
-    partner_rows(1)
-    for half in range(2):
-        arrive(4, half)
-        arrive(5, half)
-    own_rows(2)
-    for r in range(4):
+    for b in range(2):
+        if b:
+            arrive_groups(b)
+            cross_dkv()
+        take_rows(b, 0)
+        take_rows(b, 1)
+        expert_in(((b, 0), (b, 1)))
+        expert_back(((b, 0), (b, 1)))
+        swap_rows(b)
+    arrive_groups(2)
+    take_rows(2, 0)
+    expert_in(((2, 0),))
+    expert_back(((2, 0),))
+    for r in range(2):
         go_home(r)
-    for half in range(2):
-        arrive(6, half)
-        arrive(7, half)
-    partner_rows(2)
-    own_rows(3)
-    for r in range(4, 6):
+    arrive_groups(3)
+    for r in range(2, 4):
         go_home(r)
-    partner_rows(3)
+    take_rows(2, 1)
+    take_rows(3, 0)
+    expert_in(((2, 1), (3, 0)))
+    expert_back(((2, 1), (3, 0)))
+    swap_rows(2)
+    take_rows(3, 1)
+    expert_in(((3, 1),))
 
     def grad_copy(t, n):
         cols = pl.ds(PARTS[n][0], PARTS[n][1])
@@ -467,10 +489,14 @@
             grad_copy(t, n).start()
 
     weight_grads(0)
-    for r in range(6, 8):
+    expert_back(((3, 1),))
+    swap_rows(3)
+    for r in range(4, 6):
         go_home(r)
     weight_grads(1)
     weight_grads(2)
+    for r in range(6, 8):
+        go_home(r)
 
     total = [dkv[c].astype(f32)]
     for i in range(1, 4):
@@ -519,6 +545,14 @@
         for half in range(2):
             forward(r, half).wait_send()
         swap(r).wait_send()
+    def add_grads(t):
+        made = grad_out(t)
+        for n, (first, count) in enumerate(PARTS):
+            cols = slice(first, min(first + count, WIDTH))
+            grad_copy(t, n).wait()
+            made[:, cols] = (made[:, cols].astype(f32) + w_in[t, : made.shape[0], cols].astype(f32)).astype(bf16)
+
+    add_grads(0)
     own_back.wait()
     most = back.at[pl.ds(0, 63)]
     for sem in (b_recv, b_send):
@@ -528,12 +562,8 @@
         count = cols.stop - cols.start
         both = [back[h * 32 : (h + 1) * 32, :, :count].reshape(512, count) for h in range(2)]
         in_out[cols] = (tn(chosen[k], both[0]) + tn(chosen[k], both[1])).T.astype(bf16)
-    for t in range(3):
-        for n, (first, count) in enumerate(PARTS):
-            cols = slice(first, min(first + count, WIDTH))
-            grad_copy(t, n).wait()
-            made = grad_out(t)
-            made[:, cols] = (made[:, cols].astype(f32) + w_in[t, : made.shape[0], cols].astype(f32)).astype(bf16)
+    add_grads(1)
+    add_grads(2)
 
 
 def layer_call(gu, ex, key_rows, value_rows, queries, out_grad, xt, gt, ids, probs, hidden):

time: 202 us -> 201 us (level)
  the two profiles are of different devices: /device:TPU:1 before, /device:TPU:63 now
where the time goes in v5:
time: 201 us; the launch traced here: 200 us
  Pallas kernels  188 us (94%)
  local copies, waits for them, and re-layouts  11.8 us (6%)
    pallas_call x1, Pallas kernels, layer_call(): pl.pallas_call(layer_kernel, out_shape=(jax.ShapeDtypeStruct(queries.shap...  188 us
    unnamed x17, local copies, waits for them, and re-layouts  11.8 us

profile of v5, /device:TPU:63, one launch (start us, length us, event | category | flops | bytes accessed | tf_op | source)
XLA Modules:
  0.0 200.5 jit_solution(4124941748032436929)
XLA Ops:
  0.6 3.2 %copy.21 = bf16[1,2880,2,180]{1,3,2,0:T(8,128)(2,1)} copy(bf16[1,2880,2,180]{1,2,3,0:T(2,128)(2,1)} %param.20) | data formatting | bytes 4147200 | tf_op args[8]
  3.8 188.1 %shard_map.163 = (bf16[128,2048]{1,0:T(8,128)(2,1)}, bf16[128,256]{1,0:T(8,128)(2,1)}, bf16[128,256]{1,0:T(8,128)(2,1)}, bf16[2880,128]{1,0:T(8,128)(2,1)}, bf16...) custom-call(bf16[2,180,2880]{2,1,0:T(8,128)(2,1)} %bitcast.32, bf16[180,2880]{1,0:T(8,128)(2,1)} %bitcast.35, ...), custom_call_target="tpu_custom_call" | custom-call | tf_op jit(solution)/shard_map/pallas_call | solution.py:576
  191.9 0.0 copy-start.2
  191.9 0.0 copy-start.4
  191.9 0.0 copy-start.3
  191.9 0.0 copy-start.1
  191.9 4.7 %copy.19 = bf16[1,2880,2,180]{1,2,3,0:T(2,128)(2,1)} copy(bf16[1,2880,2,180]{1,3,2,0:T(8,128)(2,1)} %bitcast.33) | data formatting | bytes 4147200
  196.6 0.0 copy-done.2
  196.6 0.0 copy-start
  196.6 0.8 copy.27
  197.4 0.0 copy-done.4
  197.4 0.6 copy.28
  198.0 0.0 copy-done.3
  198.0 0.6 copy.29
  198.6 0.0 copy-done.1
  198.6 0.9 copy.30
  199.5 0.0 copy-done
  199.5 1.0 copy.31
Async XLA Ops:
  191.9 4.7 %copy-start.2 = (bf16[128,2048]{1,0:T(8,128)(2,1)S(1)}, bf16[128,2048]{1,0:T(8,128)(2,1)}, u32[]{:S(2)}) copy-start(bf16[128,2048]{1,0:T(8,128)(2,1)} %get-tuple-element.12) | copy-start | bytes 1572868
  191.9 5.5 %copy-start.4 = (bf16[128,256]{1,0:T(8,128)(2,1)S(1)}, bf16[128,256]{1,0:T(8,128)(2,1)}, u32[]{:S(2)}) copy-start(bf16[128,256]{1,0:T(8,128)(2,1)} %get-tuple-element.13) | copy-start | bytes 196612
  191.9 6.1 %copy-start.3 = (bf16[128,256]{1,0:T(8,128)(2,1)S(1)}, bf16[128,256]{1,0:T(8,128)(2,1)}, u32[]{:S(2)}) copy-start(bf16[128,256]{1,0:T(8,128)(2,1)} %get-tuple-element.14) | copy-start | bytes 196612
  191.9 6.7 %copy-start.1 = (bf16[2880,128]{1,0:T(8,128)(2,1)S(1)}, bf16[2880,128]{1,0:T(8,128)(2,1)}, u32[]{:S(2)}) copy-start(bf16[2880,128]{1,0:T(8,128)(2,1)} %get-tuple-element.15) | copy-start | bytes 2211844
  196.6 2.9 %copy-start = (bf16[180,2880]{1,0:T(8,128)(2,1)S(1)}, bf16[180,2880]{1,0:T(8,128)(2,1)}, u32[]{:S(2)}) copy-start(bf16[180,2880]{1,0:T(8,128)(2,1)} %get-tuple-element.17) | copy-start | bytes 3110404

commit v6 on v5

--- a/solution.py
+++ b/solution.py
@@ -455,11 +455,9 @@
     take_rows(2, 0)
     expert_in(((2, 0),))
     expert_back(((2, 0),))
-    for r in range(2):
+    for r in range(4):
         go_home(r)
     arrive_groups(3)
-    for r in range(2, 4):
-        go_home(r)
     take_rows(2, 1)
     take_rows(3, 0)
     expert_in(((2, 1), (3, 0)))
@@ -545,14 +543,6 @@
         for half in range(2):
             forward(r, half).wait_send()
         swap(r).wait_send()
-    def add_grads(t):
-        made = grad_out(t)
-        for n, (first, count) in enumerate(PARTS):
-            cols = slice(first, min(first + count, WIDTH))
-            grad_copy(t, n).wait()
-            made[:, cols] = (made[:, cols].astype(f32) + w_in[t, : made.shape[0], cols].astype(f32)).astype(bf16)
-
-    add_grads(0)
     own_back.wait()
     most = back.at[pl.ds(0, 63)]
     for sem in (b_recv, b_send):
@@ -562,8 +552,12 @@
         count = cols.stop - cols.start
         both = [back[h * 32 : (h + 1) * 32, :, :count].reshape(512, count) for h in range(2)]
         in_out[cols] = (tn(chosen[k], both[0]) + tn(chosen[k], both[1])).T.astype(bf16)
-    add_grads(1)
-    add_grads(2)
+    for t in range(3):
+        for n, (first, count) in enumerate(PARTS):
+            cols = slice(first, min(first + count, WIDTH))
+            grad_copy(t, n).wait()
+            made = grad_out(t)
+            made[:, cols] = (made[:, cols].astype(f32) + w_in[t, : made.shape[0], cols].astype(f32)).astype(bf16)
 
 
 def layer_call(gu, ex, key_rows, value_rows, queries, out_grad, xt, gt, ids, probs, hidden):

time: 201 us -> 197 us (0.980)
  the two profiles are of different devices: /device:TPU:63 before, /device:TPU:34 now
where the time goes in v6:
time: 197 us
  Pallas kernels  184 us (93%)
  local copies, waits for them, and re-layouts  11.8 us (6%)
    pallas_call x1, Pallas kernels, layer_call(): pl.pallas_call(layer_kernel, out_shape=(jax.ShapeDtypeStruct(queries.shap...  184 us
    unnamed x17, local copies, waits for them, and re-layouts  11.8 us

profile of v6, /device:TPU:34, one launch (start us, length us, event | category | flops | bytes accessed | tf_op | source)
XLA Modules:
  0.0 196.8 jit_solution(16124339212955864866)
XLA Ops:
  0.6 3.2 %copy.21 = bf16[1,2880,2,180]{1,3,2,0:T(8,128)(2,1)} copy(bf16[1,2880,2,180]{1,2,3,0:T(2,128)(2,1)} %param.20) | data formatting | bytes 4147200 | tf_op args[8]
  3.8 184.4 %shard_map.163 = (bf16[128,2048]{1,0:T(8,128)(2,1)}, bf16[128,256]{1,0:T(8,128)(2,1)}, bf16[128,256]{1,0:T(8,128)(2,1)}, bf16[2880,128]{1,0:T(8,128)(2,1)}, bf16...) custom-call(bf16[2,180,2880]{2,1,0:T(8,128)(2,1)} %bitcast.32, bf16[180,2880]{1,0:T(8,128)(2,1)} %bitcast.35, ...), custom_call_target="tpu_custom_call" | custom-call | tf_op jit(solution)/shard_map/pallas_call | solution.py:570
  188.2 0.0 copy-start.2
  188.2 0.0 copy-start.4
  188.2 0.0 copy-start.3
  188.2 0.0 copy-start.1
  188.2 4.7 %copy.19 = bf16[1,2880,2,180]{1,2,3,0:T(2,128)(2,1)} copy(bf16[1,2880,2,180]{1,3,2,0:T(8,128)(2,1)} %bitcast.33) | data formatting | bytes 4147200
  192.9 0.0 copy-done.2
  192.9 0.0 copy-start
  192.9 0.8 copy.27
  193.7 0.0 copy-done.4
  193.7 0.6 copy.28
  194.3 0.0 copy-done.3
  194.3 0.6 copy.29
  194.9 0.0 copy-done.1
  194.9 0.9 copy.30
  195.8 0.0 copy-done
  195.8 1.0 copy.31
Async XLA Ops:
  188.2 4.7 %copy-start.2 = (bf16[128,2048]{1,0:T(8,128)(2,1)S(1)}, bf16[128,2048]{1,0:T(8,128)(2,1)}, u32[]{:S(2)}) copy-start(bf16[128,2048]{1,0:T(8,128)(2,1)} %get-tuple-element.12) | copy-start | bytes 1572868
  188.2 5.5 %copy-start.4 = (bf16[128,256]{1,0:T(8,128)(2,1)S(1)}, bf16[128,256]{1,0:T(8,128)(2,1)}, u32[]{:S(2)}) copy-start(bf16[128,256]{1,0:T(8,128)(2,1)} %get-tuple-element.13) | copy-start | bytes 196612
  188.2 6.1 %copy-start.3 = (bf16[128,256]{1,0:T(8,128)(2,1)S(1)}, bf16[128,256]{1,0:T(8,128)(2,1)}, u32[]{:S(2)}) copy-start(bf16[128,256]{1,0:T(8,128)(2,1)} %get-tuple-element.14) | copy-start | bytes 196612
  188.2 6.7 %copy-start.1 = (bf16[2880,128]{1,0:T(8,128)(2,1)S(1)}, bf16[2880,128]{1,0:T(8,128)(2,1)}, u32[]{:S(2)}) copy-start(bf16[2880,128]{1,0:T(8,128)(2,1)} %get-tuple-element.15) | copy-start | bytes 2211844
  192.9 2.9 %copy-start = (bf16[180,2880]{1,0:T(8,128)(2,1)S(1)}, bf16[180,2880]{1,0:T(8,128)(2,1)}, u32[]{:S(2)}) copy-start(bf16[180,2880]{1,0:T(8,128)(2,1)} %get-tuple-element.17) | copy-start | bytes 3110404
